TPU v7x, 128 devices: a whole 4x4x4 slice. The times are simulated.
128 devices in a mesh: dp: 4 (over x), seq: 32 (over y, z, core).
Axes of the slice: x: 4, y: 4, z: 4, core: 2. Of those that a mesh axis runs over, the one named last changes fastest.
Arguments:
- query: bfloat16 [4, 8192, 1536], P('dp', 'seq'), may hold values from -9 to 9
- key: bfloat16 [4, 8192, 1536], P('dp', 'seq'), may hold values from -9 to 9
- value: bfloat16 [4, 8192, 1536], P('dp', 'seq'), may hold values from -16 to 16
- w_out: bfloat16 [1536, 1536], replicated, may hold values from -0.15625 to 0.15625
- grad_out: bfloat16 [4, 8192, 1536], P('dp', 'seq'), may hold values from -6 to 6
Outputs:
- mixed: bfloat16 [4, 8192, 1536], P('dp', 'seq')
- grad_query: bfloat16 [4, 8192, 1536], P('dp', 'seq')
- grad_key: bfloat16 [4, 8192, 1536], P('dp', 'seq')
- grad_value: bfloat16 [4, 8192, 1536], P('dp', 'seq')
- grad_weight: float32 [1536, 1536], P(('dp', 'seq'))
All inputs are finite; a program needn't handle non-finite values.
Results may differ from a plain program's by a relative error of at most 0.025.
Values may be sent and summed in bfloat16 or wider, within the bound.
No kernel may reach another device: no remote copies, remote signals or barrier semaphores. Data moves between devices by JAX's collectives and lax.ppermute only.
A program may use at most 192 MiB of HBM per device.

v0:
```python
import math

import jax
import jax.numpy as jnp
from jax import lax
from jax.sharding import PartitionSpec as P

H = 12
HD = 128
BS = 32


def swapped(block, axis, stride):
    count = lax.axis_size(axis)
    route = []
    for low in range(count):
        high = low | 1 << stride
        if high != low and high < count:
            route += [(low, high), (high, low)]
    return lax.ppermute(block, axis, route)


def for_sending(x):

    def short(part):
        return part.astype(jnp.bfloat16) if part.dtype == jnp.float32 else part

    return jax.tree.map(short, x)


def pair_mean(rows):
    wide = rows.astype(jnp.float32).reshape(rows.shape[0] // 2, 2, rows.shape[1])
    return ((wide[:, 0] + wide[:, 1]) * 0.5).astype(jnp.bfloat16)


def halve_back(grads):
    return jnp.repeat(grads, 2, axis=0) * 0.5


def spread_level(rows, level, blocks):
    width = rows.shape[1]
    nodes = rows.shape[0] // BS
    flipped = rows.reshape(nodes // 2, 2, BS, width)[:, ::-1].reshape(nodes, 1, BS, width)
    return jnp.broadcast_to(flipped, (nodes, 2**level, BS, width)).reshape(blocks, BS, width)


def collect_level(grads, level):
    blocks = grads.shape[0]
    width = grads.shape[2]
    nodes = blocks // 2**level
    summed = grads.reshape(nodes, 2**level, BS, width).sum(axis=1)
    return summed.reshape(nodes // 2, 2, BS, width)[:, ::-1].reshape(nodes * BS, width)


def local(query, key, value, w_out, grad_out):
    tokens_dev = query.shape[1]
    width = query.shape[2]
    blocks = tokens_dev // BS
    local_levels = blocks.bit_length() - 1
    seq_bits = lax.axis_size("seq").bit_length() - 1
    position = lax.axis_index("seq")
    scale_factor = HD ** (-0.5)
    log_two = math.log(2.0)
    pairs = jnp.concatenate([key[0], value[0]], axis=1)
    pyramid = [pairs]
    for level in range(local_levels):
        pyramid.append(pair_mean(pyramid[-1]))
    coarse = pyramid[local_levels]
    lower_side = [position >> depth & 1 == 0 for depth in range(seq_bits)]
    siblings = []
    current = coarse
    for depth in range(seq_bits):
        partner = swapped(current, "seq", depth)
        siblings.append(partner)
        if depth + 1 < seq_bits:
            first = jnp.where(lower_side[depth], current, partner)
            second = jnp.where(lower_side[depth], partner, current)
            current = pair_mean(jnp.concatenate([first, second], axis=0))
    local_set = jnp.concatenate(
        [pairs.reshape(blocks, BS, 2 * width)]
        + [spread_level(pyramid[level], level, blocks) for level in range(local_levels)],
        axis=1,
    )
    cross_set = jnp.concatenate(siblings, axis=0)
    local_keys = local_set.shape[1]
    cross_keys = cross_set.shape[0]
    bias_local = jnp.concatenate(
        [jnp.zeros((BS,), jnp.float32)]
        + [jnp.full((BS,), level * log_two, jnp.float32) for level in range(local_levels)]
    )
    bias_cross = jnp.concatenate(
        [
            jnp.full((BS,), (local_levels + depth) * log_two, jnp.float32)
            for depth in range(seq_bits)
        ]
    )
    query_heads = query[0].reshape(blocks, BS, H, HD)
    key_local = local_set[..., :width].reshape(blocks, local_keys, H, HD)
    value_local = local_set[..., width:].reshape(blocks, local_keys, H, HD)
    key_cross = cross_set[:, :width].reshape(cross_keys, H, HD)
    value_cross = cross_set[:, width:].reshape(cross_keys, H, HD)
    scores_local = (
        jnp.einsum("bqhd,bkhd->bhqk", query_heads, key_local, preferred_element_type=jnp.float32)
        * scale_factor
        + bias_local
    )
    scores_cross = (
        jnp.einsum("bqhd,khd->bhqk", query_heads, key_cross, preferred_element_type=jnp.float32)
        * scale_factor
        + bias_cross
    )
    highest = jnp.maximum(jnp.max(scores_local, axis=-1), jnp.max(scores_cross, axis=-1))[..., None]
    expo_local = jnp.exp(scores_local - highest)
    expo_cross = jnp.exp(scores_cross - highest)
    denom = jnp.sum(expo_local, axis=-1, keepdims=True) + jnp.sum(
        expo_cross, axis=-1, keepdims=True
    )
    probs_local = expo_local / denom
    probs_cross = expo_cross / denom
    probs_local_b = probs_local.astype(jnp.bfloat16)
    probs_cross_b = probs_cross.astype(jnp.bfloat16)
    attended_f = jnp.einsum(
        "bhqk,bkhd->bqhd", probs_local_b, value_local, preferred_element_type=jnp.float32
    )
    attended_f = attended_f + jnp.einsum(
        "bhqk,khd->bqhd", probs_cross_b, value_cross, preferred_element_type=jnp.float32
    )
    attended = attended_f.astype(jnp.bfloat16).reshape(tokens_dev, width)
    mixed = jnp.dot(attended, w_out, preferred_element_type=jnp.float32).astype(jnp.bfloat16)
    grad_attended = jnp.dot(grad_out[0], w_out.T, preferred_element_type=jnp.float32).astype(
        jnp.bfloat16
    )
    grad_heads = grad_attended.reshape(blocks, BS, H, HD)
    delta = jnp.swapaxes(jnp.sum(grad_heads.astype(jnp.float32) * attended_f, axis=-1), 1, 2)[
        ..., None
    ]
    grad_probs_local = jnp.einsum(
        "bqhd,bkhd->bhqk", grad_heads, value_local, preferred_element_type=jnp.float32
    )
    grad_probs_cross = jnp.einsum(
        "bqhd,khd->bhqk", grad_heads, value_cross, preferred_element_type=jnp.float32
    )
    grad_scores_local = (probs_local * (grad_probs_local - delta) * scale_factor).astype(
        jnp.bfloat16
    )
    grad_scores_cross = (probs_cross * (grad_probs_cross - delta) * scale_factor).astype(
        jnp.bfloat16
    )
    grad_query = jnp.einsum(
        "bhqk,bkhd->bqhd", grad_scores_local, key_local, preferred_element_type=jnp.float32
    )
    grad_query = grad_query + jnp.einsum(
        "bhqk,khd->bqhd", grad_scores_cross, key_cross, preferred_element_type=jnp.float32
    )
    grad_query = grad_query.astype(jnp.bfloat16).reshape(tokens_dev, width)
    grad_key_local = jnp.einsum(
        "bhqk,bqhd->bkhd", grad_scores_local, query_heads, preferred_element_type=jnp.float32
    )
    grad_value_local = jnp.einsum(
        "bhqk,bqhd->bkhd", probs_local_b, grad_heads, preferred_element_type=jnp.float32
    )
    grad_key_cross = jnp.einsum(
        "bhqk,bqhd->khd", grad_scores_cross, query_heads, preferred_element_type=jnp.float32
    )
    grad_value_cross = jnp.einsum(
        "bhqk,bqhd->khd", probs_cross_b, grad_heads, preferred_element_type=jnp.float32
    )
    grad_set = jnp.concatenate(
        [
            grad_key_local.reshape(blocks, local_keys, width),
            grad_value_local.reshape(blocks, local_keys, width),
        ],
        axis=-1,
    )
    grad_cross = jnp.concatenate(
        [grad_key_cross.reshape(cross_keys, width), grad_value_cross.reshape(cross_keys, width)],
        axis=-1,
    )
    sibling_grads = [grad_cross[depth * BS : (depth + 1) * BS] for depth in range(seq_bits)]
    carried = jnp.zeros((BS, 2 * width), jnp.float32)
    for depth in reversed(range(seq_bits)):
        if depth + 1 < seq_bits:
            spread = halve_back(carried)
            first = spread[:BS]
            second = spread[BS:]
            own_part = jnp.where(lower_side[depth], first, second)
            partner_part = jnp.where(lower_side[depth], second, first)
        else:
            own_part = jnp.zeros((BS, 2 * width), jnp.float32)
            partner_part = jnp.zeros((BS, 2 * width), jnp.float32)
        carried = own_part + swapped(for_sending(partner_part + sibling_grads[depth]), "seq", depth)
    top_grad = carried
    carried = top_grad
    for place in range(local_levels, 0, -1):
        carried = halve_back(carried) + collect_level(
            grad_set[:, BS * place : BS * (place + 1)], place - 1
        )
    grad_fine = carried + grad_set[:, :BS].reshape(tokens_dev, 2 * width)
    grad_key = grad_fine[:, :width].astype(jnp.bfloat16)
    grad_value = grad_fine[:, width:].astype(jnp.bfloat16)
    groups = lax.axis_size("dp") * lax.axis_size("seq")
    weight_rows = lax.psum_scatter(
        jnp.dot(attended.T, grad_out[0], preferred_element_type=jnp.float32),
        ("dp", "seq"),
        scatter_dimension=0,
        tiled=True,
    )
    grad_weight = weight_rows * (1.0 / math.sqrt(groups * tokens_dev))
    return (mixed[None], grad_query[None], grad_key[None], grad_value[None], grad_weight)


def solution(mesh):
    return jax.shard_map(
        local,
        mesh=mesh,
        in_specs=(
            P("dp", "seq", None),
            P("dp", "seq", None),
            P("dp", "seq", None),
            P(),
            P("dp", "seq", None),
        ),
        out_specs=(
            P("dp", "seq", None),
            P("dp", "seq", None),
            P("dp", "seq", None),
            P("dp", "seq", None),
            P(("dp", "seq"), None),
        ),
        check_vma=False,
    )
```

profile of v0, /device:TPU:1, one launch (start us, length us, event | category | flops | bytes accessed | tf_op | source)
XLA Modules:
  0.0 752.6 jit_solution(1997999927546693069)
XLA Ops:
  6.4 7.0 convert_reduce_fusion
  44.7 6.1 fusion.72
  62.4 4.6 copy.249
  67.0 4.6 copy.248
  95.9 3.8 fusion.58
  102.4 5.2 fusion.22
  107.5 376.7 %fusion = f32[16,1536]{1,0:T(8,128)S(1)} fusion(f32[1536,1536]{1,0:T(8,128)} %fusion.22), kind=kCustom, calls=%all-reduce-scatter | all-reduce-scatter fusion | flops 3145729 | bytes 9535488
  501.6 8.5 %bitcast_reduce_fusion.1 = f32[2,32,3072]{1,2,0:T(8,128)} fusion(f32[8,128,1536]{1,2,0:T(8,128)S(1)} %bitcast.192, f32[8,128,1536]{1,2,0:T(8,128)S(1)} %bitcast.194), kind=kLoop, calls=%fused_computation.11 | loop fusion | flops 1376256 | bytes 13369344 | tf_op jit(solution)/shard_map/reduce_sum | solution.py:51
  510.1 9.6 %fusion.1 = (f32[8,32,3072]{1,2,0:T(8,128)}, f32[8,32,3072]{1,2,0:T(8,128)}) fusion(f32[8,128,1536]{1,2,0:T(8,128)S(1)} %bitcast.195, f32[8,128,1536]{1,2,0:T(8,128)S(1)} %bitcast.193), kind=kLoop, calls=%fused_computation.6 | loop fusion | flops 1572864 | bytes 18874368 | tf_op jit(solution)/shard_map/concatenate | solution.py:168
  521.4 10.3 %bitcast_reduce_fusion = f32[4,32,3072]{1,2,0:T(8,128)} fusion(f32[8,128,1536]{1,2,0:T(8,128)} %bitcast.189, f32[8,128,1536]{1,2,0:T(8,128)} %bitcast.196), kind=kLoop, calls=%fused_computation.10 | loop fusion | flops 1179648 | bytes 14155776 | tf_op jit(solution)/shard_map/reduce_sum | solution.py:51
  533.4 9.7 %collective-permute-start.41 = (f32[12,1536]{1,0:T(8,128)S(1)}, f32[12,1536]{1,0:T(8,128)S(1)}, u32[]{:S(2)}, u32[]{:S(2)}) collective-permute-start(f32[12,1536]{1,0:T(8,128)S(1)} %slice.206), channel_id=1, source_target_pairs={{0,32},{1,33},{2,34},{3,35},{4,36},{5,37},{6,38},{7,39},{8,40},{9,... | collective-permute-start | bytes 221192
  546.6 6.1 collective-permute-start.35
  562.2 4.8 collective-permute-start.31
  576.7 4.0 collective-permute-start.28
  592.8 4.1 collective-permute-start.22
  615.2 4.0 collective-permute-start.14
  630.2 4.2 collective-permute-start.10
  648.0 4.4 copy.289
  653.6 8.8 %copy.290 = f32[4,2,32,3072]{3,2,1,0:T(8,128)} copy(f32[4,2,32,3072]{2,3,1,0:T(8,128)} %bitcast.199) | data formatting | bytes 6291456 | tf_op jit(solution)/shard_map/reshape | solution.py:52
  662.4 3.8 rev.20
  666.4 9.0 %copy.291 = f32[8,32,3072]{2,1,0:T(8,128)} copy(f32[8,32,3072]{1,2,0:T(8,128)} %get-tuple-element.8) | data formatting | bytes 6291456 | tf_op jit(solution)/shard_map/slice | solution.py:198
  675.6 51.2 %concatenate.63 = f32[524,1536]{1,0:T(8,128)} concatenate(f32[12,1536]{1,0:T(8,128)S(1)} %copy-done.26, f32[16,1536]{1,0:T(8,128)} %collective-permute-done.40, f32[16,1536]{1,0:T(8,128)} %collective-permute-done.39, f32[16,1536]{1,0:T(8,128)} %collective-permute-done.38, f32[16,1536]{1,0:T(8,128)S(1)} %copy-done.24, f32[16,1536]{1,0:T(8,128)S(1)} %copy-done.28, ...), dimensions={0} | concatenate | bytes 6438912
  741.2 5.2 mul.137
  746.4 4.5 fusion.4
  (314 shorter events, 190.0 us)
Async XLA Ops:
  52.8 18.8 %collective-permute-start.3 = (bf16[32,3072]{1,0:T(8,128)(2,1)S(1)}, bf16[32,3072]{1,0:T(8,128)(2,1)S(1)}, u32[]{:S(2)}, u32[]{:S(2)}) collective-permute-start(bf16[32,3072]{1,0:T(8,128)(2,1)S(1)} %fusion.67), channel_id=1, source_target_pairs={{0,8},{8,0},{1,9},{9,1},{2,10},{10,2},{3,11},{11,3},{4,12},{12,4},... | collective-permute-start | bytes 589832 | tf_op jit(solution)/shard_map/ppermute | solution.py:20
  484.2 62.4 %collective-permute-start.40 = (f32[16,1536]{1,0:T(8,128)S(1)}, f32[16,1536]{1,0:T(8,128)}, u32[]{:S(2)}, u32[]{:S(2)}) collective-permute-start(f32[16,1536]{1,0:T(8,128)S(1)} %fusion), channel_id=1, source_target_pairs={{0,31},{1,32},{2,33},{3,34},{4,35},{5,36},{6,37},{7,38},{8,39},{9,... | collective-permute-start | bytes 294920
  486.3 66.4 %collective-permute-start.39 = (f32[16,1536]{1,0:T(8,128)S(1)}, f32[16,1536]{1,0:T(8,128)}, u32[]{:S(2)}, u32[]{:S(2)}) collective-permute-start(f32[16,1536]{1,0:T(8,128)S(1)} %fusion), channel_id=1, source_target_pairs={{0,30},{1,31},{2,32},{3,33},{4,34},{5,35},{6,36},{7,37},{8,38},{9,... | collective-permute-start | bytes 294920
  488.2 65.9 %collective-permute-start.38 = (f32[16,1536]{1,0:T(8,128)S(1)}, f32[16,1536]{1,0:T(8,128)}, u32[]{:S(2)}, u32[]{:S(2)}) collective-permute-start(f32[16,1536]{1,0:T(8,128)S(1)} %fusion), channel_id=1, source_target_pairs={{0,29},{1,30},{2,31},{3,32},{4,33},{5,34},{6,35},{7,36},{8,37},{9,... | collective-permute-start | bytes 294920
  499.4 20.3 %collective-permute-start.5 = (bf16[32,3072]{1,0:T(8,128)(2,1)S(1)}, bf16[32,3072]{1,0:T(8,128)(2,1)S(1)}, u32[]{:S(2)}, u32[]{:S(2)}) collective-permute-start(bf16[32,3072]{1,0:T(8,128)(2,1)S(1)} %slice.274), channel_id=1, source_target_pairs={{0,16},{16,0},{1,17},{17,1},{2,18},{18,2},{3,19},{19,3},{4,20},{20... | collective-permute-start | bytes 589832 | tf_op jit(solution)/shard_map/ppermute | solution.py:20
  531.7 27.3 %collective-permute-start.37 = (f32[16,1536]{1,0:T(8,128)S(1)}, f32[16,1536]{1,0:T(8,128)S(1)}, u32[]{:S(2)}, u32[]{:S(2)}) collective-permute-start(f32[16,1536]{1,0:T(8,128)S(1)} %fusion), channel_id=1, source_target_pairs={{0,28},{1,29},{2,30},{3,31},{4,32},{5,33},{6,34},{7,35},{8,36},{9,... | collective-permute-start | bytes 294920
  545.3 16.9 %collective-permute-start.36 = (f32[16,1536]{1,0:T(8,128)S(1)}, f32[16,1536]{1,0:T(8,128)S(1)}, u32[]{:S(2)}, u32[]{:S(2)}) collective-permute-start(f32[16,1536]{1,0:T(8,128)S(1)} %fusion), channel_id=1, source_target_pairs={{0,27},{1,28},{2,29},{3,30},{4,31},{5,32},{6,33},{7,34},{8,35},{9,... | collective-permute-start | bytes 294920
  546.6 20.3 %collective-permute-start.35 = (f32[16,1536]{1,0:T(8,128)S(1)}, f32[16,1536]{1,0:T(8,128)S(1)}, u32[]{:S(2)}, u32[]{:S(2)}) collective-permute-start(f32[16,1536]{1,0:T(8,128)S(1)} %fusion), channel_id=1, source_target_pairs={{0,26},{1,27},{2,28},{3,29},{4,30},{5,31},{6,32},{7,33},{8,34},{9,... | collective-permute-start | bytes 294920
  552.7 17.4 %collective-permute-start.34 = (f32[16,1536]{1,0:T(8,128)S(1)}, f32[16,1536]{1,0:T(8,128)S(1)}, u32[]{:S(2)}, u32[]{:S(2)}) collective-permute-start(f32[16,1536]{1,0:T(8,128)S(1)} %fusion), channel_id=1, source_target_pairs={{0,25},{1,26},{2,27},{3,28},{4,29},{5,30},{6,31},{7,32},{8,33},{9,... | collective-permute-start | bytes 294920
  554.1 17.9 %collective-permute-start.33 = (f32[16,1536]{1,0:T(8,128)S(1)}, f32[16,1536]{1,0:T(8,128)S(1)}, u32[]{:S(2)}, u32[]{:S(2)}) collective-permute-start(f32[16,1536]{1,0:T(8,128)S(1)} %fusion), channel_id=1, source_target_pairs={{0,24},{1,25},{2,26},{3,27},{4,28},{5,29},{6,30},{7,31},{8,32},{9,... | collective-permute-start | bytes 294920
  558.9 17.7 %collective-permute-start.32 = (f32[16,1536]{1,0:T(8,128)S(1)}, f32[16,1536]{1,0:T(8,128)}, u32[]{:S(2)}, u32[]{:S(2)}) collective-permute-start(f32[16,1536]{1,0:T(8,128)S(1)} %fusion), channel_id=1, source_target_pairs={{0,23},{1,24},{2,25},{3,26},{4,27},{5,28},{6,29},{7,30},{8,31},{9,... | collective-permute-start | bytes 294920
  562.2 18.5 %collective-permute-start.31 = (f32[16,1536]{1,0:T(8,128)S(1)}, f32[16,1536]{1,0:T(8,128)}, u32[]{:S(2)}, u32[]{:S(2)}) collective-permute-start(f32[16,1536]{1,0:T(8,128)S(1)} %fusion), channel_id=1, source_target_pairs={{0,22},{1,23},{2,24},{3,25},{4,26},{5,27},{6,28},{7,29},{8,30},{9,... | collective-permute-start | bytes 294920
  566.9 16.8 %collective-permute-start.30 = (f32[16,1536]{1,0:T(8,128)S(1)}, f32[16,1536]{1,0:T(8,128)}, u32[]{:S(2)}, u32[]{:S(2)}) collective-permute-start(f32[16,1536]{1,0:T(8,128)S(1)} %fusion), channel_id=1, source_target_pairs={{0,21},{1,22},{2,23},{3,24},{4,25},{5,26},{6,27},{7,28},{8,29},{9,... | collective-permute-start | bytes 294920
  586.5 17.3 %collective-permute-start.24 = (f32[16,1536]{1,0:T(8,128)S(1)}, f32[16,1536]{1,0:T(8,128)S(1)}, u32[]{:S(2)}, u32[]{:S(2)}) collective-permute-start(f32[16,1536]{1,0:T(8,128)S(1)} %fusion), channel_id=1, source_target_pairs={{0,15},{1,16},{2,17},{3,18},{4,19},{5,20},{6,21},{7,22},{8,23},{9,... | collective-permute-start | bytes 294920
  592.8 15.7 %collective-permute-start.22 = (f32[16,1536]{1,0:T(8,128)S(1)}, f32[16,1536]{1,0:T(8,128)}, u32[]{:S(2)}, u32[]{:S(2)}) collective-permute-start(f32[16,1536]{1,0:T(8,128)S(1)} %fusion), channel_id=1, source_target_pairs={{0,13},{1,14},{2,15},{3,16},{4,17},{5,18},{6,19},{7,20},{8,21},{9,... | collective-permute-start | bytes 294920
  608.5 15.8 %collective-permute-start.17 = (f32[16,1536]{1,0:T(8,128)S(1)}, f32[16,1536]{1,0:T(8,128)S(1)}, u32[]{:S(2)}, u32[]{:S(2)}) collective-permute-start(f32[16,1536]{1,0:T(8,128)S(1)} %fusion), channel_id=1, source_target_pairs={{0,8},{1,9},{2,10},{3,11},{4,12},{5,13},{6,14},{7,15},{8,16},{9,17... | collective-permute-start | bytes 294920
  610.0 18.1 %collective-permute-start.16 = (f32[16,1536]{1,0:T(8,128)S(1)}, f32[16,1536]{1,0:T(8,128)S(1)}, u32[]{:S(2)}, u32[]{:S(2)}) collective-permute-start(f32[16,1536]{1,0:T(8,128)S(1)} %fusion), channel_id=1, source_target_pairs={{0,7},{1,8},{2,9},{3,10},{4,11},{5,12},{6,13},{7,14},{8,15},{9,16}... | collective-permute-start | bytes 294920
  612.0 18.2 %collective-permute-start.15 = (f32[16,1536]{1,0:T(8,128)S(1)}, f32[16,1536]{1,0:T(8,128)S(1)}, u32[]{:S(2)}, u32[]{:S(2)}) collective-permute-start(f32[16,1536]{1,0:T(8,128)S(1)} %fusion), channel_id=1, source_target_pairs={{0,6},{1,7},{2,8},{3,9},{4,10},{5,11},{6,12},{7,13},{8,14},{9,15},... | collective-permute-start | bytes 294920
  615.2 19.2 %collective-permute-start.14 = (f32[16,1536]{1,0:T(8,128)S(1)}, f32[16,1536]{1,0:T(8,128)S(1)}, u32[]{:S(2)}, u32[]{:S(2)}) collective-permute-start(f32[16,1536]{1,0:T(8,128)S(1)} %fusion), channel_id=1, source_target_pairs={{0,5},{1,6},{2,7},{3,8},{4,9},{5,10},{6,11},{7,12},{8,13},{9,14},{... | collective-permute-start | bytes 294920
  620.8 54.6 %collective-permute-start.13 = (f32[16,1536]{1,0:T(8,128)S(1)}, f32[16,1536]{1,0:T(8,128)}, u32[]{:S(2)}, u32[]{:S(2)}) collective-permute-start(f32[16,1536]{1,0:T(8,128)S(1)} %fusion), channel_id=1, source_target_pairs={{0,4},{1,5},{2,6},{3,7},{4,8},{5,9},{6,10},{7,11},{8,12},{9,13},{1... | collective-permute-start | bytes 294920
  624.3 51.1 %collective-permute-start.12 = (f32[16,1536]{1,0:T(8,128)S(1)}, f32[16,1536]{1,0:T(8,128)}, u32[]{:S(2)}, u32[]{:S(2)}) collective-permute-start(f32[16,1536]{1,0:T(8,128)S(1)} %fusion), channel_id=1, source_target_pairs={{0,3},{1,4},{2,5},{3,6},{4,7},{5,8},{6,9},{7,10},{8,11},{9,12},{10... | collective-permute-start | bytes 294920
  628.1 47.3 %collective-permute-start.11 = (f32[16,1536]{1,0:T(8,128)S(1)}, f32[16,1536]{1,0:T(8,128)}, u32[]{:S(2)}, u32[]{:S(2)}) collective-permute-start(f32[16,1536]{1,0:T(8,128)S(1)} %fusion), channel_id=1, source_target_pairs={{0,2},{1,3},{2,4},{3,5},{4,6},{5,7},{6,8},{7,9},{8,10},{9,11},{10,... | collective-permute-start | bytes 294920
  630.2 45.2 %collective-permute-start.10 = (f32[16,1536]{1,0:T(8,128)S(1)}, f32[16,1536]{1,0:T(8,128)}, u32[]{:S(2)}, u32[]{:S(2)}) collective-permute-start(f32[16,1536]{1,0:T(8,128)S(1)} %fusion), channel_id=1, source_target_pairs={{0,1},{1,2},{2,3},{3,4},{4,5},{5,6},{6,7},{7,8},{8,9},{9,10},{10,1... | collective-permute-start | bytes 294920
  635.1 92.1 %collective-permute-start.8 = (bf16[32,3072]{1,0:T(8,128)(2,1)}, bf16[32,3072]{1,0:T(8,128)(2,1)}, u32[]{:S(2)}, u32[]{:S(2)}) collective-permute-start(bf16[32,3072]{1,0:T(8,128)(2,1)} %fusion.45), channel_id=1, source_target_pairs={{0,2},{2,0},{1,3},{3,1},{4,6},{6,4},{5,7},{7,5},{8,10},{10,8},{9,1... | collective-permute-start | bytes 589832 | tf_op jit(solution)/shard_map/ppermute | solution.py:20
  (79 other events, 1525.0 us)
where the time goes:
time: 764 us; the launch traced here: 753 us
  blocking collectives  377 us (49%)
  local copies, waits for them, and re-layouts  153 us (20%)
  starting transfers between devices  112 us (15%)
  other arithmetic  70 us (9%)
  matrix products  36.1 us (5%)
    unnamed x1, blocking collectives  377 us
    unnamed x32, starting transfers between devices  96.1 us
    unnamed x127, local copies, waits for them, and re-layouts  58 us
    reduce_sum x2, other arithmetic, collect_level(): summed = grads.reshape(nodes, 2 ** level, BS, width).sum(axis=1)  18.8 us
    ppermute x10, starting transfers between devices, swapped(): return lax.ppermute(block, axis, route)  16.1 us
  transfers between devices with their start and end apart: 42, of which 3 were waited for; matrix products, arithmetic and copies ran while one was open for 23% of the time, Pallas kernels for 0%

commit v1 on v0

v1 whole, which is shorter than its diff:
```python
import math
import jax
import jax.numpy as jnp
from jax import lax
from jax.experimental import pallas as pl
from jax.experimental.pallas import tpu as pltpu
from jax.sharding import PartitionSpec as P
H=12; HD=128; BS=32; D=1536; T=256
BF=jnp.bfloat16; F=jnp.float32
HS=2
NT=(((1,),(1,)),((),()))
TN=(((0,),(0,)),((),()))
NN=(((1,),(0,)),((),()))
def mm(a,b,dims): return lax.dot_general(a,b,dims,preferred_element_type=F)

def head(q,k0,v0,k12,v12,xk,xv,ga,xbias,expand):
    scale=HD**-0.5
    kall=jnp.concatenate([k0,k12,xk],0)
    vall=jnp.concatenate([v0,v12,xv],0)
    s_all=mm(kall,q,NT)
    g_all=mm(vall,ga,NT)
    low=lax.broadcasted_iota(jnp.int32,(1,128),1)<64
    ln2=math.log(2.0)
    att=[];gq=[];ps=[];gs_=[];g0=[];g1=[];g2=[None,None]
    def pick(full,j):
        c=full[:,128*j:128*j+128]
        a=jnp.where(low,c[128*j:128*j+64],c[128*j+64:128*j+128])
        b=jnp.where(low,c[256+64*j+32:256+64*j+64],c[256+64*j:256+64*j+32])
        d=c[384+32*(1-j):384+32*(2-j)]
        return a,b,d,c[448:608]
    def widen(x):
        z=jnp.zeros_like(x[:64]); lowb=jnp.broadcast_to(low,(64,128)); lowc=jnp.broadcast_to(low,(32,128))
        a=x[:64]; b=x[64:96]; zb=jnp.zeros_like(b)
        return jnp.concatenate([jnp.where(lowb,a,z),jnp.where(lowb,z,a),jnp.where(lowc,zb,b),jnp.where(lowc,b,zb),x[96:]],0)
    for j in range(2):
        a,b,d,x=pick(s_all,j)
        s=jnp.concatenate([a*scale,b*scale+ln2,d*scale+2*ln2,x*scale+xbias],0)
        m=jnp.max(s,axis=0,keepdims=True)
        e=jnp.exp(s-m)
        l=jnp.sum(e,axis=0,keepdims=True)
        p=e*(1.0/l)
        pb=p.astype(BF)
        gp=jnp.concatenate(pick(g_all,j),0)
        delta=jnp.sum(pb.astype(F)*gp,axis=0,keepdims=True)
        gs=(p*(gp-delta)*scale).astype(BF)
        pw=widen(pb); gw=widen(gs)
        rows=slice(128*j,128*j+128); o=1-j
        kh=jnp.concatenate([k0[rows],k12[64*j:64*j+64],k12[128+32*o:160+32*o],xk],0)
        vh=jnp.concatenate([v0[rows],v12[64*j:64*j+64],v12[128+32*o:160+32*o],xv],0)
        att.append(mm(pw,vh,TN)); gq.append(mm(gw,kh,TN))
        gk=mm(gw[:224],q[rows],NN); gv=mm(pw[:224],ga[rows],NN)
        both=jnp.concatenate([gk,gv],1)
        g0.append(both[:128]); g1.append(both[128:192]); g2[o]=both[192:224]
        ps.append(pw[224:]); gs_.append(gw[224:])
    gxk=mm(jnp.concatenate(gs_,1),q,NN); gxv=mm(jnp.concatenate(ps,1),ga,NN)
    g0=jnp.concatenate(g0,0); g12=jnp.concatenate(g1+g2,0).astype(BF)
    fine=g0+mm(expand,g12,NN)
    return jnp.concatenate(att,0),jnp.concatenate(gq,0),fine[:,:128],fine[:,128:],gxk,gxv

def expansion():
    r=lax.broadcasted_iota(jnp.int32,(T,192),0); c=lax.broadcasted_iota(jnp.int32,(T,192),1)
    return jnp.where(c<128,jnp.where((r>>1)==c,0.5,0.0),jnp.where((r>>2)==c-128,0.25,0.0)).astype(BF)

def attention_kernel(q,k0,v0,k12,v12,xk,xv,ga,go,att_o,gq_o,fk_o,fv_o,gxk_o,gxv_o,gw_o):
    expand=expansion()
    r=lax.broadcasted_iota(jnp.int32,(160,1),0)
    ln2=math.log(2.0)
    xb=(3+ (r>>5)).astype(F)*ln2
    for i in range(HS):
        c=slice(i*HD,i*HD+HD)
        att,gq,fk,fv,gxk,gxv=head(q[:,c],k0[:,c],v0[:,c],k12[:,c],v12[:,c],xk[:,c],xv[:,c],ga[:,c],xb,expand)
        attb=att.astype(BF)
        att_o[:,c]=attb; gq_o[:,c]=gq.astype(BF); fk_o[:,c]=fk; fv_o[:,c]=fv
        gxk_o[:,c]=gxk; gxv_o[:,c]=gxv
        gw_o[i*HD:i*HD+HD,:]=mm(attb,go[...],TN).astype(BF)

def attention(q,k,v,l12,xs,ga,go):
    W=HS*HD; n=H//HS
    def sp(rows,off=0): return pl.BlockSpec((rows,W),lambda h:(0,h+off))
    return pl.pallas_call(attention_kernel,grid=(n,),
        in_specs=[sp(T),sp(T),sp(T),sp(192),sp(192,n),sp(160),sp(160,n),sp(T),pl.BlockSpec((T,D),lambda h:(0,0))],
        out_specs=[sp(T),sp(T),sp(T),sp(T),sp(160),sp(160),pl.BlockSpec((W,D),lambda h:(h,0))],
        out_shape=[jax.ShapeDtypeStruct((T,D),BF)]*2+[jax.ShapeDtypeStruct((T,D),F)]*2+[jax.ShapeDtypeStruct((160,D),F)]*2+[jax.ShapeDtypeStruct((D,D),BF)],
        compiler_params=pltpu.CompilerParams(vmem_limit_bytes=48*2**20),name="attention")(q,k,v,l12,l12,xs,xs,ga,go)

def pyramid_kernel(k,v,l12,l3):
    def avg(n):
        r=lax.broadcasted_iota(jnp.int32,(n,2*n),0); c=lax.broadcasted_iota(jnp.int32,(n,2*n),1)
        return jnp.where((c>>1)==r,0.5,0.0).astype(BF)
    a1,a2,a3=avg(128),avg(64),avg(32)
    for i,x in enumerate((k,v)):
        c=slice(i*D,i*D+D)
        x1=mm(a1,x[...],NN).astype(BF); x2=mm(a2,x1,NN).astype(BF); x3=mm(a3,x2,NN).astype(BF)
        l12[:128,c]=x1; l12[128:,c]=x2; l3[:,c]=x3

def pyramid(k,v):
    return pl.pallas_call(pyramid_kernel,out_shape=[jax.ShapeDtypeStruct((192,2*D),BF),jax.ShapeDtypeStruct((32,2*D),BF)],
        compiler_params=pltpu.CompilerParams(vmem_limit_bytes=48*2**20),name="pyramid")(k,v)


def fold_matrix(n):
    r = lax.broadcasted_iota(jnp.int32, (n, 2 * n), 0)
    c = lax.broadcasted_iota(jnp.int32, (n, 2 * n), 1)
    return jnp.where((c >> 1) == r, 0.5, 0.0).astype(BF)


def spread_matrix(n, bits):
    r = lax.broadcasted_iota(jnp.int32, (n << bits, n), 0)
    c = lax.broadcasted_iota(jnp.int32, (n << bits, n), 1)
    return jnp.where((r >> bits) == c, 0.5**bits, 0.0).astype(BF)


def chip_kernel(mine, other, l4, l5):
    x = jnp.concatenate([mine[...], other[...]], 0)
    x = mm(fold_matrix(32), x, NN).astype(BF)
    l4[...] = x
    l5[...] = mm(fold_matrix(16), x, NN).astype(BF)


def row_kernel(l5, z1, z2, z3, l6, l7):
    x = jnp.concatenate([l5[...], mm(fold_matrix(16), z1[...], NN).astype(BF), z2[...], z3[...]], 0)
    x = mm(fold_matrix(32), x, NN).astype(BF)
    l6[...] = x
    l7[...] = mm(fold_matrix(16), x, NN).astype(BF)


def spread(x, bits):
    return mm(spread_matrix(x.shape[0], bits), x.astype(BF), NN)


def back_row_kernel(gk, gv, y1, y2, y3, s1, s2, s3, own):
    g6 = y1[...].astype(F) + spread(y2[...].astype(F) + y3[...].astype(F), 1)
    for i, g in enumerate((gk, gv)):
        c = slice(i * D, i * D + D)
        s1[:, c] = (g[32:64, :] + spread(g6[8:16, c], 2)).astype(BF)
        s2[:, c] = (g[64:80, :] + spread(g6[16:24, c], 1)).astype(BF)
        s3[:, c] = (g[80:96, :] + spread(g6[24:32, c], 1)).astype(BF)
        own[:, c] = spread(g6[:8, c], 2)


def back_chip_kernel(gk, gv, own, z1, z2, z3, send, keep):
    g4 = own[...] + z1[...].astype(F) + spread(z2[...].astype(F) + z3[...].astype(F), 1)
    for i, g in enumerate((gk, gv)):
        c = slice(i * D, i * D + D)
        send[:, c] = (g[:32, :] + spread(g4[16:, c], 1)).astype(BF)
        keep[:, c] = spread(g4[:16, c], 1)


def finish_kernel(fk, fv, keep, c1, ok, ov):
    g3 = keep[...] + c1[...].astype(F)
    for i, (f, o) in enumerate(((fk, ok), (fv, ov))):
        c = slice(i * D, i * D + D)
        o[...] = (f[...] + spread(g3[:, c], 3)).astype(BF)


def small(kernel, shapes, name):
    return pl.pallas_call(
        kernel,
        out_shape=[jax.ShapeDtypeStruct(s, t) for s, t in shapes],
        compiler_params=pltpu.CompilerParams(vmem_limit_bytes=48 * 2**20),
        name=name,
    )


def across(x, flip):
    return lax.ppermute(x, "seq", [(i, i ^ flip) for i in range(32)])


def along_x(x, step):
    return lax.ppermute(x, "dp", [(i, (i + step) % 4) for i in range(4)])


def along_y(x, step):
    return lax.ppermute(x, "seq", [(i, (i + 8 * step) % 32) for i in range(32)])


def along_z(x, step):
    return lax.ppermute(x, "seq", [(i, i // 8 * 8 + (i + 2 * step) % 8) for i in range(32)])


def scatter_four(rows, move, place):
    n = rows.shape[0] // 4

    def part(i):
        return lax.dynamic_slice_in_dim(rows, i % 4 * n, n, 0)

    total = part(place).astype(F)
    for step in (1, 2, 3):
        total = total + move(part(place + step), step).astype(F)
    return total


def local(query, key, value, w_out, grad_out):
    q, k, v, go = query[0], key[0], value[0], grad_out[0]
    place = lax.axis_index("seq")
    l12, l3 = pyramid(k, v)
    c1 = across(l3, 1)
    ga = mm(go, w_out, NT).astype(BF)
    W = 2 * D
    l4, l5 = small(chip_kernel, [((32, W), BF), ((16, W), BF)], "chip")(l3, c1)
    z1, z2, z3 = across(l4, 2), across(l5, 4), across(l5, 6)
    l6, l7 = small(row_kernel, [((32, W), BF), ((16, W), BF)], "row")(l5, z1, z2, z3)
    y1, y2, y3 = across(l6, 8), across(l7, 16), across(l7, 24)
    xs = jnp.concatenate([c1, z1, z2, z3, y1, y2, y3], 0)
    att, gq, fk, fv, gxk, gxv, gw = attention(q, k, v, l12, xs, ga, go)
    gxb = jnp.concatenate([gxk[96:], gxv[96:]], 1).astype(BF)
    y1, y2, y3 = across(gxb[:32], 8), across(gxb[32:48], 16), across(gxb[48:], 24)
    s1, s2, s3, own = small(
        back_row_kernel, [((32, W), BF), ((16, W), BF), ((16, W), BF), ((32, W), F)], "back_row"
    )(gxk, gxv, y1, y2, y3)
    z1, z2, z3 = across(s1, 2), across(s2, 4), across(s3, 6)
    send, keep = small(back_chip_kernel, [((32, W), BF), ((32, W), F)], "back_chip")(
        gxk, gxv, own, z1, z2, z3
    )
    c1 = across(send, 1)
    gk, gv = small(finish_kernel, [((T, D), BF), ((T, D), BF)], "finish")(fk, fv, keep, c1)
    mixed = mm(att, w_out, NN).astype(BF)
    core = place % 2
    half = D // 2
    mine = lax.dynamic_slice_in_dim(gw, core * half, half, 1)
    theirs = lax.dynamic_slice_in_dim(gw, (1 - core) * half, half, 1)
    part = (mine.astype(F) + across(theirs, 1).astype(F)).astype(BF)
    part = scatter_four(part, along_x, lax.axis_index("dp")).astype(BF)
    part = scatter_four(part, along_y, place // 8).astype(BF)
    part = scatter_four(part, along_z, place // 2 % 4)
    first = core == 0
    mine = jnp.where(first, part[:12], part[12:])
    theirs = across(jnp.where(first, part[12:], part[:12]), 1)
    total = jnp.concatenate([jnp.where(first, mine, theirs), jnp.where(first, theirs, mine)], 1)
    gw = total * (1.0 / math.sqrt(4 * 32 * T))
    return mixed[None], gq[None], gk[None], gv[None], gw


def solution(mesh):
    rows = P("dp", "seq", None)
    return jax.shard_map(
        local,
        mesh=mesh,
        in_specs=(rows, rows, rows, P(), rows),
        out_specs=(rows, rows, rows, rows, P(("dp", "seq"), None)),
        check_vma=False,
    )
```

time: 764 us -> 136 us (0.18); the launches traced: 753 us -> 136 us
  blocking collectives: 377 us -> 0 us
  local copies, waits for them, and re-layouts: 153 us -> 10.9 us
  starting transfers between devices: 112 us -> 32.2 us
  other arithmetic: 70 us -> 6.02 us
  waiting for transfers between devices: 2.11 us -> 56.7 us
  matrix products: 36.1 us -> 9.63 us
  Pallas kernels: 0 us -> 19.2 us
    unnamed x1 -> x0, blocking collectives: 377 us -> none
    unnamed x32 -> x0, starting transfers between devices: 96.1 us -> none
    ppermute x10 -> x25, waiting for transfers between devices: 1.04 us -> 56.7 us  [the longest x16 28.6 us: across(): return lax.ppermute(x, 'seq', [(i, i ^ flip) for i in range(32)])]
    unnamed x127 -> x38, local copies, waits for them, and re-layouts: 58 us -> 5.58 us
    slice x11 -> x2, local copies, waits for them, and re-layouts: 30.2 us -> 0.05 us  [local(): gxb = jnp.concatenate([gxk[96:], gxv[96:]], 1).astype(BF)]
    dot_general x13 -> x2, matrix products: 34.9 us -> 9.63 us  [mm(): return lax.dot_general(a, b, dims, preferred_element_type=F)]
    reduce_sum x4 -> x0, other arithmetic: 20.9 us -> none  [the longest x2 18.8 us: collect_level(): summed = grads.reshape(nodes, 2 ** level, BS, width).sum(axis=1)]
    pallas_call x0 -> x7, Pallas kernels: none -> 19.2 us  [the longest x1 14.5 us: attention(): pl.pallas_call(attention_kernel, grid=(n,), in_specs=[sp(T), sp(T), sp(T)...]
  transfers between devices with their start and end apart: 42 -> 25, of which waited for: 3 -> 10; matrix products, arithmetic and copies ran while one was open for 23% -> 10% of each run, Pallas kernels for 0% -> 2%
where the time goes in v1:
time: 136 us
  waiting for transfers between devices  56.7 us (42%)
  starting transfers between devices  32.2 us (24%)
  Pallas kernels  19.2 us (14%)
  local copies, waits for them, and re-layouts  10.9 us (8%)
  matrix products  9.63 us (7%)
  other arithmetic  6.02 us (4%)
    ppermute x16, waiting for transfers between devices, across(): return lax.ppermute(x, 'seq', [(i, i ^ flip) for i in range(32)])  28.6 us
    ppermute x3, waiting for transfers between devices, along_x(): return lax.ppermute(x, 'dp', [(i, (i + step) % 4) for i in range(4)])  25.8 us
    ppermute x16, starting transfers between devices, across(): return lax.ppermute(x, 'seq', [(i, i ^ flip) for i in range(32)])  24.7 us
    pallas_call x1, Pallas kernels, attention(): pl.pallas_call(attention_kernel, grid=(n,), in_specs=[sp(T), sp(T), sp(T)...  14.5 us
    dot_general x2, matrix products, mm(): return lax.dot_general(a, b, dims, preferred_element_type=F)  9.63 us
    unnamed x38, local copies, waits for them, and re-layouts  5.58 us
    ppermute x3, starting transfers between devices, along_x(): return lax.ppermute(x, 'dp', [(i, (i + step) % 4) for i in range(4)])  3.66 us
    dynamic_slice x1, local copies, waits for them, and re-layouts, local(): theirs = lax.dynamic_slice_in_dim(gw, (1 - core) * half, half, 1)  3.61 us
  transfers between devices with their start and end apart: 25, of which 10 were waited for; matrix products, arithmetic and copies ran while one was open for 10% of the time, Pallas kernels for 2%

profile of v1, /device:TPU:1, one launch (start us, length us, event | category | flops | bytes accessed | tf_op | source)
XLA Modules:
  0.0 135.5 jit_solution(9515525563173733279)
XLA Ops:
  5.4 4.9 %convolution_convert_fusion.1.ga = bf16[256,1536]{1,0:T(8,128)(2,1)} fusion(bf16[1536,1536]{1,0:T(8,128)(2,1)} %param.8, bf16[1,256,1536]{2,1,0:T(8,128)(2,1)} %param.9), kind=kOutput, calls=%fused_computation.2 | convolution fusion | flops 1208352768 | bytes 6291456 | tf_op jit(solution)/shard_map/dot_general | solution.py:14
  10.6 3.8 %collective-permute-start.2 = (bf16[16,3072]{1,0:T(8,128)(2,1)S(1)}, bf16[16,3072]{1,0:T(8,128)(2,1)S(1)}, u32[]{:S(2)}, u32[]{:S(2)}) collective-permute-start(bf16[16,3072]{1,0:T(8,128)(2,1)S(1)} %get-tuple-element.29.l5), channel_id=1, source_target_pairs={{0,4},{1,5},{2,6},{3,7},{4,0},{5,1},{6,2},{7,3},{8,12},{9,13},{10,... | collective-permute-start | bytes 294920 | tf_op jit(solution)/shard_map/ppermute | solution.py:166
  15.1 2.1 %collective-permute-done.2.z2 = bf16[16,3072]{1,0:T(8,128)(2,1)S(1)} collective-permute-done((bf16[16,3072]{1,0:T(8,128)(2,1)S(1)}, bf16[16,3072]{1,0:T(8,128)(2,1)S(1)}, u32[]{:S(2)}, u32[]{:S(2)}) %collective-permute-start.2) | collective-permute-done | bytes 98336 | tf_op jit(solution)/shard_map/ppermute | solution.py:166
  17.2 2.0 %collective-permute-done.3.z3 = bf16[16,3072]{1,0:T(8,128)(2,1)S(1)} collective-permute-done((bf16[16,3072]{1,0:T(8,128)(2,1)S(1)}, bf16[16,3072]{1,0:T(8,128)(2,1)S(1)}, u32[]{:S(2)}, u32[]{:S(2)}) %collective-permute-start.3) | collective-permute-done | bytes 98336 | tf_op jit(solution)/shard_map/ppermute | solution.py:166
  19.2 2.6 %collective-permute-done.1.z1 = bf16[32,3072]{1,0:T(8,128)(2,1)S(1)} collective-permute-done((bf16[32,3072]{1,0:T(8,128)(2,1)S(1)}, bf16[32,3072]{1,0:T(8,128)(2,1)S(1)}, u32[]{:S(2)}, u32[]{:S(2)}) %collective-permute-start.1) | collective-permute-done | bytes 196640 | tf_op jit(solution)/shard_map/ppermute | solution.py:166
  22.3 3.0 %collective-permute-start.5 = (bf16[16,3072]{1,0:T(8,128)(2,1)S(1)}, bf16[16,3072]{1,0:T(8,128)(2,1)S(1)}, u32[]{:S(2)}, u32[]{:S(2)}) collective-permute-start(bf16[16,3072]{1,0:T(8,128)(2,1)S(1)} %get-tuple-element.31), channel_id=1, source_target_pairs={{0,16},{1,17},{2,18},{3,19},{4,20},{5,21},{6,22},{7,23},{8,24},{9,... | collective-permute-start | bytes 294920 | tf_op jit(solution)/shard_map/ppermute | solution.py:166
  26.1 6.3 %collective-permute-done.4 = bf16[32,3072]{1,0:T(8,128)(2,1)S(1)} collective-permute-done((bf16[32,3072]{1,0:T(8,128)(2,1)S(1)}, bf16[32,3072]{1,0:T(8,128)(2,1)S(1)}, u32[]{:S(2)}, u32[]{:S(2)}) %collective-permute-start.4) | collective-permute-done | bytes 196640 | tf_op jit(solution)/shard_map/ppermute | solution.py:166
  35.8 14.5 %attention.1 = (bf16[256,1536]{1,0:T(8,128)(2,1)S(1)}, bf16[256,1536]{1,0:T(8,128)(2,1)}, f32[256,1536]{1,0:T(8,128)}, f32[256,1536]{1,0:T(8,128)}, f32[160,1536...) custom-call(bf16[256,1536]{1,0:T(8,128)(2,1)S(1)} %bitcast.18, bf16[256,1536]{1,0:T(8,128)(2,1)S(1)} %bitcast.15, ...), custom_call_target="tpu_custom_call" | custom-call | tf_op jit(solution)/shard_map/attention/pallas_call | solution.py:80
  50.3 3.6 %constant_dynamic-slice_fusion.9 = bf16[1536,768]{1,0:T(8,128)(2,1)} fusion(bf16[1536,1536]{1,0:T(8,128)(2,1)} %get-tuple-element.46, s32[]{:T(128)S(6)} %select_n.131), kind=kLoop, calls=%fused_computation.37 | loop fusion | bytes 4718596 | tf_op jit(solution)/shard_map/dynamic_slice | solution.py:221
  53.9 1.8 %collective-permute-start.14 = (bf16[1536,768]{1,0:T(8,128)(2,1)}, bf16[1536,768]{1,0:T(8,128)(2,1)}, u32[]{:S(2)}, u32[]{:S(2)}) collective-permute-start(bf16[1536,768]{1,0:T(8,128)(2,1)} %constant_dynamic-slice_fusion.9), channel_id=1, source_target_pairs={{0,1},{1,0},{2,3},{3,2},{4,5},{5,4},{6,7},{7,6},{8,9},{9,8},{10,11... | collective-permute-start | bytes 7077896 | tf_op jit(solution)/shard_map/ppermute | solution.py:166
  55.8 4.4 %collective-permute-done.14 = bf16[1536,768]{1,0:T(8,128)(2,1)} collective-permute-done((bf16[1536,768]{1,0:T(8,128)(2,1)}, bf16[1536,768]{1,0:T(8,128)(2,1)}, u32[]{:S(2)}, u32[]{:S(2)}) %collective-permute-start.14) | collective-permute-done | bytes 2359328 | tf_op jit(solution)/shard_map/ppermute | solution.py:166
  60.2 3.0 %add_convert_fusion = bf16[1536,768]{1,0:T(8,128)(2,1)S(1)} fusion(bf16[1536,768]{1,0:T(8,128)(2,1)} %collective-permute-done.14, bf16[1536,1536]{1,0:T(8,128)(2,1)} %get-tuple-element.46, s32[]{:T(128)S(6)} %select_n.130), kind=kLoop, calls=%fused_computation | loop fusion | flops 4718592 | bytes 7077892 | tf_op jit(solution)/shard_map/convert_element_type | solution.py:222
  63.3 2.5 %collective-permute-start.17 = (bf16[384,768]{1,0:T(8,128)(2,1)S(1)}, bf16[384,768]{1,0:T(8,128)(2,1)S(1)}, u32[]{:S(2)}, u32[]{:S(2)}) collective-permute-start(bf16[384,768]{1,0:T(8,128)(2,1)S(1)} %get-tuple-element.48), channel_id=1, source_target_pairs={{0,96},{32,0},{64,32},{96,64},{1,97},{33,1},{65,33},{97,65},{2,98}... | collective-permute-start | bytes 1769480 | tf_op jit(solution)/shard_map/ppermute | solution.py:170
  67.6 1.9 %collective-permute-start.8 = (bf16[16,3072]{1,0:T(8,128)(2,1)S(1)}, bf16[16,3072]{1,0:T(8,128)(2,1)S(1)}, u32[]{:S(2)}, u32[]{:S(2)}) collective-permute-start(bf16[16,3072]{1,0:T(8,128)(2,1)S(1)} %get-tuple-element.54), channel_id=1, source_target_pairs={{0,16},{1,17},{2,18},{3,19},{4,20},{5,21},{6,22},{7,23},{8,24},{9,... | collective-permute-start | bytes 294920 | tf_op jit(solution)/shard_map/ppermute | solution.py:166
  69.5 21.2 %collective-permute-done.17 = bf16[384,768]{1,0:T(8,128)(2,1)S(1)} collective-permute-done((bf16[384,768]{1,0:T(8,128)(2,1)S(1)}, bf16[384,768]{1,0:T(8,128)(2,1)S(1)}, u32[]{:S(2)}, u32[]{:S(2)}) %collective-permute-start.17) | collective-permute-done | bytes 589856 | tf_op jit(solution)/shard_map/ppermute | solution.py:170
  90.7 4.6 %collective-permute-done.15 = bf16[384,768]{1,0:T(8,128)(2,1)S(1)} collective-permute-done((bf16[384,768]{1,0:T(8,128)(2,1)S(1)}, bf16[384,768]{1,0:T(8,128)(2,1)S(1)}, u32[]{:S(2)}, u32[]{:S(2)}) %collective-permute-start.15) | collective-permute-done | bytes 589856 | tf_op jit(solution)/shard_map/ppermute | solution.py:170
  98.9 2.5 %collective-permute-start.9 = (bf16[16,3072]{1,0:T(8,128)(2,1)S(1)}, bf16[16,3072]{1,0:T(8,128)(2,1)S(1)}, u32[]{:S(2)}, u32[]{:S(2)}) collective-permute-start(bf16[16,3072]{1,0:T(8,128)(2,1)S(1)} %get-tuple-element.53), channel_id=1, source_target_pairs={{0,24},{1,25},{2,26},{3,27},{4,28},{5,29},{6,30},{7,31},{8,16},{9,... | collective-permute-start | bytes 294920 | tf_op jit(solution)/shard_map/ppermute | solution.py:166
  101.4 8.8 %collective-permute-done.9.y3 = bf16[16,3072]{1,0:T(8,128)(2,1)S(1)} collective-permute-done((bf16[16,3072]{1,0:T(8,128)(2,1)S(1)}, bf16[16,3072]{1,0:T(8,128)(2,1)S(1)}, u32[]{:S(2)}, u32[]{:S(2)}) %collective-permute-start.9) | collective-permute-done | bytes 98336 | tf_op jit(solution)/shard_map/ppermute | solution.py:166
  112.0 1.8 %collective-permute-start.11 = (bf16[16,3072]{1,0:T(8,128)(2,1)S(1)}, bf16[16,3072]{1,0:T(8,128)(2,1)S(1)}, u32[]{:S(2)}, u32[]{:S(2)}) collective-permute-start(bf16[16,3072]{1,0:T(8,128)(2,1)S(1)} %get-tuple-element.40), channel_id=1, source_target_pairs={{0,4},{1,5},{2,6},{3,7},{4,0},{5,1},{6,2},{7,3},{8,12},{9,13},{10,... | collective-permute-start | bytes 294920 | tf_op jit(solution)/shard_map/ppermute | solution.py:166
  118.5 2.2 %collective-permute-done.11.z2 = bf16[16,3072]{1,0:T(8,128)(2,1)S(1)} collective-permute-done((bf16[16,3072]{1,0:T(8,128)(2,1)S(1)}, bf16[16,3072]{1,0:T(8,128)(2,1)S(1)}, u32[]{:S(2)}, u32[]{:S(2)}) %collective-permute-start.11) | collective-permute-done | bytes 98336 | tf_op jit(solution)/shard_map/ppermute | solution.py:166
  121.1 2.0 %collective-permute-start.13 = (bf16[32,3072]{1,0:T(8,128)(2,1)S(1)}, bf16[32,3072]{1,0:T(8,128)(2,1)S(1)}, u32[]{:S(2)}, u32[]{:S(2)}) collective-permute-start(bf16[32,3072]{1,0:T(8,128)(2,1)S(1)} %get-tuple-element.43), channel_id=1, source_target_pairs={{0,1},{1,0},{2,3},{3,2},{4,5},{5,4},{6,7},{7,6},{8,9},{9,8},{10,11... | collective-permute-start | bytes 589832 | tf_op jit(solution)/shard_map/ppermute | solution.py:166
  123.1 2.4 %collective-permute-done.21 = bf16[24,768]{1,0:T(8,128)(2,1)} collective-permute-done((bf16[24,768]{1,0:T(8,128)(2,1)}, bf16[24,768]{1,0:T(8,128)(2,1)}, u32[]{:S(2)}, u32[]{:S(2)}) %collective-permute-start.21) | collective-permute-done | bytes 36896 | tf_op jit(solution)/shard_map/ppermute | solution.py:178
  126.3 2.3 %collective-permute-start.24 = (f32[12,768]{1,0:T(8,128)S(1)}, f32[12,768]{1,0:T(8,128)S(1)}, u32[]{:S(2)}, u32[]{:S(2)}) collective-permute-start(f32[12,768]{1,0:T(8,128)S(1)} %slice_select_fusion), channel_id=1, source_target_pairs={{0,1},{1,0},{2,3},{3,2},{4,5},{5,4},{6,7},{7,6},{8,9},{9,8},{10,11... | collective-permute-start | bytes 110600 | tf_op jit(solution)/shard_map/ppermute | solution.py:166
  128.6 4.7 %fusion = bf16[1,256,1536]{2,1,0:T(8,128)(2,1)} fusion(bf16[256,1536]{1,0:T(8,128)(2,1)S(1)} %copy-done.12, bf16[1536,1536]{1,0:T(8,128)(2,1)} %param.8), kind=kOutput, calls=%fused_computation.3 | convolution fusion | flops 1208352768 | bytes 6291456 | tf_op jit(solution)/shard_map/dot_general | solution.py:14
  (89 shorter events, 25.5 us)
Async XLA Ops:
  3.9 6.4 %collective-permute-start = (bf16[32,3072]{1,0:T(8,128)(2,1)S(1)}, bf16[32,3072]{1,0:T(8,128)(2,1)S(1)}, u32[]{:S(2)}, u32[]{:S(2)}) collective-permute-start(bf16[32,3072]{1,0:T(8,128)(2,1)S(1)} %get-tuple-element.27.mine), channel_id=1, source_target_pairs={{0,1},{1,0},{2,3},{3,2},{4,5},{5,4},{6,7},{7,6},{8,9},{9,8},{10,11... | collective-permute-start | bytes 589832 | tf_op jit(solution)/shard_map/ppermute | solution.py:166
  10.6 6.6 %collective-permute-start.2 = (bf16[16,3072]{1,0:T(8,128)(2,1)S(1)}, bf16[16,3072]{1,0:T(8,128)(2,1)S(1)}, u32[]{:S(2)}, u32[]{:S(2)}) collective-permute-start(bf16[16,3072]{1,0:T(8,128)(2,1)S(1)} %get-tuple-element.29.l5), channel_id=1, source_target_pairs={{0,4},{1,5},{2,6},{3,7},{4,0},{5,1},{6,2},{7,3},{8,12},{9,13},{10,... | collective-permute-start | bytes 294920 | tf_op jit(solution)/shard_map/ppermute | solution.py:166
  14.4 4.9 %collective-permute-start.3 = (bf16[16,3072]{1,0:T(8,128)(2,1)S(1)}, bf16[16,3072]{1,0:T(8,128)(2,1)S(1)}, u32[]{:S(2)}, u32[]{:S(2)}) collective-permute-start(bf16[16,3072]{1,0:T(8,128)(2,1)S(1)} %get-tuple-element.29.l5), channel_id=1, source_target_pairs={{0,6},{1,7},{2,4},{3,5},{4,2},{5,3},{6,0},{7,1},{8,14},{9,15},{10,... | collective-permute-start | bytes 294920 | tf_op jit(solution)/shard_map/ppermute | solution.py:166
  14.8 7.1 %collective-permute-start.1 = (bf16[32,3072]{1,0:T(8,128)(2,1)S(1)}, bf16[32,3072]{1,0:T(8,128)(2,1)S(1)}, u32[]{:S(2)}, u32[]{:S(2)}) collective-permute-start(bf16[32,3072]{1,0:T(8,128)(2,1)S(1)} %get-tuple-element.28), channel_id=1, source_target_pairs={{0,2},{1,3},{2,0},{3,1},{4,6},{5,7},{6,4},{7,5},{8,10},{9,11},{10,... | collective-permute-start | bytes 589832 | tf_op jit(solution)/shard_map/ppermute | solution.py:166
  22.3 10.2 %collective-permute-start.5 = (bf16[16,3072]{1,0:T(8,128)(2,1)S(1)}, bf16[16,3072]{1,0:T(8,128)(2,1)S(1)}, u32[]{:S(2)}, u32[]{:S(2)}) collective-permute-start(bf16[16,3072]{1,0:T(8,128)(2,1)S(1)} %get-tuple-element.31), channel_id=1, source_target_pairs={{0,16},{1,17},{2,18},{3,19},{4,20},{5,21},{6,22},{7,23},{8,24},{9,... | collective-permute-start | bytes 294920 | tf_op jit(solution)/shard_map/ppermute | solution.py:166
  25.3 7.2 %collective-permute-start.6 = (bf16[16,3072]{1,0:T(8,128)(2,1)S(1)}, bf16[16,3072]{1,0:T(8,128)(2,1)S(1)}, u32[]{:S(2)}, u32[]{:S(2)}) collective-permute-start(bf16[16,3072]{1,0:T(8,128)(2,1)S(1)} %get-tuple-element.31), channel_id=1, source_target_pairs={{0,24},{1,25},{2,26},{3,27},{4,28},{5,29},{6,30},{7,31},{8,16},{9,... | collective-permute-start | bytes 294920 | tf_op jit(solution)/shard_map/ppermute | solution.py:166
  26.1 6.4 %collective-permute-start.4 = (bf16[32,3072]{1,0:T(8,128)(2,1)S(1)}, bf16[32,3072]{1,0:T(8,128)(2,1)S(1)}, u32[]{:S(2)}, u32[]{:S(2)}) collective-permute-start(bf16[32,3072]{1,0:T(8,128)(2,1)S(1)} %get-tuple-element.30), channel_id=1, source_target_pairs={{0,8},{1,9},{2,10},{3,11},{4,12},{5,13},{6,14},{7,15},{8,0},{9,1},... | collective-permute-start | bytes 589832 | tf_op jit(solution)/shard_map/ppermute | solution.py:166
  53.9 6.3 %collective-permute-start.14 = (bf16[1536,768]{1,0:T(8,128)(2,1)}, bf16[1536,768]{1,0:T(8,128)(2,1)}, u32[]{:S(2)}, u32[]{:S(2)}) collective-permute-start(bf16[1536,768]{1,0:T(8,128)(2,1)} %constant_dynamic-slice_fusion.9), channel_id=1, source_target_pairs={{0,1},{1,0},{2,3},{3,2},{4,5},{5,4},{6,7},{7,6},{8,9},{9,8},{10,11... | collective-permute-start | bytes 7077896 | tf_op jit(solution)/shard_map/ppermute | solution.py:166
  63.3 27.4 %collective-permute-start.17 = (bf16[384,768]{1,0:T(8,128)(2,1)S(1)}, bf16[384,768]{1,0:T(8,128)(2,1)S(1)}, u32[]{:S(2)}, u32[]{:S(2)}) collective-permute-start(bf16[384,768]{1,0:T(8,128)(2,1)S(1)} %get-tuple-element.48), channel_id=1, source_target_pairs={{0,96},{32,0},{64,32},{96,64},{1,97},{33,1},{65,33},{97,65},{2,98}... | collective-permute-start | bytes 1769480 | tf_op jit(solution)/shard_map/ppermute | solution.py:170
  65.9 24.8 %collective-permute-start.16 = (bf16[384,768]{1,0:T(8,128)(2,1)S(1)}, bf16[384,768]{1,0:T(8,128)(2,1)S(1)}, u32[]{:S(2)}, u32[]{:S(2)}) collective-permute-start(bf16[384,768]{1,0:T(8,128)(2,1)S(1)} %get-tuple-element.49), channel_id=1, source_target_pairs={{0,64},{32,96},{64,0},{96,32},{1,65},{33,97},{65,1},{97,33},{2,66}... | collective-permute-start | bytes 1769480 | tf_op jit(solution)/shard_map/ppermute | solution.py:170
  66.4 28.9 %collective-permute-start.15 = (bf16[384,768]{1,0:T(8,128)(2,1)S(1)}, bf16[384,768]{1,0:T(8,128)(2,1)S(1)}, u32[]{:S(2)}, u32[]{:S(2)}) collective-permute-start(bf16[384,768]{1,0:T(8,128)(2,1)S(1)} %get-tuple-element.47), channel_id=1, source_target_pairs={{0,32},{32,64},{64,96},{96,0},{1,33},{33,65},{65,97},{97,1},{2,34}... | collective-permute-start | bytes 1769480 | tf_op jit(solution)/shard_map/ppermute | solution.py:170
  67.0 43.2 %collective-permute-start.7 = (bf16[32,3072]{1,0:T(8,128)(2,1)S(1)}, bf16[32,3072]{1,0:T(8,128)(2,1)S(1)}, u32[]{:S(2)}, u32[]{:S(2)}) collective-permute-start(bf16[32,3072]{1,0:T(8,128)(2,1)S(1)} %fusion.1), channel_id=1, source_target_pairs={{0,8},{1,9},{2,10},{3,11},{4,12},{5,13},{6,14},{7,15},{8,0},{9,1},... | collective-permute-start | bytes 589832 | tf_op jit(solution)/shard_map/ppermute | solution.py:166
  67.6 31.3 %collective-permute-start.8 = (bf16[16,3072]{1,0:T(8,128)(2,1)S(1)}, bf16[16,3072]{1,0:T(8,128)(2,1)S(1)}, u32[]{:S(2)}, u32[]{:S(2)}) collective-permute-start(bf16[16,3072]{1,0:T(8,128)(2,1)S(1)} %get-tuple-element.54), channel_id=1, source_target_pairs={{0,16},{1,17},{2,18},{3,19},{4,20},{5,21},{6,22},{7,23},{8,24},{9,... | collective-permute-start | bytes 294920 | tf_op jit(solution)/shard_map/ppermute | solution.py:166
  96.5 17.4 %collective-permute-start.20 = (bf16[96,768]{1,0:T(8,128)(2,1)}, bf16[96,768]{1,0:T(8,128)(2,1)}, u32[]{:S(2)}, u32[]{:S(2)}) collective-permute-start(bf16[96,768]{1,0:T(8,128)(2,1)} %get-tuple-element.51), channel_id=1, source_target_pairs={{0,24},{1,25},{2,26},{3,27},{4,28},{5,29},{6,30},{7,31},{8,0},{9,1... | collective-permute-start | bytes 442376 | tf_op jit(solution)/shard_map/ppermute | solution.py:174
  97.6 17.6 %collective-permute-start.19 = (bf16[96,768]{1,0:T(8,128)(2,1)}, bf16[96,768]{1,0:T(8,128)(2,1)}, u32[]{:S(2)}, u32[]{:S(2)}) collective-permute-start(bf16[96,768]{1,0:T(8,128)(2,1)} %get-tuple-element.52), channel_id=1, source_target_pairs={{0,16},{1,17},{2,18},{3,19},{4,20},{5,21},{6,22},{7,23},{8,24},{9,... | collective-permute-start | bytes 442376 | tf_op jit(solution)/shard_map/ppermute | solution.py:174
  98.7 16.4 %collective-permute-start.18 = (bf16[96,768]{1,0:T(8,128)(2,1)}, bf16[96,768]{1,0:T(8,128)(2,1)}, u32[]{:S(2)}, u32[]{:S(2)}) collective-permute-start(bf16[96,768]{1,0:T(8,128)(2,1)} %get-tuple-element.50), channel_id=1, source_target_pairs={{0,8},{1,9},{2,10},{3,11},{4,12},{5,13},{6,14},{7,15},{8,16},{9,17... | collective-permute-start | bytes 442376 | tf_op jit(solution)/shard_map/ppermute | solution.py:174
  98.9 11.3 %collective-permute-start.9 = (bf16[16,3072]{1,0:T(8,128)(2,1)S(1)}, bf16[16,3072]{1,0:T(8,128)(2,1)S(1)}, u32[]{:S(2)}, u32[]{:S(2)}) collective-permute-start(bf16[16,3072]{1,0:T(8,128)(2,1)S(1)} %get-tuple-element.53), channel_id=1, source_target_pairs={{0,24},{1,25},{2,26},{3,27},{4,28},{5,29},{6,30},{7,31},{8,16},{9,... | collective-permute-start | bytes 294920 | tf_op jit(solution)/shard_map/ppermute | solution.py:166
  111.3 9.4 %collective-permute-start.10 = (bf16[32,3072]{1,0:T(8,128)(2,1)}, bf16[32,3072]{1,0:T(8,128)(2,1)S(1)}, u32[]{:S(2)}, u32[]{:S(2)}) collective-permute-start(bf16[32,3072]{1,0:T(8,128)(2,1)} %get-tuple-element.39), channel_id=1, source_target_pairs={{0,2},{1,3},{2,0},{3,1},{4,6},{5,7},{6,4},{7,5},{8,10},{9,11},{10,... | collective-permute-start | bytes 589832 | tf_op jit(solution)/shard_map/ppermute | solution.py:166
  112.0 8.6 %collective-permute-start.11 = (bf16[16,3072]{1,0:T(8,128)(2,1)S(1)}, bf16[16,3072]{1,0:T(8,128)(2,1)S(1)}, u32[]{:S(2)}, u32[]{:S(2)}) collective-permute-start(bf16[16,3072]{1,0:T(8,128)(2,1)S(1)} %get-tuple-element.40), channel_id=1, source_target_pairs={{0,4},{1,5},{2,6},{3,7},{4,0},{5,1},{6,2},{7,3},{8,12},{9,13},{10,... | collective-permute-start | bytes 294920 | tf_op jit(solution)/shard_map/ppermute | solution.py:166
  113.9 6.8 %collective-permute-start.12 = (bf16[16,3072]{1,0:T(8,128)(2,1)}, bf16[16,3072]{1,0:T(8,128)(2,1)S(1)}, u32[]{:S(2)}, u32[]{:S(2)}) collective-permute-start(bf16[16,3072]{1,0:T(8,128)(2,1)} %get-tuple-element.41), channel_id=1, source_target_pairs={{0,6},{1,7},{2,4},{3,5},{4,2},{5,3},{6,0},{7,1},{8,14},{9,15},{10,... | collective-permute-start | bytes 294920 | tf_op jit(solution)/shard_map/ppermute | solution.py:166
  117.1 6.0 %collective-permute-start.23 = (bf16[24,768]{1,0:T(8,128)(2,1)}, bf16[24,768]{1,0:T(8,128)(2,1)}, u32[]{:S(2)}, u32[]{:S(2)}) collective-permute-start(bf16[24,768]{1,0:T(8,128)(2,1)} %get-tuple-element.56), channel_id=1, source_target_pairs={{0,6},{1,7},{2,0},{3,1},{4,2},{5,3},{6,4},{7,5},{8,14},{9,15},{10,... | collective-permute-start | bytes 110600 | tf_op jit(solution)/shard_map/ppermute | solution.py:178
  120.7 4.8 %collective-permute-start.21 = (bf16[24,768]{1,0:T(8,128)(2,1)}, bf16[24,768]{1,0:T(8,128)(2,1)}, u32[]{:S(2)}, u32[]{:S(2)}) collective-permute-start(bf16[24,768]{1,0:T(8,128)(2,1)} %get-tuple-element.55), channel_id=1, source_target_pairs={{0,2},{1,3},{2,4},{3,5},{4,6},{5,7},{6,0},{7,1},{8,10},{9,11},{10,... | collective-permute-start | bytes 110600 | tf_op jit(solution)/shard_map/ppermute | solution.py:178
  121.1 12.2 %collective-permute-start.13 = (bf16[32,3072]{1,0:T(8,128)(2,1)S(1)}, bf16[32,3072]{1,0:T(8,128)(2,1)S(1)}, u32[]{:S(2)}, u32[]{:S(2)}) collective-permute-start(bf16[32,3072]{1,0:T(8,128)(2,1)S(1)} %get-tuple-element.43), channel_id=1, source_target_pairs={{0,1},{1,0},{2,3},{3,2},{4,5},{5,4},{6,7},{7,6},{8,9},{9,8},{10,11... | collective-permute-start | bytes 589832 | tf_op jit(solution)/shard_map/ppermute | solution.py:166
  126.3 8.5 %collective-permute-start.24 = (f32[12,768]{1,0:T(8,128)S(1)}, f32[12,768]{1,0:T(8,128)S(1)}, u32[]{:S(2)}, u32[]{:S(2)}) collective-permute-start(f32[12,768]{1,0:T(8,128)S(1)} %slice_select_fusion), channel_id=1, source_target_pairs={{0,1},{1,0},{2,3},{3,2},{4,5},{5,4},{6,7},{7,6},{8,9},{9,8},{10,11... | collective-permute-start | bytes 110600 | tf_op jit(solution)/shard_map/ppermute | solution.py:166
  (17 other events, 129.7 us)

commit v2 on v1

v2 whole, which is shorter than its diff:
```python
import math

import jax
import jax.numpy as jnp
from jax import lax
from jax.experimental import pallas as pl
from jax.experimental.pallas import tpu as pltpu
from jax.sharding import PartitionSpec as P

H = 12
HD = 128
D = 1536
T = 256
HS = 2
W = HS * HD
STEPS = H // HS
BF = jnp.bfloat16
F = jnp.float32
NT = (((1,), (1,)), ((), ()))
TN = (((0,), (0,)), ((), ()))
NN = (((1,), (0,)), ((), ()))
LN2 = math.log(2.0)
SCALE = HD**-0.5
PART = D // 4
PAIR = 2 * D


def mm(a, b, dims):
    return lax.dot_general(a, b, dims, preferred_element_type=F)


def params(mib):
    return pltpu.CompilerParams(vmem_limit_bytes=mib * 2**20)


def cost(us):
    return pl.CostEstimate(flops=0, bytes_accessed=int(us * 3.7e6), transcendentals=0)


def shapes(*items):
    return [jax.ShapeDtypeStruct(s, t) for s, t in items]


def fold_matrix(n):
    r = lax.broadcasted_iota(jnp.int32, (n, 2 * n), 0)
    c = lax.broadcasted_iota(jnp.int32, (n, 2 * n), 1)
    return jnp.where((c >> 1) == r, 0.5, 0.0).astype(BF)


def fold(x):
    return mm(fold_matrix(x.shape[0] // 2), x, NN).astype(BF)


def spread(x, bits):
    n = x.shape[0]
    r = lax.broadcasted_iota(jnp.int32, (n << bits, n), 0)
    c = lax.broadcasted_iota(jnp.int32, (n << bits, n), 1)
    return mm(jnp.where((r >> bits) == c, 0.5**bits, 0.0).astype(BF), x.astype(BF), NN)


def pyramid_kernel(k, v, l12, l3, rows, sems):
    copies = []
    for step in range(STEPS):
        for i, x in enumerate((k, v)):
            n = 2 * step + i
            copies.append(
                pltpu.make_async_copy(x.at[:, pl.ds(step * W, W)], rows.at[:, pl.ds(n * W, W)], sems.at[n])
            )
            copies[-1].start()
    for part in range(3):
        c = slice(part * 4 * W, part * 4 * W + 4 * W)
        for copy in copies[4 * part : 4 * part + 4]:
            copy.wait()
        x1 = fold(rows[:, c])
        x2 = fold(x1)
        l12[:128, c] = x1
        l12[128:, c] = x2
        l3[:, c] = fold(x2)


def pyramid(k, v):
    far = pl.BlockSpec(memory_space=pl.ANY)
    near = pl.BlockSpec(memory_space=pltpu.VMEM)
    return pl.pallas_call(
        pyramid_kernel,
        in_specs=[far, far],
        out_specs=[near, near],
        out_shape=shapes(((192, PAIR), BF), ((32, PAIR), BF)),
        scratch_shapes=[pltpu.VMEM((T, PAIR), BF), pltpu.SemaphoreType.DMA((2 * STEPS,))],
        cost_estimate=cost(1.9),
        compiler_params=params(10),
        name="pyramid",
    )(k, v)


def chip_kernel(mine, other, l4, l5):
    x = fold(jnp.concatenate([mine[...], other[...]], 0))
    l4[...] = x
    l5[...] = fold(x)


def row_kernel(l5, z1, z2, z3, l6, l7):
    x = fold(jnp.concatenate([l5[...], fold(z1[...]), z2[...], z3[...]], 0))
    l6[...] = x
    l7[...] = fold(x)


def head(q, k0, v0, k12, v12, xk, xv, ga, bias, expand):
    s_all = mm(jnp.concatenate([k0, k12, xk], 0), q, NT)
    g_all = mm(jnp.concatenate([v0, v12, xv], 0), ga, NT)
    low = lax.broadcasted_iota(jnp.int32, (1, 128), 1) < 64
    low64 = jnp.broadcast_to(low, (64, 128))
    low32 = low64[:32]

    def pick(full, j):
        c = full[:, 128 * j : 128 * j + 128]
        a = jnp.where(low, c[128 * j : 128 * j + 64], c[128 * j + 64 : 128 * j + 128])
        b = jnp.where(low, c[288 + 64 * j : 320 + 64 * j], c[256 + 64 * j : 288 + 64 * j])
        d = c[416 - 32 * j : 448 - 32 * j]
        return jnp.concatenate([a, b, d, c[448:608]], 0)

    def widen(x):
        a, b = x[:64], x[64:96]
        za, zb = jnp.zeros_like(a), jnp.zeros_like(b)
        return jnp.concatenate(
            [
                jnp.where(low64, a, za),
                jnp.where(low64, za, a),
                jnp.where(low32, zb, b),
                jnp.where(low32, b, zb),
                x[96:],
            ],
            0,
        )

    att, gq, g0, g1, g2, px, sx = [], [], [], [], [None, None], [], []
    for j in range(2):
        s = pick(s_all, j) * SCALE + bias
        e = jnp.exp(s - jnp.max(s, axis=0, keepdims=True))
        p = e * (1.0 / jnp.sum(e, axis=0, keepdims=True))
        pb = p.astype(BF)
        gp = pick(g_all, j)
        delta = jnp.sum(pb.astype(F) * gp, axis=0, keepdims=True)
        gs = (p * (gp - delta) * SCALE).astype(BF)
        pw, sw = widen(pb), widen(gs)
        rows, o = slice(128 * j, 128 * j + 128), 1 - j
        near = slice(64 * j, 64 * j + 64)
        far = slice(128 + 32 * o, 160 + 32 * o)
        kh = jnp.concatenate([k0[rows], k12[near], k12[far], xk], 0)
        vh = jnp.concatenate([v0[rows], v12[near], v12[far], xv], 0)
        att.append(mm(pw, vh, TN))
        gq.append(mm(sw, kh, TN))
        both = jnp.concatenate([mm(sw[:224], q[rows], NN), mm(pw[:224], ga[rows], NN)], 1)
        g0.append(both[:128])
        g1.append(both[128:192])
        g2[o] = both[192:224]
        px.append(pw[224:])
        sx.append(sw[224:])
    gxk = mm(jnp.concatenate(sx, 1), q, NN)
    gxv = mm(jnp.concatenate(px, 1), ga, NN)
    coarse = jnp.concatenate(g1 + g2, 0).astype(BF)
    fine = jnp.concatenate(g0, 0) + mm(expand, coarse, NN)
    return jnp.concatenate(att, 0), jnp.concatenate(gq, 0), fine, gxk, gxv


def attention_kernel(base, q, k, v, l12, c1, z1, z2, z3, y1, y2, y3, ga, *rest):
    att_o, gq_o, fine_o, gc_o, gz_o, gy1_o, gy2_o, gy3_o, attt_o = rest[-9:]
    r = lax.broadcasted_iota(jnp.int32, (T, 192), 0)
    c = lax.broadcasted_iota(jnp.int32, (T, 192), 1)
    half = jnp.where((r >> 1) == c, 0.5, 0.0)
    expand = jnp.where(c < 128, half, jnp.where((r >> 2) == c - 128, 0.25, 0.0)).astype(BF)
    r = lax.broadcasted_iota(jnp.int32, (288, 1), 0)
    bias = jnp.where(r < 64, 0, (r >> 5) - 1).astype(F) * LN2
    x = jnp.concatenate([c1[...], z1[...], z2[...], z3[...], y1[...], y2[...], y3[...]], 0)
    for i in range(HS):
        c = slice(i * HD, i * HD + HD)
        cv = slice(W + i * HD, W + i * HD + HD)
        att, gq, fine, gxk, gxv = head(
            q[:, c], k[:, c], v[:, c], l12[:, c], l12[:, cv], x[:, c], x[:, cv], ga[:, c], bias, expand
        )
        att_o[:, c] = att.astype(BF)
        attt_o[c, :] = jnp.transpose(att).astype(BF)
        gq_o[:, c] = gq.astype(BF)
        for cols, g, f in ((c, gxk, fine[:, :HD]), (cv, gxv, fine[:, HD:])):
            fine_o[:, cols] = f
            gc_o[:, cols] = g[:32]
            gz_o[:, cols] = g[32:96]
            gy1_o[:, cols] = g[96:128].astype(BF)
            gy2_o[:, cols] = g[128:144].astype(BF)
            gy3_o[:, cols] = g[144:].astype(BF)


def attention(bits, flip, q, k, v, l12, pieces, ga, begun=()):
    def cols(rows, wide=W):
        return pl.BlockSpec((rows, wide), lambda h, s: (0, h + (s[XH] ^ flip) * (STEPS // 2)))

    outs = shapes(
        ((T, D), BF),
        ((T, D), BF),
        ((T, PAIR), F),
        ((32, PAIR), F),
        ((64, PAIR), F),
        ((32, PAIR), BF),
        ((16, PAIR), BF),
        ((16, PAIR), BF),
        ((D // 2, T), BF),
    )
    operands = (q, k, v, l12, *pieces, ga)
    return pl.pallas_call(
        attention_kernel,
        grid_spec=pltpu.PrefetchScalarGridSpec(
            num_scalar_prefetch=1,
            grid=(STEPS // 2,),
            in_specs=[cols(T)] * 3
            + [cols(192, 2 * W)]
            + [cols(p.shape[0], 2 * W) for p in pieces]
            + [cols(T)]
            + [pl.BlockSpec(memory_space=pl.ANY)] * len(begun),
            out_specs=[cols(T), cols(T)]
            + [cols(n, 2 * W) for n in (T, 32, 64, 32, 16, 16)]
            + [pl.BlockSpec((W, T), lambda h, s: (h, 0))],
        ),
        out_shape=outs,
        input_output_aliases={1 + len(operands) + i: i for i in range(len(begun))},
        cost_estimate=cost(7),
        compiler_params=params(24),
        name="attention",
    )(bits, *operands, *begun)


def back_row_kernel(gz, y1, y2, y3, s1, s2, s3, own):
    g6 = y1[...].astype(F) + spread(y2[...].astype(F) + y3[...].astype(F), 1)
    s1[...] = (gz[:32, :] + spread(g6[8:16], 2)).astype(BF)
    s2[...] = (gz[32:48, :] + spread(g6[16:24], 1)).astype(BF)
    s3[...] = (gz[48:, :] + spread(g6[24:], 1)).astype(BF)
    own[...] = spread(g6[:8], 2)


def back_chip_kernel(gc, own, z1, z2, z3, send, keep):
    g4 = own[...] + z1[...].astype(F) + spread(z2[...].astype(F) + z3[...].astype(F), 1)
    send[...] = (gc[...] + spread(g4[16:], 1)).astype(BF)
    keep[...] = spread(g4[:16], 1)


def finish_kernel(fine, keep, c1, gk, gv):
    g3 = keep[...] + c1[...].astype(F)
    for step in range(STEPS):
        for i, out in enumerate((gk, gv)):
            c = slice((2 * step + i) * W, (2 * step + i) * W + W)
            out[:, step * W : step * W + W] = (fine[:, c] + spread(g3[:, c], 3)).astype(BF)


def split_kernel(bits, go, go_m, go_o):
    mine = bits[CORE]
    half = D // 2
    go_m[...] = go[:, pl.ds(pl.multiple_of(mine * half, half), half)]
    go_o[...] = go[:, pl.ds(pl.multiple_of((1 - mine) * half, half), half)]


def split(bits, go):
    vmem = pl.BlockSpec(memory_space=pltpu.VMEM)
    return pl.pallas_call(
        split_kernel,
        in_specs=[pl.BlockSpec(memory_space=pltpu.SMEM), vmem],
        out_specs=[vmem] * 2,
        out_shape=shapes(*[((T, D // 2), BF)] * 2),
        cost_estimate=cost(0.3),
        compiler_params=params(10),
        name="split",
    )(bits, go)


def grad_attended_kernel(go, w, ga):
    for c in range(0, D, 256):
        ga[:, c : c + 256] = mm(go[...], w[c : c + 256, :], NT).astype(BF)


def mixed_kernel(att, w, out):
    for c in range(0, D, 256):
        out[:, c : c + 256] = mm(att[...], w[:, c : c + 256], NN).astype(BF)


def small(kernel, outs, name, us=0.4):
    return pl.pallas_call(kernel, out_shape=shapes(*outs), cost_estimate=cost(us),
        compiler_params=params(12), name=name)


def halves(which, outer, half):
    for o in range(outer):
        first = pl.multiple_of((2 * o + which) * half, 16 if half % 16 == 0 else 8)
        yield slice(o * half, o * half + half), pl.ds(first, half)


def weight_kernel(bits, *refs, color, bit, outer, half):
    send, keep = refs[-2:]
    n = (len(refs) - 2) // 2
    atts, gos = refs[:n], refs[n : 2 * n]
    away = 1 - bits[bit]
    c = slice(color * PART, color * PART + PART)
    for out, which in ((send, away), (keep, 1 - away)):
        for to, rows in halves(which, outer, half):
            out[to, :] = sum(mm(a[rows, :], g[:, c], NN) for a, g in zip(atts, gos, strict=True)).astype(BF)


def weight(bits, atts, gos, color, bit, outer, half):
    vmem = pl.BlockSpec(memory_space=pltpu.VMEM)
    return pl.pallas_call(
        lambda *refs: weight_kernel(*refs, color=color, bit=bit, outer=outer, half=half),
        in_specs=[pl.BlockSpec(memory_space=pltpu.SMEM)] + [vmem] * (2 * len(atts)),
        out_specs=[vmem, vmem],
        out_shape=shapes(((D // 4, PART), BF), ((D // 4, PART), BF)),
        cost_estimate=cost(1.5),
        compiler_params=params(10),
        name="weight_part",
    )(bits, *atts, *gos)


def merge_kernel(bits, *refs, bit, outer, half):
    away = 1 - bits[bit]
    n = (len(refs) - 2) // 2
    for out, which in ((refs[-2], away), (refs[-1], 1 - away)):
        for to, rows in halves(which, outer, half):
            for i in range(n):
                a, b = refs[2 * i], refs[2 * i + 1]
                w = a.shape[1]
                s = a[rows, :].astype(F) + b[rows, :].astype(F)
                out[to, i * w : i * w + w] = s.astype(out.dtype)


def merge(bits, pairs, bit, outer, half, dtype=BF):
    operands = [x for pair in pairs for x in pair]
    wide = sum(pair[0].shape[1] for pair in pairs)
    vmem = pl.BlockSpec(memory_space=pltpu.VMEM)
    return pl.pallas_call(
        lambda *refs: merge_kernel(*refs, bit=bit, outer=outer, half=half),
        in_specs=[pl.BlockSpec(memory_space=pltpu.SMEM)] + [vmem] * len(operands),
        out_specs=[vmem, vmem],
        out_shape=shapes(*[((outer * half, wide), dtype)] * 2),
        cost_estimate=cost(0.6),
        compiler_params=params(10),
        name="merge",
    )(bits, *operands)


def last_merge_kernel(bits, a_k, a_r, b_k, b_r, *outs):
    y, z = bits[YL], bits[ZL]
    total = jnp.concatenate(
        [a_k[...].astype(F) + a_r[...].astype(F), b_k[...].astype(F) + b_r[...].astype(F)], 1
    )
    quarters = [total[24 * i : 24 * i + 24] for i in range(4)]
    for out, dy, dz in zip(outs, (1, 0, 1, 0), (0, 1, 1, 0), strict=True):
        low = [jnp.where((z ^ dz) == 0, quarters[2 * i], quarters[2 * i + 1]) for i in range(2)]
        out[...] = jnp.where((y ^ dy) == 0, low[0], low[1])


def last_merge(bits, *operands):
    vmem = pl.BlockSpec(memory_space=pltpu.VMEM)
    return pl.pallas_call(
        last_merge_kernel,
        in_specs=[pl.BlockSpec(memory_space=pltpu.SMEM)] + [vmem] * 4,
        out_specs=[vmem] * 4,
        out_shape=shapes(*[((24, D // 2), F)] * 4),
        cost_estimate=cost(0.6),
        compiler_params=params(10),
        name="last_merge",
    )(bits, *operands)


def after(x, *others):
    return lax.optimization_barrier((x, *others))[0]


def across(x, flip):
    return lax.ppermute(x, "seq", [(i, i ^ flip) for i in range(32)])


def across_x(x, flip):
    return lax.ppermute(x, "dp", [(i, i ^ flip) for i in range(4)])


XH, XL, YH, YL, ZH, ZL, CORE = range(7)


def local(query, key, value, w_out, grad_out):
    q, k, v, go = query[0], key[0], value[0], grad_out[0]
    place = lax.axis_index("seq")
    row = lax.axis_index("dp")
    core = place & 1
    bits = jnp.stack(
        [row >> 1, row & 1, place >> 4 & 1, place >> 3 & 1, place >> 2 & 1, place >> 1 & 1, core]
    ).astype(jnp.int32)
    l12, l3 = pyramid(after(k, bits), v)
    c1 = across(l3, 1)
    l4, l5 = small(chip_kernel, [((32, PAIR), BF), ((16, PAIR), BF)], "chip")(l3, c1)
    z1, z3, z2 = across(l4, 2), across(l5, 6), across(l5, 4)
    go_m, go_s = split(bits, after(go, l3))
    go_o = across(go_s, 1)
    l5 = after(l5, go_o)
    ga = small(grad_attended_kernel, [((T, D), BF)], "grad_attended", 2.0)(after(go, z1), w_out)[0]
    l6, l7 = small(row_kernel, [((32, PAIR), BF), ((16, PAIR), BF)], "row")(l5, z1, z2, z3)
    gox_m, gox_o = across_x(go_m, 3), across_x(go_o, 3)
    y1, y3, y2 = across(l6, 8), across(l7, 24), across(l7, 16)
    pieces = (c1, z1, z2, z3, y1, y2, y3)
    *begun, sent = attention(bits, 1, after(q, gox_m), k, v, l12, pieces, ga)
    att_x = across_x(sent, 3)
    att, gq, fine, gc, gz, gy1, gy2, gy3, att_m = attention(
        bits, 0, after(q, gox_o), k, v, l12, pieces, ga, begun
    )
    att_o, att_xo = across(att_m, 1), across(att_x, 1)
    y1, y3, y2 = across(gy1, 8), across(gy3, 24), across(gy2, 16)
    atts = (att_m, att_o, att_x, att_xo)
    gos = (go_m, go_o, gox_m, gox_o)
    b_s, b_k = weight(bits, atts, gos, 1, ZH, 8, 48)
    b_r = across(b_s, 6)
    a_s, a_k = weight(bits, (after(att_m, b_k), *atts[1:]), gos, 0, XL, 1, 384)
    a_r = across_x(a_s, 1)
    s1, s2, s3, own = small(
        back_row_kernel, [((32, PAIR), BF), ((16, PAIR), BF), ((16, PAIR), BF), ((32, PAIR), F)], "back_row"
    )(after(gz, a_k), y1, y2, y3)
    z1, z3, z2 = across(s1, 2), across(s3, 6), across(s2, 4)
    b_s, b_k = merge(bits, [(after(b_k, own), b_r)], YH, 2, 96)
    b_r = across(b_s, 24)
    a_s, a_k = merge(bits, [(after(a_k, b_k), a_r)], ZH, 4, 48)
    a_r = across(a_s, 6)
    mixed = small(mixed_kernel, [((T, D), BF)], "mixed", 2.3)(after(att, a_k), w_out)[0]
    send, keep = small(back_chip_kernel, [((32, PAIR), BF), ((32, PAIR), F)], "back_chip")(
        after(gc, mixed), own, z1, z2, z3
    )
    c1 = across(send, 1)
    b_s, b_k = merge(bits, [(after(b_k, keep), b_r)], XL, 1, 96)
    b_r = across_x(b_s, 1)
    a_s, a_k = merge(bits, [(after(a_k, b_k), a_r)], YH, 1, 96)
    a_r = across(a_s, 24)
    gk, gv = small(finish_kernel, [((T, D), BF), ((T, D), BF)], "finish", 1.7)(after(fine, a_k), keep, c1)
    s1, s2, s3, kept = last_merge(bits, after(a_k, gk), a_r, b_k, b_r)
    part = kept + across(s1, 8) + across(s2, 2) + across(s3, 10)
    first = core == 0
    mine = jnp.where(first, part[:12], part[12:])
    theirs = across(jnp.where(first, part[12:], part[:12]), 1)
    total = jnp.concatenate([jnp.where(first, mine, theirs), jnp.where(first, theirs, mine)], 1)
    gw = total * (1.0 / math.sqrt(4 * 32 * T))
    return mixed[None], gq[None], gk[None], gv[None], gw


def solution(mesh):
    rows = P("dp", "seq", None)
    return jax.shard_map(
        local,
        mesh=mesh,
        in_specs=(rows, rows, rows, P(), rows),
        out_specs=(rows, rows, rows, rows, P(("dp", "seq"), None)),
        check_vma=False,
    )
```

time: 136 us -> 98.7 us (0.73)
  waiting for transfers between devices: 56.7 us -> 15 us
  starting transfers between devices: 32.2 us -> 45.2 us
  Pallas kernels: 19.2 us -> 30.7 us
  matrix products: 9.63 us -> 0 us
  other arithmetic: 6.02 us -> 0.7 us
  local copies, waits for them, and re-layouts: 10.9 us -> 5.97 us
    ppermute x9 -> x5, waiting for transfers between devices: 28.1 us -> 0.01 us  [across_x(): return lax.ppermute(x, 'dp', [(i, i ^ flip) for i in range(4)])]
    ppermute x16 -> x25, waiting for transfers between devices: 28.6 us -> 14.9 us  [across(): return lax.ppermute(x, 'seq', [(i, i ^ flip) for i in range(32)])]
    ppermute x16 -> x25, starting transfers between devices: 24.7 us -> 37.6 us  [across(): return lax.ppermute(x, 'seq', [(i, i ^ flip) for i in range(32)])]
    pallas_call x7 -> x18, Pallas kernels: 19.2 us -> 30.7 us  [the longest x2 14.4 us: attention(): pl.pallas_call(attention_kernel, grid_spec=pltpu.PrefetchScalarGridSpec(n...]
    dot_general x2 -> x0, matrix products: 9.63 us -> none  [mm(): return lax.dot_general(a, b, dims, preferred_element_type=F)]
    dynamic_slice x4 -> x0, local copies, waits for them, and re-layouts: 5.26 us -> none  [the longest x1 3.61 us: local(): theirs = lax.dynamic_slice_in_dim(gw, (1 - core) * half, half, 1)]
    convert_element_type x3 -> x0, other arithmetic: 4.47 us -> none  [the longest x1 2.96 us: local(): part = (mine.astype(F) + across(theirs, 1).astype(F)).astype(BF)]
    unnamed x38 -> x20, local copies, waits for them, and re-layouts: 5.58 us -> 5.88 us
  transfers between devices with their start and end apart: 25 -> 30, of which waited for: 10 -> 10; matrix products, arithmetic and copies ran while one was open for 10% -> 0% of each run, Pallas kernels for 2% -> 28%
where the time goes in v2:
time: 98.7 us; the launch traced here: 98.4 us
  starting transfers between devices  45.2 us (46%)
  Pallas kernels  30.7 us (31%)
  waiting for transfers between devices  15 us (15%)
  local copies, waits for them, and re-layouts  5.97 us (6%)
    ppermute x25, starting transfers between devices, across(): return lax.ppermute(x, 'seq', [(i, i ^ flip) for i in range(32)])  37.6 us
    ppermute x25, waiting for transfers between devices, across(): return lax.ppermute(x, 'seq', [(i, i ^ flip) for i in range(32)])  14.9 us
    pallas_call x2, Pallas kernels, attention(): pl.pallas_call(attention_kernel, grid_spec=pltpu.PrefetchScalarGridSpec(n...  14.4 us
    ppermute x5, starting transfers between devices, across_x(): return lax.ppermute(x, 'dp', [(i, i ^ flip) for i in range(4)])  7.59 us
    unnamed x20, local copies, waits for them, and re-layouts  5.88 us
    pallas_call x2, Pallas kernels, weight(): pl.pallas_call(lambda *refs: weight_kernel(*refs, color=color, bit=bit, o...  3.9 us
    pallas_call x4, Pallas kernels, merge(): pl.pallas_call(lambda *refs: merge_kernel(*refs, bit=bit, outer=outer, ha...  2.42 us
    pallas_call x1, Pallas kernels, local(): small(mixed_kernel, [((T, D), BF)], 'mixed', 2.3)(after(att, a_k), w_out)[0]  2.26 us
  transfers between devices with their start and end apart: 30, of which 10 were waited for; matrix products, arithmetic and copies ran while one was open for 0% of the time, Pallas kernels for 28%

profile of v2, /device:TPU:1, one launch (start us, length us, event | category | flops | bytes accessed | tf_op | source)
XLA Modules:
  0.0 98.4 jit_solution(1894156562833829352)
XLA Ops:
  3.0 1.8 %pyramid.1 = (bf16[192,3072]{1,0:T(8,128)(2,1)S(1)}, bf16[32,3072]{1,0:T(8,128)(2,1)S(1)}) custom-call(bf16[256,1536]{1,0:T(8,128)(2,1)S(1)} %bitcast.17, bf16[256,1536]{1,0:T(8,128)(2,1)S(1)} %bitcast.20), custom_call_target="tpu_custom_call" | custom-call | bytes 7030000 | tf_op jit(solution)/shard_map/pyramid/pallas_call | solution.py:84
  8.2 2.6 %collective-permute-start.9 = (bf16[256,768]{1,0:T(8,128)(2,1)S(1)}, bf16[256,768]{1,0:T(8,128)(2,1)S(1)}, u32[]{:S(2)}, u32[]{:S(2)}) collective-permute-start(bf16[256,768]{1,0:T(8,128)(2,1)S(1)} %get-tuple-element.83.refs_5_), channel_id=1, source_target_pairs={{0,96},{32,64},{64,32},{96,0},{1,97},{33,65},{65,33},{97,1},{2,98}... | collective-permute-start | bytes 1179656 | tf_op jit(solution)/shard_map/ppermute | solution.py:378
  11.1 1.7 %collective-permute-start.3 = (bf16[32,3072]{1,0:T(8,128)(2,1)S(1)}, bf16[32,3072]{1,0:T(8,128)(2,1)S(1)}, u32[]{:S(2)}, u32[]{:S(2)}) collective-permute-start(bf16[32,3072]{1,0:T(8,128)(2,1)S(1)} %get-tuple-element.77), channel_id=1, source_target_pairs={{0,2},{1,3},{2,0},{3,1},{4,6},{5,7},{6,4},{7,5},{8,10},{9,11},{10,... | collective-permute-start | bytes 589832 | tf_op jit(solution)/shard_map/ppermute | solution.py:374
  12.8 2.2 %collective-permute-start.5 = (bf16[16,3072]{1,0:T(8,128)(2,1)S(1)}, bf16[16,3072]{1,0:T(8,128)(2,1)S(1)}, u32[]{:S(2)}, u32[]{:S(2)}) collective-permute-start(bf16[16,3072]{1,0:T(8,128)(2,1)S(1)} %get-tuple-element.79.l5), channel_id=1, source_target_pairs={{0,6},{1,7},{2,4},{3,5},{4,2},{5,3},{6,0},{7,1},{8,14},{9,15},{10,... | collective-permute-start | bytes 294920 | tf_op jit(solution)/shard_map/ppermute | solution.py:374
  16.1 1.7 %collective-permute-done.5.z3 = bf16[16,3072]{1,0:T(8,128)(2,1)S(1)} collective-permute-done((bf16[16,3072]{1,0:T(8,128)(2,1)S(1)}, bf16[16,3072]{1,0:T(8,128)(2,1)S(1)}, u32[]{:S(2)}, u32[]{:S(2)}) %collective-permute-start.5) | collective-permute-done | bytes 98336 | tf_op jit(solution)/shard_map/ppermute | solution.py:374
  17.7 4.4 %collective-permute-done.4.z2 = bf16[16,3072]{1,0:T(8,128)(2,1)S(1)} collective-permute-done((bf16[16,3072]{1,0:T(8,128)(2,1)S(1)}, bf16[16,3072]{1,0:T(8,128)(2,1)S(1)}, u32[]{:S(2)}, u32[]{:S(2)}) %collective-permute-start.4) | collective-permute-done | bytes 98336 | tf_op jit(solution)/shard_map/ppermute | solution.py:374
  24.0 1.9 %collective-permute-start.8 = (bf16[16,3072]{1,0:T(8,128)(2,1)S(1)}, bf16[16,3072]{1,0:T(8,128)(2,1)S(1)}, u32[]{:S(2)}, u32[]{:S(2)}) collective-permute-start(bf16[16,3072]{1,0:T(8,128)(2,1)S(1)} %get-tuple-element.81), channel_id=1, source_target_pairs={{0,24},{1,25},{2,26},{3,27},{4,28},{5,29},{6,30},{7,31},{8,16},{9,... | collective-permute-start | bytes 294920 | tf_op jit(solution)/shard_map/ppermute | solution.py:374
  26.6 2.2 %collective-permute-start.1 = (bf16[256,768]{1,0:T(8,128)(2,1)S(1)}, bf16[256,768]{1,0:T(8,128)(2,1)S(1)}, u32[]{:S(2)}, u32[]{:S(2)}) collective-permute-start(bf16[256,768]{1,0:T(8,128)(2,1)S(1)} %collective-permute-done.refs_6_), channel_id=1, source_target_pairs={{0,96},{32,64},{64,32},{96,0},{1,97},{33,65},{65,33},{97,1},{2,98}... | collective-permute-start | bytes 1179656 | tf_op jit(solution)/shard_map/ppermute | solution.py:378
  28.8 2.3 %copy-done = bf16[1536,1536]{1,0:T(8,128)(2,1)S(1)} copy-done((bf16[1536,1536]{1,0:T(8,128)(2,1)S(1)}, bf16[1536,1536]{1,0:T(8,128)(2,1)}, u32[]{:S(2)}) %copy-start) | copy-done | bytes 4718616
  32.7 7.2 %attention.2 = (bf16[256,1536]{1,0:T(8,128)(2,1)S(1)}, bf16[256,1536]{1,0:T(8,128)(2,1)}, f32[256,3072]{1,0:T(8,128)S(1)}, f32[32,3072]{1,0:T(8,128)S(1)}, f32[6...) custom-call(s32[7]{0:T(128)S(1)} %stack.31.bits.base.refs_0_, ...), custom_call_target="tpu_custom_call" | custom-call | bytes 25900000 | tf_op jit(solution)/shard_map/attention/pallas_call | solution.py:209
  41.6 7.2 %attention.3 = (bf16[256,1536]{1,0:T(8,128)(2,1)S(1)}, bf16[256,1536]{1,0:T(8,128)(2,1)}, f32[256,3072]{1,0:T(8,128)S(1)}, f32[32,3072]{1,0:T(8,128)S(1)}, f32[6...) custom-call(s32[7]{0:T(128)S(1)} %stack.31.bits.base.refs_0_, ...), custom_call_target="tpu_custom_call", output_to_operand_aliasing={{0}: (13, {}), {1}: (14, {}), {2}: (15, {}), {3}: (16, {}),... | custom-call | bytes 25900000 | tf_op jit(solution)/shard_map/attention/pallas_call | solution.py:209
  48.8 2.7 %collective-permute-start.10 = (bf16[768,256]{1,0:T(8,128)(2,1)S(1)}, bf16[768,256]{1,0:T(8,128)(2,1)S(1)}, u32[]{:S(2)}, u32[]{:S(2)}) collective-permute-start(bf16[768,256]{1,0:T(8,128)(2,1)S(1)} %get-tuple-element.97.refs_1_), channel_id=1, source_target_pairs={{0,1},{1,0},{2,3},{3,2},{4,5},{5,4},{6,7},{7,6},{8,9},{9,8},{10,11... | collective-permute-start | bytes 1179656 | tf_op jit(solution)/shard_map/ppermute | solution.py:374
  54.1 2.4 %weight_part.2 = (bf16[384,384]{1,0:T(8,128)(2,1)S(1)}, bf16[384,384]{1,0:T(8,128)(2,1)S(1)}) custom-call(s32[7]{0:T(128)S(1)} %stack.31.bits.base.refs_0_, bf16[768,256]{1,0:T(8,128)(2,1)S(1)} %get-tuple-element.97.refs_1_, bf16[768,256]{1,0:T(8,128)(2,1)S(1)} %collective-permute-done.10.refs_2_, bf16[768,256]{1,0:T(8,128)(2,1)S(1)} %collective-permute-done.11.refs_3_, ...), custom_call_target="tpu_custom_call" | custom-call | bytes 5550000 | tf_op jit(solution)/shard_map/weight_part/pallas_call | solution.py:307
  58.3 2.3 %collective-permute-start.14 = (bf16[16,3072]{1,0:T(8,128)(2,1)S(1)}, bf16[16,3072]{1,0:T(8,128)(2,1)S(1)}, u32[]{:S(2)}, u32[]{:S(2)}) collective-permute-start(bf16[16,3072]{1,0:T(8,128)(2,1)S(1)} %get-tuple-element.102), channel_id=1, source_target_pairs={{0,16},{1,17},{2,18},{3,19},{4,20},{5,21},{6,22},{7,23},{8,24},{9,... | collective-permute-start | bytes 294920 | tf_op jit(solution)/shard_map/ppermute | solution.py:374
  61.5 2.5 %collective-permute-done.14.y2 = bf16[16,3072]{1,0:T(8,128)(2,1)S(1)} collective-permute-done((bf16[16,3072]{1,0:T(8,128)(2,1)S(1)}, bf16[16,3072]{1,0:T(8,128)(2,1)S(1)}, u32[]{:S(2)}, u32[]{:S(2)}) %collective-permute-start.14) | collective-permute-done | bytes 98336 | tf_op jit(solution)/shard_map/ppermute | solution.py:374
  63.9 1.9 %collective-permute-done.15.y3 = bf16[16,3072]{1,0:T(8,128)(2,1)S(1)} collective-permute-done((bf16[16,3072]{1,0:T(8,128)(2,1)S(1)}, bf16[16,3072]{1,0:T(8,128)(2,1)S(1)}, u32[]{:S(2)}, u32[]{:S(2)}) %collective-permute-start.15) | collective-permute-done | bytes 98336 | tf_op jit(solution)/shard_map/ppermute | solution.py:374
  66.4 3.5 %collective-permute-start.19 = (bf16[16,3072]{1,0:T(8,128)(2,1)S(1)}, bf16[16,3072]{1,0:T(8,128)(2,1)S(1)}, u32[]{:S(2)}, u32[]{:S(2)}) collective-permute-start(bf16[16,3072]{1,0:T(8,128)(2,1)S(1)} %get-tuple-element.117), channel_id=1, source_target_pairs={{0,4},{1,5},{2,6},{3,7},{4,0},{5,1},{6,2},{7,3},{8,12},{9,13},{10,... | collective-permute-start | bytes 294920 | tf_op jit(solution)/shard_map/ppermute | solution.py:374
  70.9 3.0 %collective-permute-start.21 = (bf16[192,384]{1,0:T(8,128)(2,1)S(1)}, bf16[192,384]{1,0:T(8,128)(2,1)S(1)}, u32[]{:S(2)}, u32[]{:S(2)}) collective-permute-start(bf16[192,384]{1,0:T(8,128)(2,1)S(1)} %get-tuple-element.121), channel_id=1, source_target_pairs={{0,24},{1,25},{2,26},{3,27},{4,28},{5,29},{6,30},{7,31},{8,16},{9,... | collective-permute-start | bytes 442376 | tf_op jit(solution)/shard_map/ppermute | solution.py:374
  74.6 2.7 %collective-permute-start.22 = (bf16[192,384]{1,0:T(8,128)(2,1)S(1)}, bf16[192,384]{1,0:T(8,128)(2,1)S(1)}, u32[]{:S(2)}, u32[]{:S(2)}) collective-permute-start(bf16[192,384]{1,0:T(8,128)(2,1)S(1)} %get-tuple-element.124), channel_id=1, source_target_pairs={{0,6},{1,7},{2,4},{3,5},{4,2},{5,3},{6,0},{7,1},{8,14},{9,15},{10,... | collective-permute-start | bytes 442376 | tf_op jit(solution)/shard_map/ppermute | solution.py:374
  77.3 2.3 %mixed.1 = bf16[256,1536]{1,0:T(8,128)(2,1)} custom-call(bf16[256,1536]{1,0:T(8,128)(2,1)S(1)} %get-tuple-element.111.att, bf16[1536,1536]{1,0:T(8,128)(2,1)S(1)} %bitcast.16), custom_call_target="tpu_custom_call" | custom-call | bytes 8510000 | tf_op jit(solution)/shard_map/mixed/pallas_call | solution.py:425
  79.9 2.0 %collective-permute-start.23 = (bf16[32,3072]{1,0:T(8,128)(2,1)S(1)}, bf16[32,3072]{1,0:T(8,128)(2,1)S(1)}, u32[]{:S(2)}, u32[]{:S(2)}) collective-permute-start(bf16[32,3072]{1,0:T(8,128)(2,1)S(1)} %get-tuple-element.127), channel_id=1, source_target_pairs={{0,1},{1,0},{2,3},{3,2},{4,5},{5,4},{6,7},{7,6},{8,9},{9,8},{10,11... | collective-permute-start | bytes 589832 | tf_op jit(solution)/shard_map/ppermute | solution.py:374
  85.7 1.7 %finish.1 = (bf16[256,1536]{1,0:T(8,128)(2,1)}, bf16[256,1536]{1,0:T(8,128)(2,1)}) custom-call(f32[256,3072]{1,0:T(8,128)S(1)} %get-tuple-element.126.fine, f32[32,3072]{1,0:T(8,128)S(1)} %get-tuple-element.119.keep, bf16[32,3072]{1,0:T(8,128)(2,1)S(1)} %collective-permute-done.23.c1), custom_call_target="tpu_custom_call" | custom-call | bytes 6290000 | tf_op jit(solution)/shard_map/finish/pallas_call | solution.py:434
  89.1 2.5 %collective-permute-start.28 = (f32[24,768]{1,0:T(8,128)S(1)}, f32[24,768]{1,0:T(8,128)S(1)}, u32[]{:S(2)}, u32[]{:S(2)}) collective-permute-start(f32[24,768]{1,0:T(8,128)S(1)} %get-tuple-element.136), channel_id=1, source_target_pairs={{0,10},{1,11},{2,8},{3,9},{4,14},{5,15},{6,12},{7,13},{8,2},{9,3},... | collective-permute-start | bytes 221192 | tf_op jit(solution)/shard_map/ppermute | solution.py:374
  93.5 3.3 %collective-permute-start.29 = (f32[12,768]{1,0:T(8,128)S(1)}, f32[12,768]{1,0:T(8,128)S(1)}, u32[]{:S(2)}, u32[]{:S(2)}) collective-permute-start(f32[12,768]{1,0:T(8,128)S(1)} %slice_select_fusion), channel_id=1, source_target_pairs={{0,1},{1,0},{2,3},{3,2},{4,5},{5,4},{6,7},{7,6},{8,9},{9,8},{10,11... | collective-permute-start | bytes 110600 | tf_op jit(solution)/shard_map/ppermute | solution.py:374
  (80 shorter events, 29.3 us)
Async XLA Ops:
  6.6 9.5 %collective-permute-start = (bf16[256,768]{1,0:T(8,128)(2,1)S(1)}, bf16[256,768]{1,0:T(8,128)(2,1)S(1)}, u32[]{:S(2)}, u32[]{:S(2)}) collective-permute-start(bf16[256,768]{1,0:T(8,128)(2,1)S(1)} %get-tuple-element.74), channel_id=1, source_target_pairs={{0,1},{1,0},{2,3},{3,2},{4,5},{5,4},{6,7},{7,6},{8,9},{9,8},{10,11... | collective-permute-start | bytes 1179656 | tf_op jit(solution)/shard_map/ppermute | solution.py:374
  8.2 20.6 %collective-permute-start.9 = (bf16[256,768]{1,0:T(8,128)(2,1)S(1)}, bf16[256,768]{1,0:T(8,128)(2,1)S(1)}, u32[]{:S(2)}, u32[]{:S(2)}) collective-permute-start(bf16[256,768]{1,0:T(8,128)(2,1)S(1)} %get-tuple-element.83.refs_5_), channel_id=1, source_target_pairs={{0,96},{32,64},{64,32},{96,0},{1,97},{33,65},{65,33},{97,1},{2,98}... | collective-permute-start | bytes 1179656 | tf_op jit(solution)/shard_map/ppermute | solution.py:378
  11.1 11.1 %collective-permute-start.3 = (bf16[32,3072]{1,0:T(8,128)(2,1)S(1)}, bf16[32,3072]{1,0:T(8,128)(2,1)S(1)}, u32[]{:S(2)}, u32[]{:S(2)}) collective-permute-start(bf16[32,3072]{1,0:T(8,128)(2,1)S(1)} %get-tuple-element.77), channel_id=1, source_target_pairs={{0,2},{1,3},{2,0},{3,1},{4,6},{5,7},{6,4},{7,5},{8,10},{9,11},{10,... | collective-permute-start | bytes 589832 | tf_op jit(solution)/shard_map/ppermute | solution.py:374
  12.8 5.0 %collective-permute-start.5 = (bf16[16,3072]{1,0:T(8,128)(2,1)S(1)}, bf16[16,3072]{1,0:T(8,128)(2,1)S(1)}, u32[]{:S(2)}, u32[]{:S(2)}) collective-permute-start(bf16[16,3072]{1,0:T(8,128)(2,1)S(1)} %get-tuple-element.79.l5), channel_id=1, source_target_pairs={{0,6},{1,7},{2,4},{3,5},{4,2},{5,3},{6,0},{7,1},{8,14},{9,15},{10,... | collective-permute-start | bytes 294920 | tf_op jit(solution)/shard_map/ppermute | solution.py:374
  15.0 7.1 %collective-permute-start.4 = (bf16[16,3072]{1,0:T(8,128)(2,1)S(1)}, bf16[16,3072]{1,0:T(8,128)(2,1)S(1)}, u32[]{:S(2)}, u32[]{:S(2)}) collective-permute-start(bf16[16,3072]{1,0:T(8,128)(2,1)S(1)} %get-tuple-element.79.l5), channel_id=1, source_target_pairs={{0,4},{1,5},{2,6},{3,7},{4,0},{5,1},{6,2},{7,3},{8,12},{9,13},{10,... | collective-permute-start | bytes 294920 | tf_op jit(solution)/shard_map/ppermute | solution.py:374
  22.6 10.0 %collective-permute-start.6 = (bf16[32,3072]{1,0:T(8,128)(2,1)S(1)}, bf16[32,3072]{1,0:T(8,128)(2,1)S(1)}, u32[]{:S(2)}, u32[]{:S(2)}) collective-permute-start(bf16[32,3072]{1,0:T(8,128)(2,1)S(1)} %get-tuple-element.80), channel_id=1, source_target_pairs={{0,8},{1,9},{2,10},{3,11},{4,12},{5,13},{6,14},{7,15},{8,0},{9,1},... | collective-permute-start | bytes 589832 | tf_op jit(solution)/shard_map/ppermute | solution.py:374
  24.0 8.6 %collective-permute-start.8 = (bf16[16,3072]{1,0:T(8,128)(2,1)S(1)}, bf16[16,3072]{1,0:T(8,128)(2,1)S(1)}, u32[]{:S(2)}, u32[]{:S(2)}) collective-permute-start(bf16[16,3072]{1,0:T(8,128)(2,1)S(1)} %get-tuple-element.81), channel_id=1, source_target_pairs={{0,24},{1,25},{2,26},{3,27},{4,28},{5,29},{6,30},{7,31},{8,16},{9,... | collective-permute-start | bytes 294920 | tf_op jit(solution)/shard_map/ppermute | solution.py:374
  25.9 6.7 %collective-permute-start.7 = (bf16[16,3072]{1,0:T(8,128)(2,1)S(1)}, bf16[16,3072]{1,0:T(8,128)(2,1)S(1)}, u32[]{:S(2)}, u32[]{:S(2)}) collective-permute-start(bf16[16,3072]{1,0:T(8,128)(2,1)S(1)} %get-tuple-element.81), channel_id=1, source_target_pairs={{0,16},{1,17},{2,18},{3,19},{4,20},{5,21},{6,22},{7,23},{8,24},{9,... | collective-permute-start | bytes 294920 | tf_op jit(solution)/shard_map/ppermute | solution.py:374
  26.6 15.0 %collective-permute-start.1 = (bf16[256,768]{1,0:T(8,128)(2,1)S(1)}, bf16[256,768]{1,0:T(8,128)(2,1)S(1)}, u32[]{:S(2)}, u32[]{:S(2)}) collective-permute-start(bf16[256,768]{1,0:T(8,128)(2,1)S(1)} %collective-permute-done.refs_6_), channel_id=1, source_target_pairs={{0,96},{32,64},{64,32},{96,0},{1,97},{33,65},{65,33},{97,1},{2,98}... | collective-permute-start | bytes 1179656 | tf_op jit(solution)/shard_map/ppermute | solution.py:378
  40.0 11.5 %collective-permute-start.11 = (bf16[768,256]{1,0:T(8,128)(2,1)S(1)}, bf16[768,256]{1,0:T(8,128)(2,1)S(1)}, u32[]{:S(2)}, u32[]{:S(2)}) collective-permute-start(bf16[768,256]{1,0:T(8,128)(2,1)S(1)} %get-tuple-element.95), channel_id=1, source_target_pairs={{0,96},{32,64},{64,32},{96,0},{1,97},{33,65},{65,33},{97,1},{2,98}... | collective-permute-start | bytes 1179656 | tf_op jit(solution)/shard_map/ppermute | solution.py:378
  48.8 4.5 %collective-permute-start.10 = (bf16[768,256]{1,0:T(8,128)(2,1)S(1)}, bf16[768,256]{1,0:T(8,128)(2,1)S(1)}, u32[]{:S(2)}, u32[]{:S(2)}) collective-permute-start(bf16[768,256]{1,0:T(8,128)(2,1)S(1)} %get-tuple-element.97.refs_1_), channel_id=1, source_target_pairs={{0,1},{1,0},{2,3},{3,2},{4,5},{5,4},{6,7},{7,6},{8,9},{9,8},{10,11... | collective-permute-start | bytes 1179656 | tf_op jit(solution)/shard_map/ppermute | solution.py:374
  52.7 13.2 %collective-permute-start.13 = (bf16[32,3072]{1,0:T(8,128)(2,1)S(1)}, bf16[32,3072]{1,0:T(8,128)(2,1)S(1)}, u32[]{:S(2)}, u32[]{:S(2)}) collective-permute-start(bf16[32,3072]{1,0:T(8,128)(2,1)S(1)} %get-tuple-element.101), channel_id=1, source_target_pairs={{0,8},{1,9},{2,10},{3,11},{4,12},{5,13},{6,14},{7,15},{8,0},{9,1},... | collective-permute-start | bytes 589832 | tf_op jit(solution)/shard_map/ppermute | solution.py:374
  56.5 13.8 %collective-permute-start.16 = (bf16[384,384]{1,0:T(8,128)(2,1)S(1)}, bf16[384,384]{1,0:T(8,128)(2,1)S(1)}, u32[]{:S(2)}, u32[]{:S(2)}) collective-permute-start(bf16[384,384]{1,0:T(8,128)(2,1)S(1)} %get-tuple-element.106), channel_id=1, source_target_pairs={{0,6},{1,7},{2,4},{3,5},{4,2},{5,3},{6,0},{7,1},{8,14},{9,15},{10,... | collective-permute-start | bytes 884744 | tf_op jit(solution)/shard_map/ppermute | solution.py:374
  58.3 15.7 %collective-permute-start.17 = (bf16[384,384]{1,0:T(8,128)(2,1)S(1)}, bf16[384,384]{1,0:T(8,128)(2,1)S(1)}, u32[]{:S(2)}, u32[]{:S(2)}) collective-permute-start(bf16[384,384]{1,0:T(8,128)(2,1)S(1)} %get-tuple-element.109), channel_id=1, source_target_pairs={{0,32},{32,0},{64,96},{96,64},{1,33},{33,1},{65,97},{97,65},{2,34}... | collective-permute-start | bytes 884744 | tf_op jit(solution)/shard_map/ppermute | solution.py:378
  58.3 5.6 %collective-permute-start.14 = (bf16[16,3072]{1,0:T(8,128)(2,1)S(1)}, bf16[16,3072]{1,0:T(8,128)(2,1)S(1)}, u32[]{:S(2)}, u32[]{:S(2)}) collective-permute-start(bf16[16,3072]{1,0:T(8,128)(2,1)S(1)} %get-tuple-element.102), channel_id=1, source_target_pairs={{0,16},{1,17},{2,18},{3,19},{4,20},{5,21},{6,22},{7,23},{8,24},{9,... | collective-permute-start | bytes 294920 | tf_op jit(solution)/shard_map/ppermute | solution.py:374
  60.7 5.2 %collective-permute-start.15 = (bf16[16,3072]{1,0:T(8,128)(2,1)S(1)}, bf16[16,3072]{1,0:T(8,128)(2,1)S(1)}, u32[]{:S(2)}, u32[]{:S(2)}) collective-permute-start(bf16[16,3072]{1,0:T(8,128)(2,1)S(1)} %get-tuple-element.103), channel_id=1, source_target_pairs={{0,24},{1,25},{2,26},{3,27},{4,28},{5,29},{6,30},{7,31},{8,16},{9,... | collective-permute-start | bytes 294920 | tf_op jit(solution)/shard_map/ppermute | solution.py:374
  66.3 13.2 %collective-permute-start.18 = (bf16[32,3072]{1,0:T(8,128)(2,1)S(1)}, bf16[32,3072]{1,0:T(8,128)(2,1)S(1)}, u32[]{:S(2)}, u32[]{:S(2)}) collective-permute-start(bf16[32,3072]{1,0:T(8,128)(2,1)S(1)} %get-tuple-element.116), channel_id=1, source_target_pairs={{0,2},{1,3},{2,0},{3,1},{4,6},{5,7},{6,4},{7,5},{8,10},{9,11},{10,... | collective-permute-start | bytes 589832 | tf_op jit(solution)/shard_map/ppermute | solution.py:374
  66.4 13.1 %collective-permute-start.19 = (bf16[16,3072]{1,0:T(8,128)(2,1)S(1)}, bf16[16,3072]{1,0:T(8,128)(2,1)S(1)}, u32[]{:S(2)}, u32[]{:S(2)}) collective-permute-start(bf16[16,3072]{1,0:T(8,128)(2,1)S(1)} %get-tuple-element.117), channel_id=1, source_target_pairs={{0,4},{1,5},{2,6},{3,7},{4,0},{5,1},{6,2},{7,3},{8,12},{9,13},{10,... | collective-permute-start | bytes 294920 | tf_op jit(solution)/shard_map/ppermute | solution.py:374
  69.9 9.6 %collective-permute-start.20 = (bf16[16,3072]{1,0:T(8,128)(2,1)S(1)}, bf16[16,3072]{1,0:T(8,128)(2,1)S(1)}, u32[]{:S(2)}, u32[]{:S(2)}) collective-permute-start(bf16[16,3072]{1,0:T(8,128)(2,1)S(1)} %get-tuple-element.118), channel_id=1, source_target_pairs={{0,6},{1,7},{2,4},{3,5},{4,2},{5,3},{6,0},{7,1},{8,14},{9,15},{10,... | collective-permute-start | bytes 294920 | tf_op jit(solution)/shard_map/ppermute | solution.py:374
  70.9 11.0 %collective-permute-start.21 = (bf16[192,384]{1,0:T(8,128)(2,1)S(1)}, bf16[192,384]{1,0:T(8,128)(2,1)S(1)}, u32[]{:S(2)}, u32[]{:S(2)}) collective-permute-start(bf16[192,384]{1,0:T(8,128)(2,1)S(1)} %get-tuple-element.121), channel_id=1, source_target_pairs={{0,24},{1,25},{2,26},{3,27},{4,28},{5,29},{6,30},{7,31},{8,16},{9,... | collective-permute-start | bytes 442376 | tf_op jit(solution)/shard_map/ppermute | solution.py:374
  74.6 8.0 %collective-permute-start.22 = (bf16[192,384]{1,0:T(8,128)(2,1)S(1)}, bf16[192,384]{1,0:T(8,128)(2,1)S(1)}, u32[]{:S(2)}, u32[]{:S(2)}) collective-permute-start(bf16[192,384]{1,0:T(8,128)(2,1)S(1)} %get-tuple-element.124), channel_id=1, source_target_pairs={{0,6},{1,7},{2,4},{3,5},{4,2},{5,3},{6,0},{7,1},{8,14},{9,15},{10,... | collective-permute-start | bytes 442376 | tf_op jit(solution)/shard_map/ppermute | solution.py:374
  79.9 5.7 %collective-permute-start.23 = (bf16[32,3072]{1,0:T(8,128)(2,1)S(1)}, bf16[32,3072]{1,0:T(8,128)(2,1)S(1)}, u32[]{:S(2)}, u32[]{:S(2)}) collective-permute-start(bf16[32,3072]{1,0:T(8,128)(2,1)S(1)} %get-tuple-element.127), channel_id=1, source_target_pairs={{0,1},{1,0},{2,3},{3,2},{4,5},{5,4},{6,7},{7,6},{8,9},{9,8},{10,11... | collective-permute-start | bytes 589832 | tf_op jit(solution)/shard_map/ppermute | solution.py:374
  83.1 5.1 %collective-permute-start.24 = (bf16[96,384]{1,0:T(8,128)(2,1)S(1)}, bf16[96,384]{1,0:T(8,128)(2,1)S(1)}, u32[]{:S(2)}, u32[]{:S(2)}) collective-permute-start(bf16[96,384]{1,0:T(8,128)(2,1)S(1)} %get-tuple-element.131), channel_id=1, source_target_pairs={{0,24},{1,25},{2,26},{3,27},{4,28},{5,29},{6,30},{7,31},{8,16},{9,... | collective-permute-start | bytes 221192 | tf_op jit(solution)/shard_map/ppermute | solution.py:374
  89.1 4.4 %collective-permute-start.28 = (f32[24,768]{1,0:T(8,128)S(1)}, f32[24,768]{1,0:T(8,128)S(1)}, u32[]{:S(2)}, u32[]{:S(2)}) collective-permute-start(f32[24,768]{1,0:T(8,128)S(1)} %get-tuple-element.136), channel_id=1, source_target_pairs={{0,10},{1,11},{2,8},{3,9},{4,14},{5,15},{6,12},{7,13},{8,2},{9,3},... | collective-permute-start | bytes 221192 | tf_op jit(solution)/shard_map/ppermute | solution.py:374
  (16 other events, 127.0 us)

commit v3 on v2

--- a/solution.py
+++ b/solution.py
@@ -14,6 +14,8 @@
 HS = 2
 W = HS * HD
 STEPS = H // HS
+HALF_STEPS = STEPS // 2
+UNROLL = True
 BF = jnp.bfloat16
 F = jnp.float32
 NT = (((1,), (1,)), ((), ()))
@@ -163,91 +165,106 @@
     return jnp.concatenate(att, 0), jnp.concatenate(gq, 0), fine, gxk, gxv
 
 
-def attention_kernel(base, q, k, v, l12, c1, z1, z2, z3, y1, y2, y3, ga, *rest):
-    att_o, gq_o, fine_o, gc_o, gz_o, gy1_o, gy2_o, gy3_o, attt_o = rest[-9:]
+def lanes(n, wide):
+    return pl.ds(pl.multiple_of(n * wide, wide), wide)
+
+
+def attention_kernel(bits, q, k, v, l12, c1, z1, z2, z3, y1, y2, y3, ga, *rest, first):
+    if first:
+        att_o, gq_o, fine_o, near_o, far_o, attt_o = rest
+    else:
+        far_i, att_o, gq_o, fine_o, near_o, gy1_o, gy2_o, gy3_o, attt_o = rest
+        for out, rows in ((gy1_o, slice(0, 32)), (gy2_o, slice(32, 48)), (gy3_o, slice(48, 64))):
+            out[:, :D] = far_i[rows, :]
+    base = (1 - bits[XH] if first else bits[XH]) * HALF_STEPS
     r = lax.broadcasted_iota(jnp.int32, (T, 192), 0)
     c = lax.broadcasted_iota(jnp.int32, (T, 192), 1)
     half = jnp.where((r >> 1) == c, 0.5, 0.0)
     expand = jnp.where(c < 128, half, jnp.where((r >> 2) == c - 128, 0.25, 0.0)).astype(BF)
     r = lax.broadcasted_iota(jnp.int32, (288, 1), 0)
     bias = jnp.where(r < 64, 0, (r >> 5) - 1).astype(F) * LN2
-    x = jnp.concatenate([c1[...], z1[...], z2[...], z3[...], y1[...], y2[...], y3[...]], 0)
-    for i in range(HS):
-        c = slice(i * HD, i * HD + HD)
-        cv = slice(W + i * HD, W + i * HD + HD)
-        att, gq, fine, gxk, gxv = head(
-            q[:, c], k[:, c], v[:, c], l12[:, c], l12[:, cv], x[:, c], x[:, cv], ga[:, c], bias, expand
-        )
-        att_o[:, c] = att.astype(BF)
-        attt_o[c, :] = jnp.transpose(att).astype(BF)
-        gq_o[:, c] = gq.astype(BF)
-        for cols, g, f in ((c, gxk, fine[:, :HD]), (cv, gxv, fine[:, HD:])):
-            fine_o[:, cols] = f
-            gc_o[:, cols] = g[:32]
-            gz_o[:, cols] = g[32:96]
-            gy1_o[:, cols] = g[96:128].astype(BF)
-            gy2_o[:, cols] = g[128:144].astype(BF)
-            gy3_o[:, cols] = g[144:].astype(BF)
-
-
-def attention(bits, flip, q, k, v, l12, pieces, ga, begun=()):
-    def cols(rows, wide=W):
-        return pl.BlockSpec((rows, wide), lambda h, s: (0, h + (s[XH] ^ flip) * (STEPS // 2)))
-
-    outs = shapes(
-        ((T, D), BF),
-        ((T, D), BF),
-        ((T, PAIR), F),
-        ((32, PAIR), F),
-        ((64, PAIR), F),
-        ((32, PAIR), BF),
-        ((16, PAIR), BF),
-        ((16, PAIR), BF),
-        ((D // 2, T), BF),
-    )
-    operands = (q, k, v, l12, *pieces, ga)
-    return pl.pallas_call(
-        attention_kernel,
-        grid_spec=pltpu.PrefetchScalarGridSpec(
-            num_scalar_prefetch=1,
-            grid=(STEPS // 2,),
-            in_specs=[cols(T)] * 3
-            + [cols(192, 2 * W)]
-            + [cols(p.shape[0], 2 * W) for p in pieces]
-            + [cols(T)]
-            + [pl.BlockSpec(memory_space=pl.ANY)] * len(begun),
-            out_specs=[cols(T), cols(T)]
-            + [cols(n, 2 * W) for n in (T, 32, 64, 32, 16, 16)]
-            + [pl.BlockSpec((W, T), lambda h, s: (h, 0))],
-        ),
-        out_shape=outs,
-        input_output_aliases={1 + len(operands) + i: i for i in range(len(begun))},
-        cost_estimate=cost(7),
-        compiler_params=params(24),
-        name="attention",
-    )(bits, *operands, *begun)
-
-
-def back_row_kernel(gz, y1, y2, y3, s1, s2, s3, own):
+
+    def step(i, carry):
+        wide, pair = lanes(base + i, W), lanes(base + i, 2 * W)
+        qs, ks, vs, gas, ps = q[:, wide], k[:, wide], v[:, wide], ga[:, wide], l12[:, pair]
+        x = jnp.concatenate([p[:, pair] for p in (c1, z1, z2, z3, y1, y2, y3)], 0)
+        done = []
+        for h in range(HS):
+            a = slice(h * HD, h * HD + HD)
+            b = slice(W + h * HD, W + h * HD + HD)
+            done.append(
+                head(qs[:, a], ks[:, a], vs[:, a], ps[:, a], ps[:, b], x[:, a], x[:, b], gas[:, a], bias, expand)
+            )
+        att = jnp.concatenate([d[0] for d in done], 1)
+        att_o[:, lanes(i, W)] = att.astype(BF)
+        attt_o[lanes(i, W), :] = jnp.transpose(att).astype(BF)
+        gq_o[:, lanes(i, W)] = jnp.concatenate([d[1] for d in done], 1).astype(BF)
+        parts = [d[2][:, :HD] for d in done] + [d[2][:, HD:] for d in done]
+        fine_o[:, lanes(i, 2 * W)] = jnp.concatenate(parts, 1)
+        g = jnp.concatenate([d[3] for d in done] + [d[4] for d in done], 1)
+        near_o[:, lanes(i, 2 * W)] = g[:96]
+        gb = g[96:].astype(BF)
+        if first:
+            far_o[:, lanes(i, 2 * W)] = gb
+        else:
+            to = lanes(i + HALF_STEPS, 2 * W)
+            gy1_o[:, to] = gb[:32]
+            gy2_o[:, to] = gb[32:48]
+            gy3_o[:, to] = gb[48:]
+        return carry
+
+    lax.fori_loop(0, HALF_STEPS, step, 0, unroll=UNROLL)
+
+
+def attention(bits, q, k, v, l12, pieces, ga, *far):
+    first = not far
+    outs = [((T, D // 2), BF), ((T, D // 2), BF), ((T, D), F), ((96, D), F)]
+    outs += [((64, D), BF)] if first else [((32, PAIR), BF), ((16, PAIR), BF), ((16, PAIR), BF)]
+    outs += [((D // 2, T), BF)]
+    return placed(
+        lambda *refs: attention_kernel(*refs, first=first), outs, "attention", 7, 32, bits, q, k, v, l12, *pieces, ga, *far
+    )
+
+
+def placed(kernel, outs, name, us, mib, bits, *operands):
+    vmem = pl.BlockSpec(memory_space=pltpu.VMEM)
+    return pl.pallas_call(
+        kernel,
+        in_specs=[pl.BlockSpec(memory_space=pltpu.SMEM)] + [vmem] * len(operands),
+        out_specs=[vmem] * len(outs),
+        out_shape=shapes(*outs),
+        cost_estimate=cost(us),
+        compiler_params=params(mib),
+        name=name,
+    )(bits, *operands)
+
+
+def back_row_kernel(near_a, near_b, y1, y2, y3, s1, s2, s3, own):
     g6 = y1[...].astype(F) + spread(y2[...].astype(F) + y3[...].astype(F), 1)
-    s1[...] = (gz[:32, :] + spread(g6[8:16], 2)).astype(BF)
-    s2[...] = (gz[32:48, :] + spread(g6[16:24], 1)).astype(BF)
-    s3[...] = (gz[48:, :] + spread(g6[24:], 1)).astype(BF)
+    for i, near in enumerate((near_a, near_b)):
+        c = slice(i * D, i * D + D)
+        s1[:, c] = (near[32:64, :] + spread(g6[8:16, c], 2)).astype(BF)
+        s2[:, c] = (near[64:80, :] + spread(g6[16:24, c], 1)).astype(BF)
+        s3[:, c] = (near[80:, :] + spread(g6[24:, c], 1)).astype(BF)
     own[...] = spread(g6[:8], 2)
 
 
-def back_chip_kernel(gc, own, z1, z2, z3, send, keep):
+def back_chip_kernel(near_a, near_b, own, z1, z2, z3, send, keep):
     g4 = own[...] + z1[...].astype(F) + spread(z2[...].astype(F) + z3[...].astype(F), 1)
-    send[...] = (gc[...] + spread(g4[16:], 1)).astype(BF)
+    for i, near in enumerate((near_a, near_b)):
+        c = slice(i * D, i * D + D)
+        send[:, c] = (near[:32, :] + spread(g4[16:, c], 1)).astype(BF)
     keep[...] = spread(g4[:16], 1)
 
 
-def finish_kernel(fine, keep, c1, gk, gv):
-    g3 = keep[...] + c1[...].astype(F)
-    for step in range(STEPS):
-        for i, out in enumerate((gk, gv)):
-            c = slice((2 * step + i) * W, (2 * step + i) * W + W)
-            out[:, step * W : step * W + W] = (fine[:, c] + spread(g3[:, c], 3)).astype(BF)
+def finish_kernel(bits, fine_a, fine_b, keep, c1, gk, gv):
+    g3 = spread(keep[...] + c1[...].astype(F), 3)
+    for half, (fine, side) in enumerate(((fine_a, 1 - bits[XH]), (fine_b, bits[XH]))):
+        for step in range(HALF_STEPS):
+            for i, out in enumerate((gk, gv)):
+                n = 2 * step + i
+                total = fine[:, n * W : n * W + W] + g3[:, half * D + n * W : half * D + n * W + W]
+                out[:, lanes(side * HALF_STEPS + step, W)] = total.astype(BF)
 
 
 def split_kernel(bits, go, go_m, go_o):
@@ -275,9 +292,14 @@
         ga[:, c : c + 256] = mm(go[...], w[c : c + 256, :], NT).astype(BF)
 
 
-def mixed_kernel(att, w, out):
+def mixed_kernel(bits, att_a, att_b, gq_a, gq_b, w, mixed, gq):
+    half = D // 2
+    a, b = lanes(1 - bits[XH], half), lanes(bits[XH], half)
+    gq[:, a] = gq_a[...]
+    gq[:, b] = gq_b[...]
     for c in range(0, D, 256):
-        out[:, c : c + 256] = mm(att[...], w[:, c : c + 256], NN).astype(BF)
+        cols = slice(c, c + 256)
+        mixed[:, cols] = (mm(att_a[...], w[a, cols], NN) + mm(att_b[...], w[b, cols], NN)).astype(BF)
 
 
 def small(kernel, outs, name, us=0.4):
@@ -401,10 +423,10 @@
     gox_m, gox_o = across_x(go_m, 3), across_x(go_o, 3)
     y1, y3, y2 = across(l6, 8), across(l7, 24), across(l7, 16)
     pieces = (c1, z1, z2, z3, y1, y2, y3)
-    *begun, sent = attention(bits, 1, after(q, gox_m), k, v, l12, pieces, ga)
+    att_a, gq_a, fine_a, near_a, far, sent = attention(bits, after(q, gox_m, gox_o), k, v, l12, pieces, ga)
     att_x = across_x(sent, 3)
-    att, gq, fine, gc, gz, gy1, gy2, gy3, att_m = attention(
-        bits, 0, after(q, gox_o), k, v, l12, pieces, ga, begun
+    att_b, gq_b, fine_b, near_b, gy1, gy2, gy3, att_m = attention(
+        bits, after(q, sent), k, v, l12, pieces, ga, far
     )
     att_o, att_xo = across(att_m, 1), across(att_x, 1)
     y1, y3, y2 = across(gy1, 8), across(gy3, 24), across(gy2, 16)
@@ -416,22 +438,26 @@
     a_r = across_x(a_s, 1)
     s1, s2, s3, own = small(
         back_row_kernel, [((32, PAIR), BF), ((16, PAIR), BF), ((16, PAIR), BF), ((32, PAIR), F)], "back_row"
-    )(after(gz, a_k), y1, y2, y3)
+    )(near_a, after(near_b, a_k), y1, y2, y3)
     z1, z3, z2 = across(s1, 2), across(s3, 6), across(s2, 4)
     b_s, b_k = merge(bits, [(after(b_k, own), b_r)], YH, 2, 96)
     b_r = across(b_s, 24)
     a_s, a_k = merge(bits, [(after(a_k, b_k), a_r)], ZH, 4, 48)
     a_r = across(a_s, 6)
-    mixed = small(mixed_kernel, [((T, D), BF)], "mixed", 2.3)(after(att, a_k), w_out)[0]
+    mixed, gq = placed(
+        mixed_kernel, [((T, D), BF)] * 2, "mixed", 2.3, 12, bits, after(att_a, a_k), att_b, gq_a, gq_b, w_out
+    )
     send, keep = small(back_chip_kernel, [((32, PAIR), BF), ((32, PAIR), F)], "back_chip")(
-        after(gc, mixed), own, z1, z2, z3
+        near_a, after(near_b, mixed), own, z1, z2, z3
     )
     c1 = across(send, 1)
     b_s, b_k = merge(bits, [(after(b_k, keep), b_r)], XL, 1, 96)
     b_r = across_x(b_s, 1)
     a_s, a_k = merge(bits, [(after(a_k, b_k), a_r)], YH, 1, 96)
     a_r = across(a_s, 24)
-    gk, gv = small(finish_kernel, [((T, D), BF), ((T, D), BF)], "finish", 1.7)(after(fine, a_k), keep, c1)
+    gk, gv = placed(
+        finish_kernel, [((T, D), BF)] * 2, "finish", 1.7, 12, bits, after(fine_a, a_k), fine_b, keep, c1
+    )
     s1, s2, s3, kept = last_merge(bits, after(a_k, gk), a_r, b_k, b_r)
     part = kept + across(s1, 8) + across(s2, 2) + across(s3, 10)
     first = core == 0

time: 98.7 us -> 95.6 us (0.969)
  Pallas kernels: 30.7 us -> 27.8 us
  waiting for transfers between devices: 15 us -> 17.3 us
  local copies, waits for them, and re-layouts: 5.97 us -> 4.71 us
  starting transfers between devices: 45.2 us -> 44.1 us
    pallas_call x4, Pallas kernels: 18.4 us -> 15.4 us  [placed(): pl.pallas_call(kernel, in_specs=[pl.BlockSpec(memory_space=pltpu.SMEM)] +...]
    ppermute x25, waiting for transfers between devices: 14.9 us -> 17.3 us  [across(): return lax.ppermute(x, 'seq', [(i, i ^ flip) for i in range(32)])]
    unnamed x20 -> x18, local copies, waits for them, and re-layouts: 5.88 us -> 4.63 us
  transfers between devices with their start and end apart: 30 -> 30, of which waited for: 10 -> 10; matrix products, arithmetic and copies ran while one was open for 0% -> 0% of each run, Pallas kernels for 28% -> 21%
where the time goes in v3:
time: 95.6 us; the launch traced here: 95.4 us
  starting transfers between devices  44.1 us (46%)
  Pallas kernels  27.8 us (29%)
  waiting for transfers between devices  17.3 us (18%)
  local copies, waits for them, and re-layouts  4.71 us (5%)
    ppermute x25, starting transfers between devices, across(): return lax.ppermute(x, 'seq', [(i, i ^ flip) for i in range(32)])  37.3 us
    ppermute x25, waiting for transfers between devices, across(): return lax.ppermute(x, 'seq', [(i, i ^ flip) for i in range(32)])  17.3 us
    pallas_call x4, Pallas kernels, placed(): pl.pallas_call(kernel, in_specs=[pl.BlockSpec(memory_space=pltpu.SMEM)] +...  15.4 us
    ppermute x5, starting transfers between devices, across_x(): return lax.ppermute(x, 'dp', [(i, i ^ flip) for i in range(4)])  6.81 us
    unnamed x18, local copies, waits for them, and re-layouts  4.63 us
    pallas_call x2, Pallas kernels, weight(): pl.pallas_call(lambda *refs: weight_kernel(*refs, color=color, bit=bit, o...  3.91 us
    pallas_call x4, Pallas kernels, merge(): pl.pallas_call(lambda *refs: merge_kernel(*refs, bit=bit, outer=outer, ha...  2.42 us
  transfers between devices with their start and end apart: 30, of which 10 were waited for; matrix products, arithmetic and copies ran while one was open for 0% of the time, Pallas kernels for 21%

profile of v3, /device:TPU:1, one launch (start us, length us, event | category | flops | bytes accessed | tf_op | source)
XLA Modules:
  0.0 95.4 jit_solution(8165004748718604370)
XLA Ops:
  3.0 1.8 %pyramid.1 = (bf16[192,3072]{1,0:T(8,128)(2,1)S(1)}, bf16[32,3072]{1,0:T(8,128)(2,1)S(1)}) custom-call(bf16[256,1536]{1,0:T(8,128)(2,1)S(1)} %bitcast.17, bf16[256,1536]{1,0:T(8,128)(2,1)S(1)} %bitcast.20), custom_call_target="tpu_custom_call" | custom-call | bytes 7030000 | tf_op jit(solution)/shard_map/pyramid/pallas_call | solution.py:86
  7.1 2.6 %collective-permute-start = (bf16[256,768]{1,0:T(8,128)(2,1)S(1)}, bf16[256,768]{1,0:T(8,128)(2,1)S(1)}, u32[]{:S(2)}, u32[]{:S(2)}) collective-permute-start(bf16[256,768]{1,0:T(8,128)(2,1)S(1)} %get-tuple-element.72.refs_5_), channel_id=1, source_target_pairs={{0,96},{32,64},{64,32},{96,0},{1,97},{33,65},{65,33},{97,1},{2,98}... | collective-permute-start | bytes 1179656 | tf_op jit(solution)/shard_map/ppermute | solution.py:400
  11.2 1.7 %collective-permute-start.4 = (bf16[32,3072]{1,0:T(8,128)(2,1)S(1)}, bf16[32,3072]{1,0:T(8,128)(2,1)S(1)}, u32[]{:S(2)}, u32[]{:S(2)}) collective-permute-start(bf16[32,3072]{1,0:T(8,128)(2,1)S(1)} %get-tuple-element.76), channel_id=1, source_target_pairs={{0,2},{1,3},{2,0},{3,1},{4,6},{5,7},{6,4},{7,5},{8,10},{9,11},{10,... | collective-permute-start | bytes 589832 | tf_op jit(solution)/shard_map/ppermute | solution.py:396
  12.9 3.3 %collective-permute-start.5 = (bf16[16,3072]{1,0:T(8,128)(2,1)S(1)}, bf16[16,3072]{1,0:T(8,128)(2,1)S(1)}, u32[]{:S(2)}, u32[]{:S(2)}) collective-permute-start(bf16[16,3072]{1,0:T(8,128)(2,1)S(1)} %get-tuple-element.78.l5), channel_id=1, source_target_pairs={{0,4},{1,5},{2,6},{3,7},{4,0},{5,1},{6,2},{7,3},{8,12},{9,13},{10,... | collective-permute-start | bytes 294920 | tf_op jit(solution)/shard_map/ppermute | solution.py:396
  16.2 6.1 %collective-permute-done.5.z2.refs_7_ = bf16[16,3072]{1,0:T(8,128)(2,1)S(1)} collective-permute-done((bf16[16,3072]{1,0:T(8,128)(2,1)S(1)}, bf16[16,3072]{1,0:T(8,128)(2,1)S(1)}, u32[]{:S(2)}, u32[]{:S(2)}) %collective-permute-start.5) | collective-permute-done | bytes 98336 | tf_op jit(solution)/shard_map/ppermute | solution.py:396
  24.1 2.6 %collective-permute-start.8 = (bf16[16,3072]{1,0:T(8,128)(2,1)S(1)}, bf16[16,3072]{1,0:T(8,128)(2,1)S(1)}, u32[]{:S(2)}, u32[]{:S(2)}) collective-permute-start(bf16[16,3072]{1,0:T(8,128)(2,1)S(1)} %get-tuple-element.80), channel_id=1, source_target_pairs={{0,16},{1,17},{2,18},{3,19},{4,20},{5,21},{6,22},{7,23},{8,24},{9,... | collective-permute-start | bytes 294920 | tf_op jit(solution)/shard_map/ppermute | solution.py:396
  26.8 2.3 %copy-done = bf16[1536,1536]{1,0:T(8,128)(2,1)S(1)} copy-done((bf16[1536,1536]{1,0:T(8,128)(2,1)S(1)}, bf16[1536,1536]{1,0:T(8,128)(2,1)}, u32[]{:S(2)}) %copy-start) | copy-done | bytes 4718616
  32.0 5.1 %attention.2 = (bf16[256,768]{1,0:T(8,128)(2,1)S(1)}, bf16[256,768]{1,0:T(8,128)(2,1)S(1)}, f32[256,1536]{1,0:T(8,128)S(1)}, f32[96,1536]{1,0:T(8,128)S(1)}, bf1...) custom-call(s32[7]{0:T(128)S(1)} %stack.31.bits.refs_0_, bf16[256,1536]{1,0:T(8,128)(2,1)S(1)} %bitcast.25, ...), custom_call_target="tpu_custom_call" | custom-call | bytes 25900000 | tf_op jit(solution)/shard_map/attention/pallas_call | solution.py:231
  37.0 1.5 %collective-permute-start.11 = (bf16[768,256]{1,0:T(8,128)(2,1)S(1)}, bf16[768,256]{1,0:T(8,128)(2,1)S(1)}, u32[]{:S(2)}, u32[]{:S(2)}) collective-permute-start(bf16[768,256]{1,0:T(8,128)(2,1)S(1)} %get-tuple-element.83), channel_id=1, source_target_pairs={{0,96},{32,64},{64,32},{96,0},{1,97},{33,65},{65,33},{97,1},{2,98}... | collective-permute-start | bytes 1179656 | tf_op jit(solution)/shard_map/ppermute | solution.py:400
  38.6 5.1 %attention.3 = (bf16[256,768]{1,0:T(8,128)(2,1)S(1)}, bf16[256,768]{1,0:T(8,128)(2,1)S(1)}, f32[256,1536]{1,0:T(8,128)S(1)}, f32[96,1536]{1,0:T(8,128)S(1)}, bf1...) custom-call(s32[7]{0:T(128)S(1)} %stack.31.bits.refs_0_, ...), custom_call_target="tpu_custom_call" | custom-call | bytes 25900000 | tf_op jit(solution)/shard_map/attention/pallas_call | solution.py:231
  43.7 4.2 %collective-permute-start.10 = (bf16[768,256]{1,0:T(8,128)(2,1)S(1)}, bf16[768,256]{1,0:T(8,128)(2,1)S(1)}, u32[]{:S(2)}, u32[]{:S(2)}) collective-permute-start(bf16[768,256]{1,0:T(8,128)(2,1)S(1)} %get-tuple-element.88.refs_1_), channel_id=1, source_target_pairs={{0,1},{1,0},{2,3},{3,2},{4,5},{5,4},{6,7},{7,6},{8,9},{9,8},{10,11... | collective-permute-start | bytes 1179656 | tf_op jit(solution)/shard_map/ppermute | solution.py:396
  47.9 2.3 %collective-permute-start.12 = (bf16[768,256]{1,0:T(8,128)(2,1)S(1)}, bf16[768,256]{1,0:T(8,128)(2,1)S(1)}, u32[]{:S(2)}, u32[]{:S(2)}) collective-permute-start(bf16[768,256]{1,0:T(8,128)(2,1)S(1)} %collective-permute-done.11.refs_3_), channel_id=1, source_target_pairs={{0,1},{1,0},{2,3},{3,2},{4,5},{5,4},{6,7},{7,6},{8,9},{9,8},{10,11... | collective-permute-start | bytes 1179656 | tf_op jit(solution)/shard_map/ppermute | solution.py:396
  51.5 2.4 %weight_part.2 = (bf16[384,384]{1,0:T(8,128)(2,1)S(1)}, bf16[384,384]{1,0:T(8,128)(2,1)S(1)}) custom-call(s32[7]{0:T(128)S(1)} %stack.31.bits.refs_0_, bf16[768,256]{1,0:T(8,128)(2,1)S(1)} %get-tuple-element.88.refs_1_, bf16[768,256]{1,0:T(8,128)(2,1)S(1)} %collective-permute-done.10.refs_2_, bf16[768,256]{1,0:T(8,128)(2,1)S(1)} %collective-permute-done.11.refs_3_, ...), custom_call_target="tpu_custom_call" | custom-call | bytes 5550000 | tf_op jit(solution)/shard_map/weight_part/pallas_call | solution.py:329
  53.9 1.6 %collective-permute-start.16 = (bf16[384,384]{1,0:T(8,128)(2,1)S(1)}, bf16[384,384]{1,0:T(8,128)(2,1)S(1)}, u32[]{:S(2)}, u32[]{:S(2)}) collective-permute-start(bf16[384,384]{1,0:T(8,128)(2,1)S(1)} %get-tuple-element.98), channel_id=1, source_target_pairs={{0,6},{1,7},{2,4},{3,5},{4,2},{5,3},{6,0},{7,1},{8,14},{9,15},{10,... | collective-permute-start | bytes 884744 | tf_op jit(solution)/shard_map/ppermute | solution.py:396
  57.9 1.7 %collective-permute-start.15 = (bf16[16,3072]{1,0:T(8,128)(2,1)S(1)}, bf16[16,3072]{1,0:T(8,128)(2,1)S(1)}, u32[]{:S(2)}, u32[]{:S(2)}) collective-permute-start(bf16[16,3072]{1,0:T(8,128)(2,1)S(1)} %get-tuple-element.95), channel_id=1, source_target_pairs={{0,24},{1,25},{2,26},{3,27},{4,28},{5,29},{6,30},{7,31},{8,16},{9,... | collective-permute-start | bytes 294920 | tf_op jit(solution)/shard_map/ppermute | solution.py:396
  59.7 2.5 %collective-permute-done.14.y2 = bf16[16,3072]{1,0:T(8,128)(2,1)S(1)} collective-permute-done((bf16[16,3072]{1,0:T(8,128)(2,1)S(1)}, bf16[16,3072]{1,0:T(8,128)(2,1)S(1)}, u32[]{:S(2)}, u32[]{:S(2)}) %collective-permute-start.14) | collective-permute-done | bytes 98336 | tf_op jit(solution)/shard_map/ppermute | solution.py:396
  62.2 3.3 %collective-permute-done.15.y3 = bf16[16,3072]{1,0:T(8,128)(2,1)S(1)} collective-permute-done((bf16[16,3072]{1,0:T(8,128)(2,1)S(1)}, bf16[16,3072]{1,0:T(8,128)(2,1)S(1)}, u32[]{:S(2)}, u32[]{:S(2)}) %collective-permute-start.15) | collective-permute-done | bytes 98336 | tf_op jit(solution)/shard_map/ppermute | solution.py:396
  66.0 2.4 %collective-permute-start.19 = (bf16[16,3072]{1,0:T(8,128)(2,1)S(1)}, bf16[16,3072]{1,0:T(8,128)(2,1)S(1)}, u32[]{:S(2)}, u32[]{:S(2)}) collective-permute-start(bf16[16,3072]{1,0:T(8,128)(2,1)S(1)} %get-tuple-element.112), channel_id=1, source_target_pairs={{0,4},{1,5},{2,6},{3,7},{4,0},{5,1},{6,2},{7,3},{8,12},{9,13},{10,... | collective-permute-start | bytes 294920 | tf_op jit(solution)/shard_map/ppermute | solution.py:396
  71.8 2.0 %collective-permute-start.22 = (bf16[192,384]{1,0:T(8,128)(2,1)S(1)}, bf16[192,384]{1,0:T(8,128)(2,1)S(1)}, u32[]{:S(2)}, u32[]{:S(2)}) collective-permute-start(bf16[192,384]{1,0:T(8,128)(2,1)S(1)} %get-tuple-element.119), channel_id=1, source_target_pairs={{0,6},{1,7},{2,4},{3,5},{4,2},{5,3},{6,0},{7,1},{8,14},{9,15},{10,... | collective-permute-start | bytes 442376 | tf_op jit(solution)/shard_map/ppermute | solution.py:396
  73.8 3.0 %mixed.1 = (bf16[256,1536]{1,0:T(8,128)(2,1)}, bf16[256,1536]{1,0:T(8,128)(2,1)}) custom-call(s32[7]{0:T(128)S(1)} %stack.31.bits.refs_0_, bf16[256,768]{1,0:T(8,128)(2,1)S(1)} %get-tuple-element.103.att_a, bf16[256,768]{1,0:T(8,128)(2,1)S(1)} %get-tuple-element.104.att_b, bf16[256,768]{1,0:T(8,128)(2,1)S(1)} %get-tuple-element.105.gq_a, ...), custom_call_target="tpu_custom_call" | custom-call | bytes 8510000 | tf_op jit(solution)/shard_map/mixed/pallas_call | solution.py:231
  77.2 2.0 %collective-permute-start.23 = (bf16[32,3072]{1,0:T(8,128)(2,1)S(1)}, bf16[32,3072]{1,0:T(8,128)(2,1)S(1)}, u32[]{:S(2)}, u32[]{:S(2)}) collective-permute-start(bf16[32,3072]{1,0:T(8,128)(2,1)S(1)} %get-tuple-element.123), channel_id=1, source_target_pairs={{0,1},{1,0},{2,3},{3,2},{4,5},{5,4},{6,7},{7,6},{8,9},{9,8},{10,11... | collective-permute-start | bytes 589832 | tf_op jit(solution)/shard_map/ppermute | solution.py:396
  83.2 2.2 %finish.1 = (bf16[256,1536]{1,0:T(8,128)(2,1)}, bf16[256,1536]{1,0:T(8,128)(2,1)}) custom-call(s32[7]{0:T(128)S(1)} %stack.31.bits.refs_0_, f32[256,1536]{1,0:T(8,128)S(1)} %get-tuple-element.121.fine_a, f32[256,1536]{1,0:T(8,128)S(1)} %get-tuple-element.122.fine_b, f32[32,3072]{1,0:T(8,128)S(1)} %get-tuple-element.114.keep, ...), custom_call_target="tpu_custom_call" | custom-call | bytes 6290000 | tf_op jit(solution)/shard_map/finish/pallas_call | solution.py:231
  86.3 2.5 %collective-permute-start.28 = (f32[24,768]{1,0:T(8,128)S(1)}, f32[24,768]{1,0:T(8,128)S(1)}, u32[]{:S(2)}, u32[]{:S(2)}) collective-permute-start(f32[24,768]{1,0:T(8,128)S(1)} %get-tuple-element.132), channel_id=1, source_target_pairs={{0,10},{1,11},{2,8},{3,9},{4,14},{5,15},{6,12},{7,13},{8,2},{9,3},... | collective-permute-start | bytes 221192 | tf_op jit(solution)/shard_map/ppermute | solution.py:396
  90.6 3.3 %collective-permute-start.29 = (f32[12,768]{1,0:T(8,128)S(1)}, f32[12,768]{1,0:T(8,128)S(1)}, u32[]{:S(2)}, u32[]{:S(2)}) collective-permute-start(f32[12,768]{1,0:T(8,128)S(1)} %slice_select_fusion), channel_id=1, source_target_pairs={{0,1},{1,0},{2,3},{3,2},{4,5},{5,4},{6,7},{7,6},{8,9},{9,8},{10,11... | collective-permute-start | bytes 110600 | tf_op jit(solution)/shard_map/ppermute | solution.py:396
  (78 shorter events, 26.9 us)
Async XLA Ops:
  5.5 4.2 %collective-permute-start.1 = (bf16[256,768]{1,0:T(8,128)(2,1)S(1)}, bf16[256,768]{1,0:T(8,128)(2,1)S(1)}, u32[]{:S(2)}, u32[]{:S(2)}) collective-permute-start(bf16[256,768]{1,0:T(8,128)(2,1)S(1)} %get-tuple-element.73), channel_id=1, source_target_pairs={{0,1},{1,0},{2,3},{3,2},{4,5},{5,4},{6,7},{7,6},{8,9},{9,8},{10,11... | collective-permute-start | bytes 1179656 | tf_op jit(solution)/shard_map/ppermute | solution.py:396
  7.1 23.5 %collective-permute-start = (bf16[256,768]{1,0:T(8,128)(2,1)S(1)}, bf16[256,768]{1,0:T(8,128)(2,1)S(1)}, u32[]{:S(2)}, u32[]{:S(2)}) collective-permute-start(bf16[256,768]{1,0:T(8,128)(2,1)S(1)} %get-tuple-element.72.refs_5_), channel_id=1, source_target_pairs={{0,96},{32,64},{64,32},{96,0},{1,97},{33,65},{65,33},{97,1},{2,98}... | collective-permute-start | bytes 1179656 | tf_op jit(solution)/shard_map/ppermute | solution.py:400
  9.6 20.9 %collective-permute-start.2 = (bf16[256,768]{1,0:T(8,128)(2,1)S(1)}, bf16[256,768]{1,0:T(8,128)(2,1)S(1)}, u32[]{:S(2)}, u32[]{:S(2)}) collective-permute-start(bf16[256,768]{1,0:T(8,128)(2,1)S(1)} %collective-permute-done.1.refs_6_), channel_id=1, source_target_pairs={{0,96},{32,64},{64,32},{96,0},{1,97},{33,65},{65,33},{97,1},{2,98}... | collective-permute-start | bytes 1179656 | tf_op jit(solution)/shard_map/ppermute | solution.py:400
  11.2 11.2 %collective-permute-start.4 = (bf16[32,3072]{1,0:T(8,128)(2,1)S(1)}, bf16[32,3072]{1,0:T(8,128)(2,1)S(1)}, u32[]{:S(2)}, u32[]{:S(2)}) collective-permute-start(bf16[32,3072]{1,0:T(8,128)(2,1)S(1)} %get-tuple-element.76), channel_id=1, source_target_pairs={{0,2},{1,3},{2,0},{3,1},{4,6},{5,7},{6,4},{7,5},{8,10},{9,11},{10,... | collective-permute-start | bytes 589832 | tf_op jit(solution)/shard_map/ppermute | solution.py:396
  12.9 9.4 %collective-permute-start.5 = (bf16[16,3072]{1,0:T(8,128)(2,1)S(1)}, bf16[16,3072]{1,0:T(8,128)(2,1)S(1)}, u32[]{:S(2)}, u32[]{:S(2)}) collective-permute-start(bf16[16,3072]{1,0:T(8,128)(2,1)S(1)} %get-tuple-element.78.l5), channel_id=1, source_target_pairs={{0,4},{1,5},{2,6},{3,7},{4,0},{5,1},{6,2},{7,3},{8,12},{9,13},{10,... | collective-permute-start | bytes 294920 | tf_op jit(solution)/shard_map/ppermute | solution.py:396
  16.2 6.1 %collective-permute-start.6 = (bf16[16,3072]{1,0:T(8,128)(2,1)S(1)}, bf16[16,3072]{1,0:T(8,128)(2,1)S(1)}, u32[]{:S(2)}, u32[]{:S(2)}) collective-permute-start(bf16[16,3072]{1,0:T(8,128)(2,1)S(1)} %get-tuple-element.78.l5), channel_id=1, source_target_pairs={{0,6},{1,7},{2,4},{3,5},{4,2},{5,3},{6,0},{7,1},{8,14},{9,15},{10,... | collective-permute-start | bytes 294920 | tf_op jit(solution)/shard_map/ppermute | solution.py:396
  22.8 9.2 %collective-permute-start.7 = (bf16[32,3072]{1,0:T(8,128)(2,1)S(1)}, bf16[32,3072]{1,0:T(8,128)(2,1)S(1)}, u32[]{:S(2)}, u32[]{:S(2)}) collective-permute-start(bf16[32,3072]{1,0:T(8,128)(2,1)S(1)} %get-tuple-element.79), channel_id=1, source_target_pairs={{0,8},{1,9},{2,10},{3,11},{4,12},{5,13},{6,14},{7,15},{8,0},{9,1},... | collective-permute-start | bytes 589832 | tf_op jit(solution)/shard_map/ppermute | solution.py:396
  24.1 7.0 %collective-permute-start.8 = (bf16[16,3072]{1,0:T(8,128)(2,1)S(1)}, bf16[16,3072]{1,0:T(8,128)(2,1)S(1)}, u32[]{:S(2)}, u32[]{:S(2)}) collective-permute-start(bf16[16,3072]{1,0:T(8,128)(2,1)S(1)} %get-tuple-element.80), channel_id=1, source_target_pairs={{0,16},{1,17},{2,18},{3,19},{4,20},{5,21},{6,22},{7,23},{8,24},{9,... | collective-permute-start | bytes 294920 | tf_op jit(solution)/shard_map/ppermute | solution.py:396
  26.8 5.2 %collective-permute-start.9 = (bf16[16,3072]{1,0:T(8,128)(2,1)S(1)}, bf16[16,3072]{1,0:T(8,128)(2,1)S(1)}, u32[]{:S(2)}, u32[]{:S(2)}) collective-permute-start(bf16[16,3072]{1,0:T(8,128)(2,1)S(1)} %get-tuple-element.80), channel_id=1, source_target_pairs={{0,24},{1,25},{2,26},{3,27},{4,28},{5,29},{6,30},{7,31},{8,16},{9,... | collective-permute-start | bytes 294920 | tf_op jit(solution)/shard_map/ppermute | solution.py:396
  37.0 10.8 %collective-permute-start.11 = (bf16[768,256]{1,0:T(8,128)(2,1)S(1)}, bf16[768,256]{1,0:T(8,128)(2,1)S(1)}, u32[]{:S(2)}, u32[]{:S(2)}) collective-permute-start(bf16[768,256]{1,0:T(8,128)(2,1)S(1)} %get-tuple-element.83), channel_id=1, source_target_pairs={{0,96},{32,64},{64,32},{96,0},{1,97},{33,65},{65,33},{97,1},{2,98}... | collective-permute-start | bytes 1179656 | tf_op jit(solution)/shard_map/ppermute | solution.py:400
  43.7 6.5 %collective-permute-start.10 = (bf16[768,256]{1,0:T(8,128)(2,1)S(1)}, bf16[768,256]{1,0:T(8,128)(2,1)S(1)}, u32[]{:S(2)}, u32[]{:S(2)}) collective-permute-start(bf16[768,256]{1,0:T(8,128)(2,1)S(1)} %get-tuple-element.88.refs_1_), channel_id=1, source_target_pairs={{0,1},{1,0},{2,3},{3,2},{4,5},{5,4},{6,7},{7,6},{8,9},{9,8},{10,11... | collective-permute-start | bytes 1179656 | tf_op jit(solution)/shard_map/ppermute | solution.py:396
  50.1 15.3 %collective-permute-start.13 = (bf16[32,3072]{1,0:T(8,128)(2,1)S(1)}, bf16[32,3072]{1,0:T(8,128)(2,1)S(1)}, u32[]{:S(2)}, u32[]{:S(2)}) collective-permute-start(bf16[32,3072]{1,0:T(8,128)(2,1)S(1)} %get-tuple-element.93), channel_id=1, source_target_pairs={{0,8},{1,9},{2,10},{3,11},{4,12},{5,13},{6,14},{7,15},{8,0},{9,1},... | collective-permute-start | bytes 589832 | tf_op jit(solution)/shard_map/ppermute | solution.py:396
  53.9 16.0 %collective-permute-start.16 = (bf16[384,384]{1,0:T(8,128)(2,1)S(1)}, bf16[384,384]{1,0:T(8,128)(2,1)S(1)}, u32[]{:S(2)}, u32[]{:S(2)}) collective-permute-start(bf16[384,384]{1,0:T(8,128)(2,1)S(1)} %get-tuple-element.98), channel_id=1, source_target_pairs={{0,6},{1,7},{2,4},{3,5},{4,2},{5,3},{6,0},{7,1},{8,14},{9,15},{10,... | collective-permute-start | bytes 884744 | tf_op jit(solution)/shard_map/ppermute | solution.py:396
  57.0 14.2 %collective-permute-start.17 = (bf16[384,384]{1,0:T(8,128)(2,1)S(1)}, bf16[384,384]{1,0:T(8,128)(2,1)S(1)}, u32[]{:S(2)}, u32[]{:S(2)}) collective-permute-start(bf16[384,384]{1,0:T(8,128)(2,1)S(1)} %get-tuple-element.101), channel_id=1, source_target_pairs={{0,32},{32,0},{64,96},{96,64},{1,33},{33,1},{65,97},{97,65},{2,34}... | collective-permute-start | bytes 884744 | tf_op jit(solution)/shard_map/ppermute | solution.py:400
  57.1 5.1 %collective-permute-start.14 = (bf16[16,3072]{1,0:T(8,128)(2,1)S(1)}, bf16[16,3072]{1,0:T(8,128)(2,1)S(1)}, u32[]{:S(2)}, u32[]{:S(2)}) collective-permute-start(bf16[16,3072]{1,0:T(8,128)(2,1)S(1)} %get-tuple-element.94), channel_id=1, source_target_pairs={{0,16},{1,17},{2,18},{3,19},{4,20},{5,21},{6,22},{7,23},{8,24},{9,... | collective-permute-start | bytes 294920 | tf_op jit(solution)/shard_map/ppermute | solution.py:396
  57.9 7.5 %collective-permute-start.15 = (bf16[16,3072]{1,0:T(8,128)(2,1)S(1)}, bf16[16,3072]{1,0:T(8,128)(2,1)S(1)}, u32[]{:S(2)}, u32[]{:S(2)}) collective-permute-start(bf16[16,3072]{1,0:T(8,128)(2,1)S(1)} %get-tuple-element.95), channel_id=1, source_target_pairs={{0,24},{1,25},{2,26},{3,27},{4,28},{5,29},{6,30},{7,31},{8,16},{9,... | collective-permute-start | bytes 294920 | tf_op jit(solution)/shard_map/ppermute | solution.py:396
  65.9 10.9 %collective-permute-start.18 = (bf16[32,3072]{1,0:T(8,128)(2,1)S(1)}, bf16[32,3072]{1,0:T(8,128)(2,1)S(1)}, u32[]{:S(2)}, u32[]{:S(2)}) collective-permute-start(bf16[32,3072]{1,0:T(8,128)(2,1)S(1)} %get-tuple-element.111), channel_id=1, source_target_pairs={{0,2},{1,3},{2,0},{3,1},{4,6},{5,7},{6,4},{7,5},{8,10},{9,11},{10,... | collective-permute-start | bytes 589832 | tf_op jit(solution)/shard_map/ppermute | solution.py:396
  66.0 10.8 %collective-permute-start.19 = (bf16[16,3072]{1,0:T(8,128)(2,1)S(1)}, bf16[16,3072]{1,0:T(8,128)(2,1)S(1)}, u32[]{:S(2)}, u32[]{:S(2)}) collective-permute-start(bf16[16,3072]{1,0:T(8,128)(2,1)S(1)} %get-tuple-element.112), channel_id=1, source_target_pairs={{0,4},{1,5},{2,6},{3,7},{4,0},{5,1},{6,2},{7,3},{8,12},{9,13},{10,... | collective-permute-start | bytes 294920 | tf_op jit(solution)/shard_map/ppermute | solution.py:396
  68.4 8.5 %collective-permute-start.20 = (bf16[16,3072]{1,0:T(8,128)(2,1)S(1)}, bf16[16,3072]{1,0:T(8,128)(2,1)S(1)}, u32[]{:S(2)}, u32[]{:S(2)}) collective-permute-start(bf16[16,3072]{1,0:T(8,128)(2,1)S(1)} %get-tuple-element.113), channel_id=1, source_target_pairs={{0,6},{1,7},{2,4},{3,5},{4,2},{5,3},{6,0},{7,1},{8,14},{9,15},{10,... | collective-permute-start | bytes 294920 | tf_op jit(solution)/shard_map/ppermute | solution.py:396
  70.5 8.7 %collective-permute-start.21 = (bf16[192,384]{1,0:T(8,128)(2,1)S(1)}, bf16[192,384]{1,0:T(8,128)(2,1)S(1)}, u32[]{:S(2)}, u32[]{:S(2)}) collective-permute-start(bf16[192,384]{1,0:T(8,128)(2,1)S(1)} %get-tuple-element.116), channel_id=1, source_target_pairs={{0,24},{1,25},{2,26},{3,27},{4,28},{5,29},{6,30},{7,31},{8,16},{9,... | collective-permute-start | bytes 442376 | tf_op jit(solution)/shard_map/ppermute | solution.py:396
  71.8 8.0 %collective-permute-start.22 = (bf16[192,384]{1,0:T(8,128)(2,1)S(1)}, bf16[192,384]{1,0:T(8,128)(2,1)S(1)}, u32[]{:S(2)}, u32[]{:S(2)}) collective-permute-start(bf16[192,384]{1,0:T(8,128)(2,1)S(1)} %get-tuple-element.119), channel_id=1, source_target_pairs={{0,6},{1,7},{2,4},{3,5},{4,2},{5,3},{6,0},{7,1},{8,14},{9,15},{10,... | collective-permute-start | bytes 442376 | tf_op jit(solution)/shard_map/ppermute | solution.py:396
  77.2 6.0 %collective-permute-start.23 = (bf16[32,3072]{1,0:T(8,128)(2,1)S(1)}, bf16[32,3072]{1,0:T(8,128)(2,1)S(1)}, u32[]{:S(2)}, u32[]{:S(2)}) collective-permute-start(bf16[32,3072]{1,0:T(8,128)(2,1)S(1)} %get-tuple-element.123), channel_id=1, source_target_pairs={{0,1},{1,0},{2,3},{3,2},{4,5},{5,4},{6,7},{7,6},{8,9},{9,8},{10,11... | collective-permute-start | bytes 589832 | tf_op jit(solution)/shard_map/ppermute | solution.py:396
  80.4 5.0 %collective-permute-start.24 = (bf16[96,384]{1,0:T(8,128)(2,1)S(1)}, bf16[96,384]{1,0:T(8,128)(2,1)S(1)}, u32[]{:S(2)}, u32[]{:S(2)}) collective-permute-start(bf16[96,384]{1,0:T(8,128)(2,1)S(1)} %get-tuple-element.127), channel_id=1, source_target_pairs={{0,24},{1,25},{2,26},{3,27},{4,28},{5,29},{6,30},{7,31},{8,16},{9,... | collective-permute-start | bytes 221192 | tf_op jit(solution)/shard_map/ppermute | solution.py:396
  86.3 4.3 %collective-permute-start.28 = (f32[24,768]{1,0:T(8,128)S(1)}, f32[24,768]{1,0:T(8,128)S(1)}, u32[]{:S(2)}, u32[]{:S(2)}) collective-permute-start(f32[24,768]{1,0:T(8,128)S(1)} %get-tuple-element.132), channel_id=1, source_target_pairs={{0,10},{1,11},{2,8},{3,9},{4,14},{5,15},{6,12},{7,13},{8,2},{9,3},... | collective-permute-start | bytes 221192 | tf_op jit(solution)/shard_map/ppermute | solution.py:396
  (15 other events, 95.7 us)

commit v4 on v3

--- a/solution.py
+++ b/solution.py
@@ -60,39 +60,25 @@
     return mm(jnp.where((r >> bits) == c, 0.5**bits, 0.0).astype(BF), x.astype(BF), NN)
 
 
-def pyramid_kernel(k, v, l12, l3, rows, sems):
-    copies = []
-    for step in range(STEPS):
-        for i, x in enumerate((k, v)):
-            n = 2 * step + i
-            copies.append(
-                pltpu.make_async_copy(x.at[:, pl.ds(step * W, W)], rows.at[:, pl.ds(n * W, W)], sems.at[n])
-            )
-            copies[-1].start()
-    for part in range(3):
-        c = slice(part * 4 * W, part * 4 * W + 4 * W)
-        for copy in copies[4 * part : 4 * part + 4]:
-            copy.wait()
-        x1 = fold(rows[:, c])
-        x2 = fold(x1)
-        l12[:128, c] = x1
-        l12[128:, c] = x2
-        l3[:, c] = fold(x2)
-
-
-def pyramid(k, v):
-    far = pl.BlockSpec(memory_space=pl.ANY)
-    near = pl.BlockSpec(memory_space=pltpu.VMEM)
-    return pl.pallas_call(
-        pyramid_kernel,
-        in_specs=[far, far],
-        out_specs=[near, near],
-        out_shape=shapes(((192, PAIR), BF), ((32, PAIR), BF)),
-        scratch_shapes=[pltpu.VMEM((T, PAIR), BF), pltpu.SemaphoreType.DMA((2 * STEPS,))],
-        cost_estimate=cost(1.9),
-        compiler_params=params(10),
-        name="pyramid",
-    )(k, v)
+def means_of(x):
+    r = lax.broadcasted_iota(jnp.int32, (224, T), 0)
+    c = lax.broadcasted_iota(jnp.int32, (224, T), 1)
+    low = jnp.where(r < 192, jnp.where((c >> 2) == r - 128, 0.25, 0.0), jnp.where((c >> 3) == r - 192, 0.125, 0.0))
+    means = jnp.where(r < 128, jnp.where((c >> 1) == r, 0.5, 0.0), low).astype(BF)
+    return [mm(means, x[:, n * W : n * W + W], NN).astype(BF) for n in range(STEPS)]
+
+
+def key_means_kernel(k, l12, l3):
+    for n, x in enumerate(means_of(k)):
+        l12[:, n * W : n * W + W] = x[:192]
+        l3[:, n * W : n * W + W] = x[192:]
+
+
+def value_means_kernel(v, l3_k, l12, l3):
+    for n, x in enumerate(means_of(v)):
+        l12[:, n * W : n * W + W] = x[:192]
+        l3[:, 2 * n * W : (2 * n + 1) * W] = l3_k[:, n * W : n * W + W]
+        l3[:, (2 * n + 1) * W : (2 * n + 2) * W] = x[192:]
 
 
 def chip_kernel(mine, other, l4, l5):
@@ -169,7 +155,7 @@
     return pl.ds(pl.multiple_of(n * wide, wide), wide)
 
 
-def attention_kernel(bits, q, k, v, l12, c1, z1, z2, z3, y1, y2, y3, ga, *rest, first):
+def attention_kernel(bits, q, k, v, k12, v12, c1, z1, z2, z3, y1, y2, y3, ga, *rest, first):
     if first:
         att_o, gq_o, fine_o, near_o, far_o, attt_o = rest
     else:
@@ -186,14 +172,15 @@
 
     def step(i, carry):
         wide, pair = lanes(base + i, W), lanes(base + i, 2 * W)
-        qs, ks, vs, gas, ps = q[:, wide], k[:, wide], v[:, wide], ga[:, wide], l12[:, pair]
+        qs, ks, vs, gas = q[:, wide], k[:, wide], v[:, wide], ga[:, wide]
+        kps, vps = k12[:, wide], v12[:, wide]
         x = jnp.concatenate([p[:, pair] for p in (c1, z1, z2, z3, y1, y2, y3)], 0)
         done = []
         for h in range(HS):
             a = slice(h * HD, h * HD + HD)
             b = slice(W + h * HD, W + h * HD + HD)
             done.append(
-                head(qs[:, a], ks[:, a], vs[:, a], ps[:, a], ps[:, b], x[:, a], x[:, b], gas[:, a], bias, expand)
+                head(qs[:, a], ks[:, a], vs[:, a], kps[:, a], vps[:, a], x[:, a], x[:, b], gas[:, a], bias, expand)
             )
         att = jnp.concatenate([d[0] for d in done], 1)
         att_o[:, lanes(i, W)] = att.astype(BF)
@@ -216,13 +203,13 @@
     lax.fori_loop(0, HALF_STEPS, step, 0, unroll=UNROLL)
 
 
-def attention(bits, q, k, v, l12, pieces, ga, *far):
+def attention(bits, q, k, v, k12, v12, pieces, ga, *far):
     first = not far
     outs = [((T, D // 2), BF), ((T, D // 2), BF), ((T, D), F), ((96, D), F)]
     outs += [((64, D), BF)] if first else [((32, PAIR), BF), ((16, PAIR), BF), ((16, PAIR), BF)]
     outs += [((D // 2, T), BF)]
     return placed(
-        lambda *refs: attention_kernel(*refs, first=first), outs, "attention", 7, 32, bits, q, k, v, l12, *pieces, ga, *far
+        lambda *refs: attention_kernel(*refs, first=first), outs, "attention", 7, 32, bits, q, k, v, k12, v12, *pieces, ga, *far
     )
 
 
@@ -292,14 +279,18 @@
         ga[:, c : c + 256] = mm(go[...], w[c : c + 256, :], NT).astype(BF)
 
 
-def mixed_kernel(bits, att_a, att_b, gq_a, gq_b, w, mixed, gq):
+def mixed_kernel(bits, att_a, att_b, w, mixed):
     half = D // 2
     a, b = lanes(1 - bits[XH], half), lanes(bits[XH], half)
-    gq[:, a] = gq_a[...]
-    gq[:, b] = gq_b[...]
     for c in range(0, D, 256):
         cols = slice(c, c + 256)
         mixed[:, cols] = (mm(att_a[...], w[a, cols], NN) + mm(att_b[...], w[b, cols], NN)).astype(BF)
+
+
+def join_kernel(bits, gq_a, gq_b, gq):
+    half = D // 2
+    gq[:, lanes(1 - bits[XH], half)] = gq_a[...]
+    gq[:, lanes(bits[XH], half)] = gq_b[...]
 
 
 def small(kernel, outs, name, us=0.4):
@@ -314,14 +305,15 @@
 
 
 def weight_kernel(bits, *refs, color, bit, outer, half):
-    send, keep = refs[-2:]
-    n = (len(refs) - 2) // 2
-    atts, gos = refs[:n], refs[n : 2 * n]
+    atts, gos, (send, keep, whole) = refs[:4], refs[4:8], refs[8:]
+    c = slice(color * PART, color * PART + PART)
+    for rows in range(0, D // 2, 384):
+        r = slice(rows, rows + 384)
+        whole[r, :] = sum(mm(a[r, :], g[:, c], NN) for a, g in zip(atts, gos, strict=True)).astype(BF)
     away = 1 - bits[bit]
-    c = slice(color * PART, color * PART + PART)
     for out, which in ((send, away), (keep, 1 - away)):
         for to, rows in halves(which, outer, half):
-            out[to, :] = sum(mm(a[rows, :], g[:, c], NN) for a, g in zip(atts, gos, strict=True)).astype(BF)
+            out[to, :] = whole[rows, :]
 
 
 def weight(bits, atts, gos, color, bit, outer, half):
@@ -331,6 +323,7 @@
         in_specs=[pl.BlockSpec(memory_space=pltpu.SMEM)] + [vmem] * (2 * len(atts)),
         out_specs=[vmem, vmem],
         out_shape=shapes(((D // 4, PART), BF), ((D // 4, PART), BF)),
+        scratch_shapes=[pltpu.VMEM((D // 2, PART), BF)],
         cost_estimate=cost(1.5),
         compiler_params=params(10),
         name="weight_part",
@@ -364,11 +357,9 @@
     )(bits, *operands)
 
 
-def last_merge_kernel(bits, a_k, a_r, b_k, b_r, *outs):
+def last_merge_kernel(bits, kept, got, *outs):
     y, z = bits[YL], bits[ZL]
-    total = jnp.concatenate(
-        [a_k[...].astype(F) + a_r[...].astype(F), b_k[...].astype(F) + b_r[...].astype(F)], 1
-    )
+    total = kept[...].astype(F) + got[...].astype(F)
     quarters = [total[24 * i : 24 * i + 24] for i in range(4)]
     for out, dy, dz in zip(outs, (1, 0, 1, 0), (0, 1, 1, 0), strict=True):
         low = [jnp.where((z ^ dz) == 0, quarters[2 * i], quarters[2 * i + 1]) for i in range(2)]
@@ -379,13 +370,20 @@
     vmem = pl.BlockSpec(memory_space=pltpu.VMEM)
     return pl.pallas_call(
         last_merge_kernel,
-        in_specs=[pl.BlockSpec(memory_space=pltpu.SMEM)] + [vmem] * 4,
+        in_specs=[pl.BlockSpec(memory_space=pltpu.SMEM)] + [vmem] * 2,
         out_specs=[vmem] * 4,
         out_shape=shapes(*[((24, D // 2), F)] * 4),
         cost_estimate=cost(0.6),
         compiler_params=params(10),
         name="last_merge",
     )(bits, *operands)
+
+
+def tail_kernel(bits, kept, r1, r2, r3, mine, send):
+    total = (kept[...] + r1[...]) + (r2[...] + r3[...])
+    first = bits[CORE] == 0
+    mine[...] = jnp.where(first, total[:12], total[12:])
+    send[...] = jnp.where(first, total[12:], total[:12])
 
 
 def after(x, *others):
@@ -411,7 +409,8 @@
     bits = jnp.stack(
         [row >> 1, row & 1, place >> 4 & 1, place >> 3 & 1, place >> 2 & 1, place >> 1 & 1, core]
     ).astype(jnp.int32)
-    l12, l3 = pyramid(after(k, bits), v)
+    k12, k3 = small(key_means_kernel, [((192, D), BF), ((32, D), BF)], "key_means")(after(k, bits))
+    v12, l3 = small(value_means_kernel, [((192, D), BF), ((32, PAIR), BF)], "value_means")(v, k3)
     c1 = across(l3, 1)
     l4, l5 = small(chip_kernel, [((32, PAIR), BF), ((16, PAIR), BF)], "chip")(l3, c1)
     z1, z3, z2 = across(l4, 2), across(l5, 6), across(l5, 4)
@@ -423,46 +422,43 @@
     gox_m, gox_o = across_x(go_m, 3), across_x(go_o, 3)
     y1, y3, y2 = across(l6, 8), across(l7, 24), across(l7, 16)
     pieces = (c1, z1, z2, z3, y1, y2, y3)
-    att_a, gq_a, fine_a, near_a, far, sent = attention(bits, after(q, gox_m, gox_o), k, v, l12, pieces, ga)
+    att_a, gq_a, fine_a, near_a, far, sent = attention(bits, after(q, gox_m, gox_o), k, v, k12, v12, pieces, ga)
     att_x = across_x(sent, 3)
     att_b, gq_b, fine_b, near_b, gy1, gy2, gy3, att_m = attention(
-        bits, after(q, sent), k, v, l12, pieces, ga, far
+        bits, after(q, sent), k, v, k12, v12, pieces, ga, far
     )
     att_o, att_xo = across(att_m, 1), across(att_x, 1)
     y1, y3, y2 = across(gy1, 8), across(gy3, 24), across(gy2, 16)
     atts = (att_m, att_o, att_x, att_xo)
     gos = (go_m, go_o, gox_m, gox_o)
-    b_s, b_k = weight(bits, atts, gos, 1, ZH, 8, 48)
+    b_s, b_k = weight(bits, (att_m, *atts[1:]), gos, 1, ZH, 8, 48)
     b_r = across(b_s, 6)
     a_s, a_k = weight(bits, (after(att_m, b_k), *atts[1:]), gos, 0, XL, 1, 384)
     a_r = across_x(a_s, 1)
+    mixed = placed(mixed_kernel, [((T, D), BF)], "mixed", 2.3, 12, bits, after(att_a, a_k), att_b, w_out)[0]
+    b_s, b_k = merge(bits, [(after(b_k, mixed), b_r)], XL, 1, 192)
+    b_r = across_x(b_s, 1)
+    a_s, a_k = merge(bits, [(after(a_k, b_k), a_r)], ZH, 4, 48)
+    a_r = across(a_s, 6)
     s1, s2, s3, own = small(
         back_row_kernel, [((32, PAIR), BF), ((16, PAIR), BF), ((16, PAIR), BF), ((32, PAIR), F)], "back_row"
     )(near_a, after(near_b, a_k), y1, y2, y3)
     z1, z3, z2 = across(s1, 2), across(s3, 6), across(s2, 4)
-    b_s, b_k = merge(bits, [(after(b_k, own), b_r)], YH, 2, 96)
-    b_r = across(b_s, 24)
-    a_s, a_k = merge(bits, [(after(a_k, b_k), a_r)], ZH, 4, 48)
-    a_r = across(a_s, 6)
-    mixed, gq = placed(
-        mixed_kernel, [((T, D), BF)] * 2, "mixed", 2.3, 12, bits, after(att_a, a_k), att_b, gq_a, gq_b, w_out
-    )
+    s, kept = merge(bits, [(after(a_k, own), a_r), (b_k, b_r)], YH, 1, 96)
+    s_r = across(s, 24)
+    gq = placed(join_kernel, [((T, D), BF)], "join", 0.7, 8, bits, after(gq_a, kept), gq_b)[0]
     send, keep = small(back_chip_kernel, [((32, PAIR), BF), ((32, PAIR), F)], "back_chip")(
-        near_a, after(near_b, mixed), own, z1, z2, z3
+        near_a, after(near_b, gq), own, z1, z2, z3
     )
     c1 = across(send, 1)
-    b_s, b_k = merge(bits, [(after(b_k, keep), b_r)], XL, 1, 96)
-    b_r = across_x(b_s, 1)
-    a_s, a_k = merge(bits, [(after(a_k, b_k), a_r)], YH, 1, 96)
-    a_r = across(a_s, 24)
+    s1, s2, s3, kept = last_merge(bits, after(kept, keep), s_r)
+    r1, r2, r3 = across(s1, 8), across(s2, 2), across(s3, 10)
     gk, gv = placed(
-        finish_kernel, [((T, D), BF)] * 2, "finish", 1.7, 12, bits, after(fine_a, a_k), fine_b, keep, c1
+        finish_kernel, [((T, D), BF)] * 2, "finish", 1.7, 12, bits, after(fine_a, kept), fine_b, keep, c1
     )
-    s1, s2, s3, kept = last_merge(bits, after(a_k, gk), a_r, b_k, b_r)
-    part = kept + across(s1, 8) + across(s2, 2) + across(s3, 10)
+    mine, theirs = placed(tail_kernel, [((12, D // 2), F)] * 2, "tail", 0.4, 4, bits, after(kept, gk), r1, r2, r3)
+    theirs = across(theirs, 1)
     first = core == 0
-    mine = jnp.where(first, part[:12], part[12:])
-    theirs = across(jnp.where(first, part[12:], part[:12]), 1)
     total = jnp.concatenate([jnp.where(first, mine, theirs), jnp.where(first, theirs, mine)], 1)
     gw = total * (1.0 / math.sqrt(4 * 32 * T))
     return mixed[None], gq[None], gk[None], gv[None], gw

time: 95.6 us -> 91 us (0.952)
  waiting for transfers between devices: 17.3 us -> 11.2 us
  starting transfers between devices: 44.1 us -> 46.4 us
    ppermute x25 -> x24, waiting for transfers between devices: 17.3 us -> 10.6 us  [across(): return lax.ppermute(x, 'seq', [(i, i ^ flip) for i in range(32)])]
    ppermute x25 -> x24, starting transfers between devices: 37.3 us -> 39.9 us  [across(): return lax.ppermute(x, 'seq', [(i, i ^ flip) for i in range(32)])]
    pallas_call x4 -> x6, Pallas kernels: 15.4 us -> 17.2 us  [placed(): pl.pallas_call(kernel, in_specs=[pl.BlockSpec(memory_space=pltpu.SMEM)] +...]
    pallas_call x1 -> x2, Pallas kernels: 1.85 us -> 0.68 us  [the longest x1 0.34 us: local(): small(key_means_kernel, [((192, D), BF), ((32, D), BF)], 'key_means')]
    pallas_call x4 -> x3, Pallas kernels: 2.42 us -> 1.87 us  [merge(): pl.pallas_call(lambda *refs: merge_kernel(*refs, bit=bit, outer=outer, ha...]
  transfers between devices with their start and end apart: 30 -> 29, of which waited for: 10 -> 8; matrix products, arithmetic and copies ran while one was open for 0% -> 0% of each run, Pallas kernels for 21% -> 20%
where the time goes in v4:
time: 91 us; the launch traced here: 90.8 us
  starting transfers between devices  46.4 us (51%)
  Pallas kernels  27 us (30%)
  waiting for transfers between devices  11.2 us (12%)
  local copies, waits for them, and re-layouts  4.71 us (5%)
    ppermute x24, starting transfers between devices, across(): return lax.ppermute(x, 'seq', [(i, i ^ flip) for i in range(32)])  39.9 us
    pallas_call x6, Pallas kernels, placed(): pl.pallas_call(kernel, in_specs=[pl.BlockSpec(memory_space=pltpu.SMEM)] +...  17.2 us
    ppermute x24, waiting for transfers between devices, across(): return lax.ppermute(x, 'seq', [(i, i ^ flip) for i in range(32)])  10.6 us
    ppermute x5, starting transfers between devices, across_x(): return lax.ppermute(x, 'dp', [(i, i ^ flip) for i in range(4)])  6.48 us
    unnamed x18, local copies, waits for them, and re-layouts  4.63 us
    pallas_call x2, Pallas kernels, weight(): pl.pallas_call(lambda *refs: weight_kernel(*refs, color=color, bit=bit, o...  3.14 us
    pallas_call x3, Pallas kernels, merge(): pl.pallas_call(lambda *refs: merge_kernel(*refs, bit=bit, outer=outer, ha...  1.87 us
  transfers between devices with their start and end apart: 29, of which 8 were waited for; matrix products, arithmetic and copies ran while one was open for 0% of the time, Pallas kernels for 20%

profile of v4, /device:TPU:1, one launch (start us, length us, event | category | flops | bytes accessed | tf_op | source)
XLA Modules:
  0.0 90.8 jit_solution(13706976340298248132)
XLA Ops:
  4.3 1.5 %collective-permute-start.1 = (bf16[256,768]{1,0:T(8,128)(2,1)S(1)}, bf16[256,768]{1,0:T(8,128)(2,1)S(1)}, u32[]{:S(2)}, u32[]{:S(2)}) collective-permute-start(bf16[256,768]{1,0:T(8,128)(2,1)S(1)} %get-tuple-element.75), channel_id=1, source_target_pairs={{0,1},{1,0},{2,3},{3,2},{4,5},{5,4},{6,7},{7,6},{8,9},{9,8},{10,11... | collective-permute-start | bytes 1179656 | tf_op jit(solution)/shard_map/ppermute | solution.py:394
  5.9 2.6 %collective-permute-start = (bf16[256,768]{1,0:T(8,128)(2,1)S(1)}, bf16[256,768]{1,0:T(8,128)(2,1)S(1)}, u32[]{:S(2)}, u32[]{:S(2)}) collective-permute-start(bf16[256,768]{1,0:T(8,128)(2,1)S(1)} %get-tuple-element.74.refs_5_), channel_id=1, source_target_pairs={{0,96},{32,64},{64,32},{96,0},{1,97},{33,65},{65,33},{97,1},{2,98}... | collective-permute-start | bytes 1179656 | tf_op jit(solution)/shard_map/ppermute | solution.py:398
  10.0 1.7 %collective-permute-start.4 = (bf16[32,3072]{1,0:T(8,128)(2,1)S(1)}, bf16[32,3072]{1,0:T(8,128)(2,1)S(1)}, u32[]{:S(2)}, u32[]{:S(2)}) collective-permute-start(bf16[32,3072]{1,0:T(8,128)(2,1)S(1)} %get-tuple-element.79), channel_id=1, source_target_pairs={{0,2},{1,3},{2,0},{3,1},{4,6},{5,7},{6,4},{7,5},{8,10},{9,11},{10,... | collective-permute-start | bytes 589832 | tf_op jit(solution)/shard_map/ppermute | solution.py:394
  11.7 3.3 %collective-permute-start.5 = (bf16[16,3072]{1,0:T(8,128)(2,1)S(1)}, bf16[16,3072]{1,0:T(8,128)(2,1)S(1)}, u32[]{:S(2)}, u32[]{:S(2)}) collective-permute-start(bf16[16,3072]{1,0:T(8,128)(2,1)S(1)} %get-tuple-element.81.l5), channel_id=1, source_target_pairs={{0,4},{1,5},{2,6},{3,7},{4,0},{5,1},{6,2},{7,3},{8,12},{9,13},{10,... | collective-permute-start | bytes 294920 | tf_op jit(solution)/shard_map/ppermute | solution.py:394
  15.1 6.1 %collective-permute-done.5.z2.refs_8_ = bf16[16,3072]{1,0:T(8,128)(2,1)S(1)} collective-permute-done((bf16[16,3072]{1,0:T(8,128)(2,1)S(1)}, bf16[16,3072]{1,0:T(8,128)(2,1)S(1)}, u32[]{:S(2)}, u32[]{:S(2)}) %collective-permute-start.5) | collective-permute-done | bytes 98336 | tf_op jit(solution)/shard_map/ppermute | solution.py:394
  23.0 2.6 %collective-permute-start.8 = (bf16[16,3072]{1,0:T(8,128)(2,1)S(1)}, bf16[16,3072]{1,0:T(8,128)(2,1)S(1)}, u32[]{:S(2)}, u32[]{:S(2)}) collective-permute-start(bf16[16,3072]{1,0:T(8,128)(2,1)S(1)} %get-tuple-element.83), channel_id=1, source_target_pairs={{0,16},{1,17},{2,18},{3,19},{4,20},{5,21},{6,22},{7,23},{8,24},{9,... | collective-permute-start | bytes 294920 | tf_op jit(solution)/shard_map/ppermute | solution.py:394
  25.6 2.3 %copy-done = bf16[1536,1536]{1,0:T(8,128)(2,1)S(1)} copy-done((bf16[1536,1536]{1,0:T(8,128)(2,1)S(1)}, bf16[1536,1536]{1,0:T(8,128)(2,1)}, u32[]{:S(2)}) %copy-start) | copy-done | bytes 4718616
  30.8 5.1 %attention.2 = (bf16[256,768]{1,0:T(8,128)(2,1)S(1)}, bf16[256,768]{1,0:T(8,128)(2,1)S(1)}, f32[256,1536]{1,0:T(8,128)S(1)}, f32[96,1536]{1,0:T(8,128)S(1)}, bf1...) custom-call(s32[7]{0:T(128)S(1)} %stack.31.bits.refs_0_, bf16[256,1536]{1,0:T(8,128)(2,1)S(1)} %bitcast.25, ...), custom_call_target="tpu_custom_call" | custom-call | bytes 25900000 | tf_op jit(solution)/shard_map/attention/pallas_call | solution.py:218
  35.9 1.5 %collective-permute-start.11 = (bf16[768,256]{1,0:T(8,128)(2,1)S(1)}, bf16[768,256]{1,0:T(8,128)(2,1)S(1)}, u32[]{:S(2)}, u32[]{:S(2)}) collective-permute-start(bf16[768,256]{1,0:T(8,128)(2,1)S(1)} %get-tuple-element.86), channel_id=1, source_target_pairs={{0,96},{32,64},{64,32},{96,0},{1,97},{33,65},{65,33},{97,1},{2,98}... | collective-permute-start | bytes 1179656 | tf_op jit(solution)/shard_map/ppermute | solution.py:398
  37.4 5.1 %attention.3 = (bf16[256,768]{1,0:T(8,128)(2,1)S(1)}, bf16[256,768]{1,0:T(8,128)(2,1)S(1)}, f32[256,1536]{1,0:T(8,128)S(1)}, f32[96,1536]{1,0:T(8,128)S(1)}, bf1...) custom-call(s32[7]{0:T(128)S(1)} %stack.31.bits.refs_0_, ...), custom_call_target="tpu_custom_call" | custom-call | bytes 25900000 | tf_op jit(solution)/shard_map/attention/pallas_call | solution.py:218
  42.5 4.2 %collective-permute-start.10 = (bf16[768,256]{1,0:T(8,128)(2,1)S(1)}, bf16[768,256]{1,0:T(8,128)(2,1)S(1)}, u32[]{:S(2)}, u32[]{:S(2)}) collective-permute-start(bf16[768,256]{1,0:T(8,128)(2,1)S(1)} %get-tuple-element.91.refs_1_), channel_id=1, source_target_pairs={{0,1},{1,0},{2,3},{3,2},{4,5},{5,4},{6,7},{7,6},{8,9},{9,8},{10,11... | collective-permute-start | bytes 1179656 | tf_op jit(solution)/shard_map/ppermute | solution.py:394
  46.7 2.3 %collective-permute-start.12 = (bf16[768,256]{1,0:T(8,128)(2,1)S(1)}, bf16[768,256]{1,0:T(8,128)(2,1)S(1)}, u32[]{:S(2)}, u32[]{:S(2)}) collective-permute-start(bf16[768,256]{1,0:T(8,128)(2,1)S(1)} %collective-permute-done.11.refs_3_), channel_id=1, source_target_pairs={{0,1},{1,0},{2,3},{3,2},{4,5},{5,4},{6,7},{7,6},{8,9},{9,8},{10,11... | collective-permute-start | bytes 1179656 | tf_op jit(solution)/shard_map/ppermute | solution.py:394
  50.3 1.6 %weight_part.2 = (bf16[384,384]{1,0:T(8,128)(2,1)S(1)}, bf16[384,384]{1,0:T(8,128)(2,1)S(1)}) custom-call(s32[7]{0:T(128)S(1)} %stack.31.bits.refs_0_, bf16[768,256]{1,0:T(8,128)(2,1)S(1)} %get-tuple-element.91.refs_1_, bf16[768,256]{1,0:T(8,128)(2,1)S(1)} %collective-permute-done.10.refs_2_, bf16[768,256]{1,0:T(8,128)(2,1)S(1)} %collective-permute-done.11.refs_3_, ...), custom_call_target="tpu_custom_call" | custom-call | bytes 5550000 | tf_op jit(solution)/shard_map/weight_part/pallas_call | solution.py:321
  51.9 1.6 %collective-permute-start.13 = (bf16[384,384]{1,0:T(8,128)(2,1)S(1)}, bf16[384,384]{1,0:T(8,128)(2,1)S(1)}, u32[]{:S(2)}, u32[]{:S(2)}) collective-permute-start(bf16[384,384]{1,0:T(8,128)(2,1)S(1)} %get-tuple-element.97), channel_id=1, source_target_pairs={{0,6},{1,7},{2,4},{3,5},{4,2},{5,3},{6,0},{7,1},{8,14},{9,15},{10,... | collective-permute-start | bytes 884744 | tf_op jit(solution)/shard_map/ppermute | solution.py:394
  53.5 1.6 %weight_part.3 = (bf16[384,384]{1,0:T(8,128)(2,1)S(1)}, bf16[384,384]{1,0:T(8,128)(2,1)S(1)}) custom-call(s32[7]{0:T(128)S(1)} %stack.31.bits.refs_0_, bf16[768,256]{1,0:T(8,128)(2,1)S(1)} %get-tuple-element.91.refs_1_, bf16[768,256]{1,0:T(8,128)(2,1)S(1)} %collective-permute-done.10.refs_2_, bf16[768,256]{1,0:T(8,128)(2,1)S(1)} %collective-permute-done.11.refs_3_, ...), custom_call_target="tpu_custom_call" | custom-call | bytes 5550000 | tf_op jit(solution)/shard_map/weight_part/pallas_call | solution.py:321
  55.3 2.1 %collective-permute-start.16 = (bf16[16,3072]{1,0:T(8,128)(2,1)S(1)}, bf16[16,3072]{1,0:T(8,128)(2,1)S(1)}, u32[]{:S(2)}, u32[]{:S(2)}) collective-permute-start(bf16[16,3072]{1,0:T(8,128)(2,1)S(1)} %get-tuple-element.106), channel_id=1, source_target_pairs={{0,16},{1,17},{2,18},{3,19},{4,20},{5,21},{6,22},{7,23},{8,24},{9,... | collective-permute-start | bytes 294920 | tf_op jit(solution)/shard_map/ppermute | solution.py:394
  57.3 1.8 %collective-permute-start.17 = (bf16[16,3072]{1,0:T(8,128)(2,1)S(1)}, bf16[16,3072]{1,0:T(8,128)(2,1)S(1)}, u32[]{:S(2)}, u32[]{:S(2)}) collective-permute-start(bf16[16,3072]{1,0:T(8,128)(2,1)S(1)} %get-tuple-element.107), channel_id=1, source_target_pairs={{0,24},{1,25},{2,26},{3,27},{4,28},{5,29},{6,30},{7,31},{8,16},{9,... | collective-permute-start | bytes 294920 | tf_op jit(solution)/shard_map/ppermute | solution.py:394
  59.1 2.8 %mixed.1 = bf16[256,1536]{1,0:T(8,128)(2,1)} custom-call(s32[7]{0:T(128)S(1)} %stack.31.bits.refs_0_, bf16[256,768]{1,0:T(8,128)(2,1)S(1)} %get-tuple-element.93.att_a, bf16[256,768]{1,0:T(8,128)(2,1)S(1)} %get-tuple-element.94.att_b, bf16[1536,1536]{1,0:T(8,128)(2,1)S(1)} %bitcast.16), custom_call_target="tpu_custom_call" | custom-call | bytes 8510000 | tf_op jit(solution)/shard_map/mixed/pallas_call | solution.py:218
  66.7 1.6 %collective-permute-start.21 = (bf16[16,3072]{1,0:T(8,128)(2,1)S(1)}, bf16[16,3072]{1,0:T(8,128)(2,1)S(1)}, u32[]{:S(2)}, u32[]{:S(2)}) collective-permute-start(bf16[16,3072]{1,0:T(8,128)(2,1)S(1)} %get-tuple-element.118), channel_id=1, source_target_pairs={{0,4},{1,5},{2,6},{3,7},{4,0},{5,1},{6,2},{7,3},{8,12},{9,13},{10,... | collective-permute-start | bytes 294920 | tf_op jit(solution)/shard_map/ppermute | solution.py:394
  68.4 1.5 %collective-permute-start.22 = (bf16[16,3072]{1,0:T(8,128)(2,1)S(1)}, bf16[16,3072]{1,0:T(8,128)(2,1)S(1)}, u32[]{:S(2)}, u32[]{:S(2)}) collective-permute-start(bf16[16,3072]{1,0:T(8,128)(2,1)S(1)} %get-tuple-element.119), channel_id=1, source_target_pairs={{0,6},{1,7},{2,4},{3,5},{4,2},{5,3},{6,0},{7,1},{8,14},{9,15},{10,... | collective-permute-start | bytes 294920 | tf_op jit(solution)/shard_map/ppermute | solution.py:394
  74.6 4.6 %collective-permute-start.24 = (bf16[32,3072]{1,0:T(8,128)(2,1)S(1)}, bf16[32,3072]{1,0:T(8,128)(2,1)S(1)}, u32[]{:S(2)}, u32[]{:S(2)}) collective-permute-start(bf16[32,3072]{1,0:T(8,128)(2,1)S(1)} %get-tuple-element.126), channel_id=1, source_target_pairs={{0,1},{1,0},{2,3},{3,2},{4,5},{5,4},{6,7},{7,6},{8,9},{9,8},{10,11... | collective-permute-start | bytes 589832 | tf_op jit(solution)/shard_map/ppermute | solution.py:394
  80.7 1.9 %collective-permute-start.27 = (f32[24,768]{1,0:T(8,128)S(1)}, f32[24,768]{1,0:T(8,128)S(1)}, u32[]{:S(2)}, u32[]{:S(2)}) collective-permute-start(f32[24,768]{1,0:T(8,128)S(1)} %get-tuple-element.132), channel_id=1, source_target_pairs={{0,10},{1,11},{2,8},{3,9},{4,14},{5,15},{6,12},{7,13},{8,2},{9,3},... | collective-permute-start | bytes 221192 | tf_op jit(solution)/shard_map/ppermute | solution.py:394
  82.6 2.2 %finish.1 = (bf16[256,1536]{1,0:T(8,128)(2,1)}, bf16[256,1536]{1,0:T(8,128)(2,1)}) custom-call(s32[7]{0:T(128)S(1)} %stack.31.bits.refs_0_, f32[256,1536]{1,0:T(8,128)S(1)} %get-tuple-element.124.fine_a, f32[256,1536]{1,0:T(8,128)S(1)} %get-tuple-element.125.fine_b, f32[32,3072]{1,0:T(8,128)S(1)} %get-tuple-element.120.keep, ...), custom_call_target="tpu_custom_call" | custom-call | bytes 6290000 | tf_op jit(solution)/shard_map/finish/pallas_call | solution.py:218
  85.4 3.9 %collective-permute-start.28 = (f32[12,768]{1,0:T(8,128)S(1)}, f32[12,768]{1,0:T(8,128)S(1)}, u32[]{:S(2)}, u32[]{:S(2)}) collective-permute-start(f32[12,768]{1,0:T(8,128)S(1)} %get-tuple-element.134), channel_id=1, source_target_pairs={{0,1},{1,0},{2,3},{3,2},{4,5},{5,4},{6,7},{7,6},{8,9},{9,8},{10,11... | collective-permute-start | bytes 110600 | tf_op jit(solution)/shard_map/ppermute | solution.py:394
  (76 shorter events, 24.4 us)
Async XLA Ops:
  5.9 23.5 %collective-permute-start = (bf16[256,768]{1,0:T(8,128)(2,1)S(1)}, bf16[256,768]{1,0:T(8,128)(2,1)S(1)}, u32[]{:S(2)}, u32[]{:S(2)}) collective-permute-start(bf16[256,768]{1,0:T(8,128)(2,1)S(1)} %get-tuple-element.74.refs_5_), channel_id=1, source_target_pairs={{0,96},{32,64},{64,32},{96,0},{1,97},{33,65},{65,33},{97,1},{2,98}... | collective-permute-start | bytes 1179656 | tf_op jit(solution)/shard_map/ppermute | solution.py:398
  8.5 20.9 %collective-permute-start.2 = (bf16[256,768]{1,0:T(8,128)(2,1)S(1)}, bf16[256,768]{1,0:T(8,128)(2,1)S(1)}, u32[]{:S(2)}, u32[]{:S(2)}) collective-permute-start(bf16[256,768]{1,0:T(8,128)(2,1)S(1)} %collective-permute-done.1.refs_6_), channel_id=1, source_target_pairs={{0,96},{32,64},{64,32},{96,0},{1,97},{33,65},{65,33},{97,1},{2,98}... | collective-permute-start | bytes 1179656 | tf_op jit(solution)/shard_map/ppermute | solution.py:398
  10.0 11.2 %collective-permute-start.4 = (bf16[32,3072]{1,0:T(8,128)(2,1)S(1)}, bf16[32,3072]{1,0:T(8,128)(2,1)S(1)}, u32[]{:S(2)}, u32[]{:S(2)}) collective-permute-start(bf16[32,3072]{1,0:T(8,128)(2,1)S(1)} %get-tuple-element.79), channel_id=1, source_target_pairs={{0,2},{1,3},{2,0},{3,1},{4,6},{5,7},{6,4},{7,5},{8,10},{9,11},{10,... | collective-permute-start | bytes 589832 | tf_op jit(solution)/shard_map/ppermute | solution.py:394
  11.7 9.4 %collective-permute-start.5 = (bf16[16,3072]{1,0:T(8,128)(2,1)S(1)}, bf16[16,3072]{1,0:T(8,128)(2,1)S(1)}, u32[]{:S(2)}, u32[]{:S(2)}) collective-permute-start(bf16[16,3072]{1,0:T(8,128)(2,1)S(1)} %get-tuple-element.81.l5), channel_id=1, source_target_pairs={{0,4},{1,5},{2,6},{3,7},{4,0},{5,1},{6,2},{7,3},{8,12},{9,13},{10,... | collective-permute-start | bytes 294920 | tf_op jit(solution)/shard_map/ppermute | solution.py:394
  15.0 6.1 %collective-permute-start.6 = (bf16[16,3072]{1,0:T(8,128)(2,1)S(1)}, bf16[16,3072]{1,0:T(8,128)(2,1)S(1)}, u32[]{:S(2)}, u32[]{:S(2)}) collective-permute-start(bf16[16,3072]{1,0:T(8,128)(2,1)S(1)} %get-tuple-element.81.l5), channel_id=1, source_target_pairs={{0,6},{1,7},{2,4},{3,5},{4,2},{5,3},{6,0},{7,1},{8,14},{9,15},{10,... | collective-permute-start | bytes 294920 | tf_op jit(solution)/shard_map/ppermute | solution.py:394
  21.6 9.2 %collective-permute-start.7 = (bf16[32,3072]{1,0:T(8,128)(2,1)S(1)}, bf16[32,3072]{1,0:T(8,128)(2,1)S(1)}, u32[]{:S(2)}, u32[]{:S(2)}) collective-permute-start(bf16[32,3072]{1,0:T(8,128)(2,1)S(1)} %get-tuple-element.82), channel_id=1, source_target_pairs={{0,8},{1,9},{2,10},{3,11},{4,12},{5,13},{6,14},{7,15},{8,0},{9,1},... | collective-permute-start | bytes 589832 | tf_op jit(solution)/shard_map/ppermute | solution.py:394
  23.0 7.0 %collective-permute-start.8 = (bf16[16,3072]{1,0:T(8,128)(2,1)S(1)}, bf16[16,3072]{1,0:T(8,128)(2,1)S(1)}, u32[]{:S(2)}, u32[]{:S(2)}) collective-permute-start(bf16[16,3072]{1,0:T(8,128)(2,1)S(1)} %get-tuple-element.83), channel_id=1, source_target_pairs={{0,16},{1,17},{2,18},{3,19},{4,20},{5,21},{6,22},{7,23},{8,24},{9,... | collective-permute-start | bytes 294920 | tf_op jit(solution)/shard_map/ppermute | solution.py:394
  25.6 5.2 %collective-permute-start.9 = (bf16[16,3072]{1,0:T(8,128)(2,1)S(1)}, bf16[16,3072]{1,0:T(8,128)(2,1)S(1)}, u32[]{:S(2)}, u32[]{:S(2)}) collective-permute-start(bf16[16,3072]{1,0:T(8,128)(2,1)S(1)} %get-tuple-element.83), channel_id=1, source_target_pairs={{0,24},{1,25},{2,26},{3,27},{4,28},{5,29},{6,30},{7,31},{8,16},{9,... | collective-permute-start | bytes 294920 | tf_op jit(solution)/shard_map/ppermute | solution.py:394
  35.9 10.8 %collective-permute-start.11 = (bf16[768,256]{1,0:T(8,128)(2,1)S(1)}, bf16[768,256]{1,0:T(8,128)(2,1)S(1)}, u32[]{:S(2)}, u32[]{:S(2)}) collective-permute-start(bf16[768,256]{1,0:T(8,128)(2,1)S(1)} %get-tuple-element.86), channel_id=1, source_target_pairs={{0,96},{32,64},{64,32},{96,0},{1,97},{33,65},{65,33},{97,1},{2,98}... | collective-permute-start | bytes 1179656 | tf_op jit(solution)/shard_map/ppermute | solution.py:398
  42.5 6.5 %collective-permute-start.10 = (bf16[768,256]{1,0:T(8,128)(2,1)S(1)}, bf16[768,256]{1,0:T(8,128)(2,1)S(1)}, u32[]{:S(2)}, u32[]{:S(2)}) collective-permute-start(bf16[768,256]{1,0:T(8,128)(2,1)S(1)} %get-tuple-element.91.refs_1_), channel_id=1, source_target_pairs={{0,1},{1,0},{2,3},{3,2},{4,5},{5,4},{6,7},{7,6},{8,9},{9,8},{10,11... | collective-permute-start | bytes 1179656 | tf_op jit(solution)/shard_map/ppermute | solution.py:394
  51.9 10.0 %collective-permute-start.13 = (bf16[384,384]{1,0:T(8,128)(2,1)S(1)}, bf16[384,384]{1,0:T(8,128)(2,1)S(1)}, u32[]{:S(2)}, u32[]{:S(2)}) collective-permute-start(bf16[384,384]{1,0:T(8,128)(2,1)S(1)} %get-tuple-element.97), channel_id=1, source_target_pairs={{0,6},{1,7},{2,4},{3,5},{4,2},{5,3},{6,0},{7,1},{8,14},{9,15},{10,... | collective-permute-start | bytes 884744 | tf_op jit(solution)/shard_map/ppermute | solution.py:394
  55.1 8.0 %collective-permute-start.14 = (bf16[384,384]{1,0:T(8,128)(2,1)S(1)}, bf16[384,384]{1,0:T(8,128)(2,1)S(1)}, u32[]{:S(2)}, u32[]{:S(2)}) collective-permute-start(bf16[384,384]{1,0:T(8,128)(2,1)S(1)} %get-tuple-element.100), channel_id=1, source_target_pairs={{0,32},{32,0},{64,96},{96,64},{1,33},{33,1},{65,97},{97,65},{2,34}... | collective-permute-start | bytes 884744 | tf_op jit(solution)/shard_map/ppermute | solution.py:398
  55.2 8.5 %collective-permute-start.15 = (bf16[32,3072]{1,0:T(8,128)(2,1)S(1)}, bf16[32,3072]{1,0:T(8,128)(2,1)S(1)}, u32[]{:S(2)}, u32[]{:S(2)}) collective-permute-start(bf16[32,3072]{1,0:T(8,128)(2,1)S(1)} %get-tuple-element.105), channel_id=1, source_target_pairs={{0,8},{1,9},{2,10},{3,11},{4,12},{5,13},{6,14},{7,15},{8,0},{9,1},... | collective-permute-start | bytes 589832 | tf_op jit(solution)/shard_map/ppermute | solution.py:394
  55.3 8.4 %collective-permute-start.16 = (bf16[16,3072]{1,0:T(8,128)(2,1)S(1)}, bf16[16,3072]{1,0:T(8,128)(2,1)S(1)}, u32[]{:S(2)}, u32[]{:S(2)}) collective-permute-start(bf16[16,3072]{1,0:T(8,128)(2,1)S(1)} %get-tuple-element.106), channel_id=1, source_target_pairs={{0,16},{1,17},{2,18},{3,19},{4,20},{5,21},{6,22},{7,23},{8,24},{9,... | collective-permute-start | bytes 294920 | tf_op jit(solution)/shard_map/ppermute | solution.py:394
  57.3 6.4 %collective-permute-start.17 = (bf16[16,3072]{1,0:T(8,128)(2,1)S(1)}, bf16[16,3072]{1,0:T(8,128)(2,1)S(1)}, u32[]{:S(2)}, u32[]{:S(2)}) collective-permute-start(bf16[16,3072]{1,0:T(8,128)(2,1)S(1)} %get-tuple-element.107), channel_id=1, source_target_pairs={{0,24},{1,25},{2,26},{3,27},{4,28},{5,29},{6,30},{7,31},{8,16},{9,... | collective-permute-start | bytes 294920 | tf_op jit(solution)/shard_map/ppermute | solution.py:394
  64.1 10.1 %collective-permute-start.20 = (bf16[32,3072]{1,0:T(8,128)(2,1)S(1)}, bf16[32,3072]{1,0:T(8,128)(2,1)S(1)}, u32[]{:S(2)}, u32[]{:S(2)}) collective-permute-start(bf16[32,3072]{1,0:T(8,128)(2,1)S(1)} %get-tuple-element.117), channel_id=1, source_target_pairs={{0,2},{1,3},{2,0},{3,1},{4,6},{5,7},{6,4},{7,5},{8,10},{9,11},{10,... | collective-permute-start | bytes 589832 | tf_op jit(solution)/shard_map/ppermute | solution.py:394
  64.2 5.7 %collective-permute-start.18 = (bf16[192,384]{1,0:T(8,128)(2,1)S(1)}, bf16[192,384]{1,0:T(8,128)(2,1)S(1)}, u32[]{:S(2)}, u32[]{:S(2)}) collective-permute-start(bf16[192,384]{1,0:T(8,128)(2,1)S(1)} %get-tuple-element.110), channel_id=1, source_target_pairs={{0,6},{1,7},{2,4},{3,5},{4,2},{5,3},{6,0},{7,1},{8,14},{9,15},{10,... | collective-permute-start | bytes 442376 | tf_op jit(solution)/shard_map/ppermute | solution.py:394
  66.7 6.7 %collective-permute-start.21 = (bf16[16,3072]{1,0:T(8,128)(2,1)S(1)}, bf16[16,3072]{1,0:T(8,128)(2,1)S(1)}, u32[]{:S(2)}, u32[]{:S(2)}) collective-permute-start(bf16[16,3072]{1,0:T(8,128)(2,1)S(1)} %get-tuple-element.118), channel_id=1, source_target_pairs={{0,4},{1,5},{2,6},{3,7},{4,0},{5,1},{6,2},{7,3},{8,12},{9,13},{10,... | collective-permute-start | bytes 294920 | tf_op jit(solution)/shard_map/ppermute | solution.py:394
  68.4 5.9 %collective-permute-start.22 = (bf16[16,3072]{1,0:T(8,128)(2,1)S(1)}, bf16[16,3072]{1,0:T(8,128)(2,1)S(1)}, u32[]{:S(2)}, u32[]{:S(2)}) collective-permute-start(bf16[16,3072]{1,0:T(8,128)(2,1)S(1)} %get-tuple-element.119), channel_id=1, source_target_pairs={{0,6},{1,7},{2,4},{3,5},{4,2},{5,3},{6,0},{7,1},{8,14},{9,15},{10,... | collective-permute-start | bytes 294920 | tf_op jit(solution)/shard_map/ppermute | solution.py:394
  70.6 8.7 %collective-permute-start.23 = (bf16[96,768]{1,0:T(8,128)(2,1)S(1)}, bf16[96,768]{1,0:T(8,128)(2,1)S(1)}, u32[]{:S(2)}, u32[]{:S(2)}) collective-permute-start(bf16[96,768]{1,0:T(8,128)(2,1)S(1)} %get-tuple-element.122), channel_id=1, source_target_pairs={{0,24},{1,25},{2,26},{3,27},{4,28},{5,29},{6,30},{7,31},{8,16},{9,... | collective-permute-start | bytes 442376 | tf_op jit(solution)/shard_map/ppermute | solution.py:394
  74.6 8.0 %collective-permute-start.24 = (bf16[32,3072]{1,0:T(8,128)(2,1)S(1)}, bf16[32,3072]{1,0:T(8,128)(2,1)S(1)}, u32[]{:S(2)}, u32[]{:S(2)}) collective-permute-start(bf16[32,3072]{1,0:T(8,128)(2,1)S(1)} %get-tuple-element.126), channel_id=1, source_target_pairs={{0,1},{1,0},{2,3},{3,2},{4,5},{5,4},{6,7},{7,6},{8,9},{9,8},{10,11... | collective-permute-start | bytes 589832 | tf_op jit(solution)/shard_map/ppermute | solution.py:394
  79.9 5.0 %collective-permute-start.25 = (f32[24,768]{1,0:T(8,128)S(1)}, f32[24,768]{1,0:T(8,128)S(1)}, u32[]{:S(2)}, u32[]{:S(2)}) collective-permute-start(f32[24,768]{1,0:T(8,128)S(1)} %get-tuple-element.130), channel_id=1, source_target_pairs={{0,8},{1,9},{2,10},{3,11},{4,12},{5,13},{6,14},{7,15},{8,0},{9,1},... | collective-permute-start | bytes 221192 | tf_op jit(solution)/shard_map/ppermute | solution.py:394
  80.0 4.9 %collective-permute-start.26 = (f32[24,768]{1,0:T(8,128)S(1)}, f32[24,768]{1,0:T(8,128)S(1)}, u32[]{:S(2)}, u32[]{:S(2)}) collective-permute-start(f32[24,768]{1,0:T(8,128)S(1)} %get-tuple-element.131), channel_id=1, source_target_pairs={{0,2},{1,3},{2,0},{3,1},{4,6},{5,7},{6,4},{7,5},{8,10},{9,11},{10,... | collective-permute-start | bytes 221192 | tf_op jit(solution)/shard_map/ppermute | solution.py:394
  85.4 4.7 %collective-permute-start.28 = (f32[12,768]{1,0:T(8,128)S(1)}, f32[12,768]{1,0:T(8,128)S(1)}, u32[]{:S(2)}, u32[]{:S(2)}) collective-permute-start(f32[12,768]{1,0:T(8,128)S(1)} %get-tuple-element.134), channel_id=1, source_target_pairs={{0,1},{1,0},{2,3},{3,2},{4,5},{5,4},{6,7},{7,6},{8,9},{9,8},{10,11... | collective-permute-start | bytes 110600 | tf_op jit(solution)/shard_map/ppermute | solution.py:394
  (14 other events, 85.1 us)

commit v5 on v4

--- a/solution.py
+++ b/solution.py
@@ -25,6 +25,16 @@
 SCALE = HD**-0.5
 PART = D // 4
 PAIR = 2 * D
+
+
+XH, XL, YH, YL, ZH, ZL, CORE = range(7)
+
+
+class Bits:
+    def __getitem__(self, n):
+        if n in (XH, XL):
+            return lax.axis_index("dp") >> (1 - n) & 1
+        return lax.axis_index("seq") >> (CORE - n) & 1
 
 
 def mm(a, b, dims):
@@ -216,14 +226,14 @@
 def placed(kernel, outs, name, us, mib, bits, *operands):
     vmem = pl.BlockSpec(memory_space=pltpu.VMEM)
     return pl.pallas_call(
-        kernel,
-        in_specs=[pl.BlockSpec(memory_space=pltpu.SMEM)] + [vmem] * len(operands),
+        lambda *refs: kernel(bits, *refs),
+        in_specs=[vmem] * len(operands),
         out_specs=[vmem] * len(outs),
         out_shape=shapes(*outs),
         cost_estimate=cost(us),
         compiler_params=params(mib),
         name=name,
-    )(bits, *operands)
+    )(*operands)
 
 
 def back_row_kernel(near_a, near_b, y1, y2, y3, s1, s2, s3, own):
@@ -264,14 +274,14 @@
 def split(bits, go):
     vmem = pl.BlockSpec(memory_space=pltpu.VMEM)
     return pl.pallas_call(
-        split_kernel,
-        in_specs=[pl.BlockSpec(memory_space=pltpu.SMEM), vmem],
+        lambda *refs: split_kernel(bits, *refs),
+        in_specs=[vmem],
         out_specs=[vmem] * 2,
         out_shape=shapes(*[((T, D // 2), BF)] * 2),
         cost_estimate=cost(0.3),
         compiler_params=params(10),
         name="split",
-    )(bits, go)
+    )(go)
 
 
 def grad_attended_kernel(go, w, ga):
@@ -319,15 +329,15 @@
 def weight(bits, atts, gos, color, bit, outer, half):
     vmem = pl.BlockSpec(memory_space=pltpu.VMEM)
     return pl.pallas_call(
-        lambda *refs: weight_kernel(*refs, color=color, bit=bit, outer=outer, half=half),
-        in_specs=[pl.BlockSpec(memory_space=pltpu.SMEM)] + [vmem] * (2 * len(atts)),
+        lambda *refs: weight_kernel(bits, *refs, color=color, bit=bit, outer=outer, half=half),
+        in_specs=[vmem] * (2 * len(atts)),
         out_specs=[vmem, vmem],
         out_shape=shapes(((D // 4, PART), BF), ((D // 4, PART), BF)),
         scratch_shapes=[pltpu.VMEM((D // 2, PART), BF)],
         cost_estimate=cost(1.5),
         compiler_params=params(10),
         name="weight_part",
-    )(bits, *atts, *gos)
+    )(*atts, *gos)
 
 
 def merge_kernel(bits, *refs, bit, outer, half):
@@ -347,14 +357,14 @@
     wide = sum(pair[0].shape[1] for pair in pairs)
     vmem = pl.BlockSpec(memory_space=pltpu.VMEM)
     return pl.pallas_call(
-        lambda *refs: merge_kernel(*refs, bit=bit, outer=outer, half=half),
-        in_specs=[pl.BlockSpec(memory_space=pltpu.SMEM)] + [vmem] * len(operands),
+        lambda *refs: merge_kernel(bits, *refs, bit=bit, outer=outer, half=half),
+        in_specs=[vmem] * len(operands),
         out_specs=[vmem, vmem],
         out_shape=shapes(*[((outer * half, wide), dtype)] * 2),
         cost_estimate=cost(0.6),
         compiler_params=params(10),
         name="merge",
-    )(bits, *operands)
+    )(*operands)
 
 
 def last_merge_kernel(bits, kept, got, *outs):
@@ -369,14 +379,14 @@
 def last_merge(bits, *operands):
     vmem = pl.BlockSpec(memory_space=pltpu.VMEM)
     return pl.pallas_call(
-        last_merge_kernel,
-        in_specs=[pl.BlockSpec(memory_space=pltpu.SMEM)] + [vmem] * 2,
+        lambda *refs: last_merge_kernel(bits, *refs),
+        in_specs=[vmem] * 2,
         out_specs=[vmem] * 4,
         out_shape=shapes(*[((24, D // 2), F)] * 4),
         cost_estimate=cost(0.6),
         compiler_params=params(10),
         name="last_merge",
-    )(bits, *operands)
+    )(*operands)
 
 
 def tail_kernel(bits, kept, r1, r2, r3, mine, send):
@@ -398,18 +408,12 @@
     return lax.ppermute(x, "dp", [(i, i ^ flip) for i in range(4)])
 
 
-XH, XL, YH, YL, ZH, ZL, CORE = range(7)
-
-
 def local(query, key, value, w_out, grad_out):
     q, k, v, go = query[0], key[0], value[0], grad_out[0]
     place = lax.axis_index("seq")
-    row = lax.axis_index("dp")
     core = place & 1
-    bits = jnp.stack(
-        [row >> 1, row & 1, place >> 4 & 1, place >> 3 & 1, place >> 2 & 1, place >> 1 & 1, core]
-    ).astype(jnp.int32)
-    k12, k3 = small(key_means_kernel, [((192, D), BF), ((32, D), BF)], "key_means")(after(k, bits))
+    bits = Bits()
+    k12, k3 = small(key_means_kernel, [((192, D), BF), ((32, D), BF)], "key_means")(k)
     v12, l3 = small(value_means_kernel, [((192, D), BF), ((32, PAIR), BF)], "value_means")(v, k3)
     c1 = across(l3, 1)
     l4, l5 = small(chip_kernel, [((32, PAIR), BF), ((16, PAIR), BF)], "chip")(l3, c1)

time: 91 us -> 87.1 us (0.957)
  Pallas kernels: 27 us -> 20 us
  waiting for transfers between devices: 11.2 us -> 13.9 us
    pallas_call x14, Pallas kernels: 23.8 us -> 16.8 us  [the longest x6 14 us: placed(): pl.pallas_call(lambda *refs: kernel(bits, *refs), in_specs=[vmem] * len(o...]
    ppermute x24, waiting for transfers between devices: 10.6 us -> 12.8 us  [across(): return lax.ppermute(x, 'seq', [(i, i ^ flip) for i in range(32)])]
  transfers between devices with their start and end apart: 29 -> 29, of which waited for: 8 -> 12; matrix products, arithmetic and copies ran while one was open for 0% -> 0% of each run, Pallas kernels for 20% -> 15%
where the time goes in v5:
time: 87.1 us; the launch traced here: 86.9 us
  starting transfers between devices  46.9 us (54%)
  Pallas kernels  20 us (23%)
  waiting for transfers between devices  13.9 us (16%)
  local copies, waits for them, and re-layouts  4.62 us (5%)
    ppermute x24, starting transfers between devices, across(): return lax.ppermute(x, 'seq', [(i, i ^ flip) for i in range(32)])  40.4 us
    pallas_call x6, Pallas kernels, placed(): pl.pallas_call(lambda *refs: kernel(bits, *refs), in_specs=[vmem] * len(o...  14 us
    ppermute x24, waiting for transfers between devices, across(): return lax.ppermute(x, 'seq', [(i, i ^ flip) for i in range(32)])  12.8 us
    ppermute x5, starting transfers between devices, across_x(): return lax.ppermute(x, 'dp', [(i, i ^ flip) for i in range(4)])  6.47 us
    unnamed x18, local copies, waits for them, and re-layouts  4.62 us
    pallas_call x2, Pallas kernels, weight(): pl.pallas_call(lambda *refs: weight_kernel(bits, *refs, color=color, bit=...  2.1 us
  transfers between devices with their start and end apart: 29, of which 12 were waited for; matrix products, arithmetic and copies ran while one was open for 0% of the time, Pallas kernels for 15%

profile of v5, /device:TPU:1, one launch (start us, length us, event | category | flops | bytes accessed | tf_op | source)
XLA Modules:
  0.0 86.9 jit_solution(3864691719550374253)
XLA Ops:
  3.7 1.5 %collective-permute-start.1 = (bf16[256,768]{1,0:T(8,128)(2,1)S(1)}, bf16[256,768]{1,0:T(8,128)(2,1)S(1)}, u32[]{:S(2)}, u32[]{:S(2)}) collective-permute-start(bf16[256,768]{1,0:T(8,128)(2,1)S(1)} %get-tuple-element.73), channel_id=1, source_target_pairs={{0,1},{1,0},{2,3},{3,2},{4,5},{5,4},{6,7},{7,6},{8,9},{9,8},{10,11... | collective-permute-start | bytes 1179656 | tf_op jit(solution)/shard_map/ppermute | solution.py:404
  5.3 2.6 %collective-permute-start = (bf16[256,768]{1,0:T(8,128)(2,1)S(1)}, bf16[256,768]{1,0:T(8,128)(2,1)S(1)}, u32[]{:S(2)}, u32[]{:S(2)}) collective-permute-start(bf16[256,768]{1,0:T(8,128)(2,1)S(1)} %get-tuple-element.72.refs_4_), channel_id=1, source_target_pairs={{0,96},{32,64},{64,32},{96,0},{1,97},{33,65},{65,33},{97,1},{2,98}... | collective-permute-start | bytes 1179656 | tf_op jit(solution)/shard_map/ppermute | solution.py:408
  9.4 1.7 %collective-permute-start.4 = (bf16[32,3072]{1,0:T(8,128)(2,1)S(1)}, bf16[32,3072]{1,0:T(8,128)(2,1)S(1)}, u32[]{:S(2)}, u32[]{:S(2)}) collective-permute-start(bf16[32,3072]{1,0:T(8,128)(2,1)S(1)} %get-tuple-element.77), channel_id=1, source_target_pairs={{0,2},{1,3},{2,0},{3,1},{4,6},{5,7},{6,4},{7,5},{8,10},{9,11},{10,... | collective-permute-start | bytes 589832 | tf_op jit(solution)/shard_map/ppermute | solution.py:404
  11.1 3.3 %collective-permute-start.5 = (bf16[16,3072]{1,0:T(8,128)(2,1)S(1)}, bf16[16,3072]{1,0:T(8,128)(2,1)S(1)}, u32[]{:S(2)}, u32[]{:S(2)}) collective-permute-start(bf16[16,3072]{1,0:T(8,128)(2,1)S(1)} %get-tuple-element.79.l5), channel_id=1, source_target_pairs={{0,4},{1,5},{2,6},{3,7},{4,0},{5,1},{6,2},{7,3},{8,12},{9,13},{10,... | collective-permute-start | bytes 294920 | tf_op jit(solution)/shard_map/ppermute | solution.py:404
  14.4 6.1 %collective-permute-done.5.z2.refs_7_ = bf16[16,3072]{1,0:T(8,128)(2,1)S(1)} collective-permute-done((bf16[16,3072]{1,0:T(8,128)(2,1)S(1)}, bf16[16,3072]{1,0:T(8,128)(2,1)S(1)}, u32[]{:S(2)}, u32[]{:S(2)}) %collective-permute-start.5) | collective-permute-done | bytes 98336 | tf_op jit(solution)/shard_map/ppermute | solution.py:404
  22.4 2.6 %collective-permute-start.8 = (bf16[16,3072]{1,0:T(8,128)(2,1)S(1)}, bf16[16,3072]{1,0:T(8,128)(2,1)S(1)}, u32[]{:S(2)}, u32[]{:S(2)}) collective-permute-start(bf16[16,3072]{1,0:T(8,128)(2,1)S(1)} %get-tuple-element.81), channel_id=1, source_target_pairs={{0,16},{1,17},{2,18},{3,19},{4,20},{5,21},{6,22},{7,23},{8,24},{9,... | collective-permute-start | bytes 294920 | tf_op jit(solution)/shard_map/ppermute | solution.py:404
  25.0 2.3 %copy-done = bf16[1536,1536]{1,0:T(8,128)(2,1)S(1)} copy-done((bf16[1536,1536]{1,0:T(8,128)(2,1)S(1)}, bf16[1536,1536]{1,0:T(8,128)(2,1)}, u32[]{:S(2)}) %copy-start) | copy-done | bytes 4718616
  30.2 4.5 %attention.2 = (bf16[256,768]{1,0:T(8,128)(2,1)S(1)}, bf16[256,768]{1,0:T(8,128)(2,1)S(1)}, f32[256,1536]{1,0:T(8,128)S(1)}, f32[96,1536]{1,0:T(8,128)S(1)}, bf1...) custom-call(bf16[256,1536]{1,0:T(8,128)(2,1)S(1)} %bitcast.18, bf16[256,1536]{1,0:T(8,128)(2,1)S(1)} %bitcast.11, ...), custom_call_target="tpu_custom_call" | custom-call | bytes 25900000 | tf_op jit(solution)/shard_map/attention/pallas_call | solution.py:228
  34.7 1.5 %collective-permute-start.11 = (bf16[768,256]{1,0:T(8,128)(2,1)S(1)}, bf16[768,256]{1,0:T(8,128)(2,1)S(1)}, u32[]{:S(2)}, u32[]{:S(2)}) collective-permute-start(bf16[768,256]{1,0:T(8,128)(2,1)S(1)} %get-tuple-element.84), channel_id=1, source_target_pairs={{0,96},{32,64},{64,32},{96,0},{1,97},{33,65},{65,33},{97,1},{2,98}... | collective-permute-start | bytes 1179656 | tf_op jit(solution)/shard_map/ppermute | solution.py:408
  36.2 4.5 %attention.3 = (bf16[256,768]{1,0:T(8,128)(2,1)S(1)}, bf16[256,768]{1,0:T(8,128)(2,1)S(1)}, f32[256,1536]{1,0:T(8,128)S(1)}, f32[96,1536]{1,0:T(8,128)S(1)}, bf1...) custom-call(bf16[256,1536]{1,0:T(8,128)(2,1)S(1)} %bitcast.19, ...), custom_call_target="tpu_custom_call" | custom-call | bytes 25900000 | tf_op jit(solution)/shard_map/attention/pallas_call | solution.py:228
  40.8 4.2 %collective-permute-start.10 = (bf16[768,256]{1,0:T(8,128)(2,1)S(1)}, bf16[768,256]{1,0:T(8,128)(2,1)S(1)}, u32[]{:S(2)}, u32[]{:S(2)}) collective-permute-start(bf16[768,256]{1,0:T(8,128)(2,1)S(1)} %get-tuple-element.89.refs_0_), channel_id=1, source_target_pairs={{0,1},{1,0},{2,3},{3,2},{4,5},{5,4},{6,7},{7,6},{8,9},{9,8},{10,11... | collective-permute-start | bytes 1179656 | tf_op jit(solution)/shard_map/ppermute | solution.py:404
  45.0 2.8 %collective-permute-start.12 = (bf16[768,256]{1,0:T(8,128)(2,1)S(1)}, bf16[768,256]{1,0:T(8,128)(2,1)S(1)}, u32[]{:S(2)}, u32[]{:S(2)}) collective-permute-start(bf16[768,256]{1,0:T(8,128)(2,1)S(1)} %collective-permute-done.11.refs_2_), channel_id=1, source_target_pairs={{0,1},{1,0},{2,3},{3,2},{4,5},{5,4},{6,7},{7,6},{8,9},{9,8},{10,11... | collective-permute-start | bytes 1179656 | tf_op jit(solution)/shard_map/ppermute | solution.py:404
  50.2 1.6 %collective-permute-start.13 = (bf16[384,384]{1,0:T(8,128)(2,1)S(1)}, bf16[384,384]{1,0:T(8,128)(2,1)S(1)}, u32[]{:S(2)}, u32[]{:S(2)}) collective-permute-start(bf16[384,384]{1,0:T(8,128)(2,1)S(1)} %get-tuple-element.95), channel_id=1, source_target_pairs={{0,6},{1,7},{2,4},{3,5},{4,2},{5,3},{6,0},{7,1},{8,14},{9,15},{10,... | collective-permute-start | bytes 884744 | tf_op jit(solution)/shard_map/ppermute | solution.py:404
  53.0 2.1 %collective-permute-start.16 = (bf16[16,3072]{1,0:T(8,128)(2,1)S(1)}, bf16[16,3072]{1,0:T(8,128)(2,1)S(1)}, u32[]{:S(2)}, u32[]{:S(2)}) collective-permute-start(bf16[16,3072]{1,0:T(8,128)(2,1)S(1)} %get-tuple-element.104), channel_id=1, source_target_pairs={{0,16},{1,17},{2,18},{3,19},{4,20},{5,21},{6,22},{7,23},{8,24},{9,... | collective-permute-start | bytes 294920 | tf_op jit(solution)/shard_map/ppermute | solution.py:404
  55.1 1.8 %collective-permute-start.17 = (bf16[16,3072]{1,0:T(8,128)(2,1)S(1)}, bf16[16,3072]{1,0:T(8,128)(2,1)S(1)}, u32[]{:S(2)}, u32[]{:S(2)}) collective-permute-start(bf16[16,3072]{1,0:T(8,128)(2,1)S(1)} %get-tuple-element.105), channel_id=1, source_target_pairs={{0,24},{1,25},{2,26},{3,27},{4,28},{5,29},{6,30},{7,31},{8,16},{9,... | collective-permute-start | bytes 294920 | tf_op jit(solution)/shard_map/ppermute | solution.py:404
  56.9 2.3 %mixed.1 = bf16[256,1536]{1,0:T(8,128)(2,1)} custom-call(bf16[256,768]{1,0:T(8,128)(2,1)S(1)} %get-tuple-element.91.refs_0_, bf16[256,768]{1,0:T(8,128)(2,1)S(1)} %get-tuple-element.92.refs_1_, bf16[1536,1536]{1,0:T(8,128)(2,1)S(1)} %bitcast.9), custom_call_target="tpu_custom_call" | custom-call | bytes 8510000 | tf_op jit(solution)/shard_map/mixed/pallas_call | solution.py:228
  61.8 1.7 %collective-permute-start.18 = (bf16[192,384]{1,0:T(8,128)(2,1)S(1)}, bf16[192,384]{1,0:T(8,128)(2,1)S(1)}, u32[]{:S(2)}, u32[]{:S(2)}) collective-permute-start(bf16[192,384]{1,0:T(8,128)(2,1)S(1)} %get-tuple-element.108), channel_id=1, source_target_pairs={{0,6},{1,7},{2,4},{3,5},{4,2},{5,3},{6,0},{7,1},{8,14},{9,15},{10,... | collective-permute-start | bytes 442376 | tf_op jit(solution)/shard_map/ppermute | solution.py:404
  64.5 1.6 %collective-permute-start.21 = (bf16[16,3072]{1,0:T(8,128)(2,1)S(1)}, bf16[16,3072]{1,0:T(8,128)(2,1)S(1)}, u32[]{:S(2)}, u32[]{:S(2)}) collective-permute-start(bf16[16,3072]{1,0:T(8,128)(2,1)S(1)} %get-tuple-element.116), channel_id=1, source_target_pairs={{0,4},{1,5},{2,6},{3,7},{4,0},{5,1},{6,2},{7,3},{8,12},{9,13},{10,... | collective-permute-start | bytes 294920 | tf_op jit(solution)/shard_map/ppermute | solution.py:404
  66.1 1.6 %collective-permute-start.22 = (bf16[16,3072]{1,0:T(8,128)(2,1)S(1)}, bf16[16,3072]{1,0:T(8,128)(2,1)S(1)}, u32[]{:S(2)}, u32[]{:S(2)}) collective-permute-start(bf16[16,3072]{1,0:T(8,128)(2,1)S(1)} %get-tuple-element.117), channel_id=1, source_target_pairs={{0,6},{1,7},{2,4},{3,5},{4,2},{5,3},{6,0},{7,1},{8,14},{9,15},{10,... | collective-permute-start | bytes 294920 | tf_op jit(solution)/shard_map/ppermute | solution.py:404
  70.5 1.5 %collective-permute-done.22.z3 = bf16[16,3072]{1,0:T(8,128)(2,1)S(1)} collective-permute-done((bf16[16,3072]{1,0:T(8,128)(2,1)S(1)}, bf16[16,3072]{1,0:T(8,128)(2,1)S(1)}, u32[]{:S(2)}, u32[]{:S(2)}) %collective-permute-start.22) | collective-permute-done | bytes 98336 | tf_op jit(solution)/shard_map/ppermute | solution.py:404
  72.5 3.7 %collective-permute-start.24 = (bf16[32,3072]{1,0:T(8,128)(2,1)S(1)}, bf16[32,3072]{1,0:T(8,128)(2,1)S(1)}, u32[]{:S(2)}, u32[]{:S(2)}) collective-permute-start(bf16[32,3072]{1,0:T(8,128)(2,1)S(1)} %get-tuple-element.124), channel_id=1, source_target_pairs={{0,1},{1,0},{2,3},{3,2},{4,5},{5,4},{6,7},{7,6},{8,9},{9,8},{10,11... | collective-permute-start | bytes 589832 | tf_op jit(solution)/shard_map/ppermute | solution.py:404
  76.8 2.2 %collective-permute-start.27 = (f32[24,768]{1,0:T(8,128)S(1)}, f32[24,768]{1,0:T(8,128)S(1)}, u32[]{:S(2)}, u32[]{:S(2)}) collective-permute-start(f32[24,768]{1,0:T(8,128)S(1)} %get-tuple-element.130), channel_id=1, source_target_pairs={{0,10},{1,11},{2,8},{3,9},{4,14},{5,15},{6,12},{7,13},{8,2},{9,3},... | collective-permute-start | bytes 221192 | tf_op jit(solution)/shard_map/ppermute | solution.py:404
  79.0 1.7 %finish.1 = (bf16[256,1536]{1,0:T(8,128)(2,1)}, bf16[256,1536]{1,0:T(8,128)(2,1)}) custom-call(f32[256,1536]{1,0:T(8,128)S(1)} %get-tuple-element.122.refs_0_, f32[256,1536]{1,0:T(8,128)S(1)} %get-tuple-element.123.refs_1_, f32[32,3072]{1,0:T(8,128)S(1)} %get-tuple-element.118.refs_2_, bf16[32,3072]{1,0:T(8,128)(2,1)S(1)} %collective-permute-done.24.refs_3_), custom_call_target="tpu_custom_call" | custom-call | bytes 6290000 | tf_op jit(solution)/shard_map/finish/pallas_call | solution.py:228
  81.0 4.4 %collective-permute-start.28 = (f32[12,768]{1,0:T(8,128)S(1)}, f32[12,768]{1,0:T(8,128)S(1)}, u32[]{:S(2)}, u32[]{:S(2)}) collective-permute-start(f32[12,768]{1,0:T(8,128)S(1)} %get-tuple-element.132), channel_id=1, source_target_pairs={{0,1},{1,0},{2,3},{3,2},{4,5},{5,4},{6,7},{7,6},{8,9},{9,8},{10,11... | collective-permute-start | bytes 110600 | tf_op jit(solution)/shard_map/ppermute | solution.py:404
  (75 shorter events, 22.2 us)
Async XLA Ops:
  5.3 23.5 %collective-permute-start = (bf16[256,768]{1,0:T(8,128)(2,1)S(1)}, bf16[256,768]{1,0:T(8,128)(2,1)S(1)}, u32[]{:S(2)}, u32[]{:S(2)}) collective-permute-start(bf16[256,768]{1,0:T(8,128)(2,1)S(1)} %get-tuple-element.72.refs_4_), channel_id=1, source_target_pairs={{0,96},{32,64},{64,32},{96,0},{1,97},{33,65},{65,33},{97,1},{2,98}... | collective-permute-start | bytes 1179656 | tf_op jit(solution)/shard_map/ppermute | solution.py:408
  7.8 20.9 %collective-permute-start.2 = (bf16[256,768]{1,0:T(8,128)(2,1)S(1)}, bf16[256,768]{1,0:T(8,128)(2,1)S(1)}, u32[]{:S(2)}, u32[]{:S(2)}) collective-permute-start(bf16[256,768]{1,0:T(8,128)(2,1)S(1)} %collective-permute-done.1.refs_5_), channel_id=1, source_target_pairs={{0,96},{32,64},{64,32},{96,0},{1,97},{33,65},{65,33},{97,1},{2,98}... | collective-permute-start | bytes 1179656 | tf_op jit(solution)/shard_map/ppermute | solution.py:408
  9.4 11.2 %collective-permute-start.4 = (bf16[32,3072]{1,0:T(8,128)(2,1)S(1)}, bf16[32,3072]{1,0:T(8,128)(2,1)S(1)}, u32[]{:S(2)}, u32[]{:S(2)}) collective-permute-start(bf16[32,3072]{1,0:T(8,128)(2,1)S(1)} %get-tuple-element.77), channel_id=1, source_target_pairs={{0,2},{1,3},{2,0},{3,1},{4,6},{5,7},{6,4},{7,5},{8,10},{9,11},{10,... | collective-permute-start | bytes 589832 | tf_op jit(solution)/shard_map/ppermute | solution.py:404
  11.1 9.4 %collective-permute-start.5 = (bf16[16,3072]{1,0:T(8,128)(2,1)S(1)}, bf16[16,3072]{1,0:T(8,128)(2,1)S(1)}, u32[]{:S(2)}, u32[]{:S(2)}) collective-permute-start(bf16[16,3072]{1,0:T(8,128)(2,1)S(1)} %get-tuple-element.79.l5), channel_id=1, source_target_pairs={{0,4},{1,5},{2,6},{3,7},{4,0},{5,1},{6,2},{7,3},{8,12},{9,13},{10,... | collective-permute-start | bytes 294920 | tf_op jit(solution)/shard_map/ppermute | solution.py:404
  14.4 6.1 %collective-permute-start.6 = (bf16[16,3072]{1,0:T(8,128)(2,1)S(1)}, bf16[16,3072]{1,0:T(8,128)(2,1)S(1)}, u32[]{:S(2)}, u32[]{:S(2)}) collective-permute-start(bf16[16,3072]{1,0:T(8,128)(2,1)S(1)} %get-tuple-element.79.l5), channel_id=1, source_target_pairs={{0,6},{1,7},{2,4},{3,5},{4,2},{5,3},{6,0},{7,1},{8,14},{9,15},{10,... | collective-permute-start | bytes 294920 | tf_op jit(solution)/shard_map/ppermute | solution.py:404
  21.0 9.2 %collective-permute-start.7 = (bf16[32,3072]{1,0:T(8,128)(2,1)S(1)}, bf16[32,3072]{1,0:T(8,128)(2,1)S(1)}, u32[]{:S(2)}, u32[]{:S(2)}) collective-permute-start(bf16[32,3072]{1,0:T(8,128)(2,1)S(1)} %get-tuple-element.80), channel_id=1, source_target_pairs={{0,8},{1,9},{2,10},{3,11},{4,12},{5,13},{6,14},{7,15},{8,0},{9,1},... | collective-permute-start | bytes 589832 | tf_op jit(solution)/shard_map/ppermute | solution.py:404
  22.4 7.0 %collective-permute-start.8 = (bf16[16,3072]{1,0:T(8,128)(2,1)S(1)}, bf16[16,3072]{1,0:T(8,128)(2,1)S(1)}, u32[]{:S(2)}, u32[]{:S(2)}) collective-permute-start(bf16[16,3072]{1,0:T(8,128)(2,1)S(1)} %get-tuple-element.81), channel_id=1, source_target_pairs={{0,16},{1,17},{2,18},{3,19},{4,20},{5,21},{6,22},{7,23},{8,24},{9,... | collective-permute-start | bytes 294920 | tf_op jit(solution)/shard_map/ppermute | solution.py:404
  25.0 5.2 %collective-permute-start.9 = (bf16[16,3072]{1,0:T(8,128)(2,1)S(1)}, bf16[16,3072]{1,0:T(8,128)(2,1)S(1)}, u32[]{:S(2)}, u32[]{:S(2)}) collective-permute-start(bf16[16,3072]{1,0:T(8,128)(2,1)S(1)} %get-tuple-element.81), channel_id=1, source_target_pairs={{0,24},{1,25},{2,26},{3,27},{4,28},{5,29},{6,30},{7,31},{8,16},{9,... | collective-permute-start | bytes 294920 | tf_op jit(solution)/shard_map/ppermute | solution.py:404
  34.7 10.3 %collective-permute-start.11 = (bf16[768,256]{1,0:T(8,128)(2,1)S(1)}, bf16[768,256]{1,0:T(8,128)(2,1)S(1)}, u32[]{:S(2)}, u32[]{:S(2)}) collective-permute-start(bf16[768,256]{1,0:T(8,128)(2,1)S(1)} %get-tuple-element.84), channel_id=1, source_target_pairs={{0,96},{32,64},{64,32},{96,0},{1,97},{33,65},{65,33},{97,1},{2,98}... | collective-permute-start | bytes 1179656 | tf_op jit(solution)/shard_map/ppermute | solution.py:408
  40.8 7.1 %collective-permute-start.10 = (bf16[768,256]{1,0:T(8,128)(2,1)S(1)}, bf16[768,256]{1,0:T(8,128)(2,1)S(1)}, u32[]{:S(2)}, u32[]{:S(2)}) collective-permute-start(bf16[768,256]{1,0:T(8,128)(2,1)S(1)} %get-tuple-element.89.refs_0_), channel_id=1, source_target_pairs={{0,1},{1,0},{2,3},{3,2},{4,5},{5,4},{6,7},{7,6},{8,9},{9,8},{10,11... | collective-permute-start | bytes 1179656 | tf_op jit(solution)/shard_map/ppermute | solution.py:404
  50.2 9.5 %collective-permute-start.13 = (bf16[384,384]{1,0:T(8,128)(2,1)S(1)}, bf16[384,384]{1,0:T(8,128)(2,1)S(1)}, u32[]{:S(2)}, u32[]{:S(2)}) collective-permute-start(bf16[384,384]{1,0:T(8,128)(2,1)S(1)} %get-tuple-element.95), channel_id=1, source_target_pairs={{0,6},{1,7},{2,4},{3,5},{4,2},{5,3},{6,0},{7,1},{8,14},{9,15},{10,... | collective-permute-start | bytes 884744 | tf_op jit(solution)/shard_map/ppermute | solution.py:404
  52.9 8.0 %collective-permute-start.14 = (bf16[384,384]{1,0:T(8,128)(2,1)S(1)}, bf16[384,384]{1,0:T(8,128)(2,1)S(1)}, u32[]{:S(2)}, u32[]{:S(2)}) collective-permute-start(bf16[384,384]{1,0:T(8,128)(2,1)S(1)} %get-tuple-element.98), channel_id=1, source_target_pairs={{0,32},{32,0},{64,96},{96,64},{1,33},{33,1},{65,97},{97,65},{2,34}... | collective-permute-start | bytes 884744 | tf_op jit(solution)/shard_map/ppermute | solution.py:408
  52.9 8.3 %collective-permute-start.15 = (bf16[32,3072]{1,0:T(8,128)(2,1)S(1)}, bf16[32,3072]{1,0:T(8,128)(2,1)S(1)}, u32[]{:S(2)}, u32[]{:S(2)}) collective-permute-start(bf16[32,3072]{1,0:T(8,128)(2,1)S(1)} %get-tuple-element.103), channel_id=1, source_target_pairs={{0,8},{1,9},{2,10},{3,11},{4,12},{5,13},{6,14},{7,15},{8,0},{9,1},... | collective-permute-start | bytes 589832 | tf_op jit(solution)/shard_map/ppermute | solution.py:404
  53.0 8.2 %collective-permute-start.16 = (bf16[16,3072]{1,0:T(8,128)(2,1)S(1)}, bf16[16,3072]{1,0:T(8,128)(2,1)S(1)}, u32[]{:S(2)}, u32[]{:S(2)}) collective-permute-start(bf16[16,3072]{1,0:T(8,128)(2,1)S(1)} %get-tuple-element.104), channel_id=1, source_target_pairs={{0,16},{1,17},{2,18},{3,19},{4,20},{5,21},{6,22},{7,23},{8,24},{9,... | collective-permute-start | bytes 294920 | tf_op jit(solution)/shard_map/ppermute | solution.py:404
  55.1 6.1 %collective-permute-start.17 = (bf16[16,3072]{1,0:T(8,128)(2,1)S(1)}, bf16[16,3072]{1,0:T(8,128)(2,1)S(1)}, u32[]{:S(2)}, u32[]{:S(2)}) collective-permute-start(bf16[16,3072]{1,0:T(8,128)(2,1)S(1)} %get-tuple-element.105), channel_id=1, source_target_pairs={{0,24},{1,25},{2,26},{3,27},{4,28},{5,29},{6,30},{7,31},{8,16},{9,... | collective-permute-start | bytes 294920 | tf_op jit(solution)/shard_map/ppermute | solution.py:404
  61.7 10.4 %collective-permute-start.20 = (bf16[32,3072]{1,0:T(8,128)(2,1)S(1)}, bf16[32,3072]{1,0:T(8,128)(2,1)S(1)}, u32[]{:S(2)}, u32[]{:S(2)}) collective-permute-start(bf16[32,3072]{1,0:T(8,128)(2,1)S(1)} %get-tuple-element.115), channel_id=1, source_target_pairs={{0,2},{1,3},{2,0},{3,1},{4,6},{5,7},{6,4},{7,5},{8,10},{9,11},{10,... | collective-permute-start | bytes 589832 | tf_op jit(solution)/shard_map/ppermute | solution.py:404
  61.8 5.9 %collective-permute-start.18 = (bf16[192,384]{1,0:T(8,128)(2,1)S(1)}, bf16[192,384]{1,0:T(8,128)(2,1)S(1)}, u32[]{:S(2)}, u32[]{:S(2)}) collective-permute-start(bf16[192,384]{1,0:T(8,128)(2,1)S(1)} %get-tuple-element.108), channel_id=1, source_target_pairs={{0,6},{1,7},{2,4},{3,5},{4,2},{5,3},{6,0},{7,1},{8,14},{9,15},{10,... | collective-permute-start | bytes 442376 | tf_op jit(solution)/shard_map/ppermute | solution.py:404
  64.5 6.0 %collective-permute-start.21 = (bf16[16,3072]{1,0:T(8,128)(2,1)S(1)}, bf16[16,3072]{1,0:T(8,128)(2,1)S(1)}, u32[]{:S(2)}, u32[]{:S(2)}) collective-permute-start(bf16[16,3072]{1,0:T(8,128)(2,1)S(1)} %get-tuple-element.116), channel_id=1, source_target_pairs={{0,4},{1,5},{2,6},{3,7},{4,0},{5,1},{6,2},{7,3},{8,12},{9,13},{10,... | collective-permute-start | bytes 294920 | tf_op jit(solution)/shard_map/ppermute | solution.py:404
  66.1 6.0 %collective-permute-start.22 = (bf16[16,3072]{1,0:T(8,128)(2,1)S(1)}, bf16[16,3072]{1,0:T(8,128)(2,1)S(1)}, u32[]{:S(2)}, u32[]{:S(2)}) collective-permute-start(bf16[16,3072]{1,0:T(8,128)(2,1)S(1)} %get-tuple-element.117), channel_id=1, source_target_pairs={{0,6},{1,7},{2,4},{3,5},{4,2},{5,3},{6,0},{7,1},{8,14},{9,15},{10,... | collective-permute-start | bytes 294920 | tf_op jit(solution)/shard_map/ppermute | solution.py:404
  67.8 8.4 %collective-permute-start.23 = (bf16[96,768]{1,0:T(8,128)(2,1)S(1)}, bf16[96,768]{1,0:T(8,128)(2,1)S(1)}, u32[]{:S(2)}, u32[]{:S(2)}) collective-permute-start(bf16[96,768]{1,0:T(8,128)(2,1)S(1)} %get-tuple-element.120), channel_id=1, source_target_pairs={{0,24},{1,25},{2,26},{3,27},{4,28},{5,29},{6,30},{7,31},{8,16},{9,... | collective-permute-start | bytes 442376 | tf_op jit(solution)/shard_map/ppermute | solution.py:404
  72.5 6.5 %collective-permute-start.24 = (bf16[32,3072]{1,0:T(8,128)(2,1)S(1)}, bf16[32,3072]{1,0:T(8,128)(2,1)S(1)}, u32[]{:S(2)}, u32[]{:S(2)}) collective-permute-start(bf16[32,3072]{1,0:T(8,128)(2,1)S(1)} %get-tuple-element.124), channel_id=1, source_target_pairs={{0,1},{1,0},{2,3},{3,2},{4,5},{5,4},{6,7},{7,6},{8,9},{9,8},{10,11... | collective-permute-start | bytes 589832 | tf_op jit(solution)/shard_map/ppermute | solution.py:404
  76.3 4.4 %collective-permute-start.25 = (f32[24,768]{1,0:T(8,128)S(1)}, f32[24,768]{1,0:T(8,128)S(1)}, u32[]{:S(2)}, u32[]{:S(2)}) collective-permute-start(f32[24,768]{1,0:T(8,128)S(1)} %get-tuple-element.128), channel_id=1, source_target_pairs={{0,8},{1,9},{2,10},{3,11},{4,12},{5,13},{6,14},{7,15},{8,0},{9,1},... | collective-permute-start | bytes 221192 | tf_op jit(solution)/shard_map/ppermute | solution.py:404
  76.4 4.3 %collective-permute-start.26 = (f32[24,768]{1,0:T(8,128)S(1)}, f32[24,768]{1,0:T(8,128)S(1)}, u32[]{:S(2)}, u32[]{:S(2)}) collective-permute-start(f32[24,768]{1,0:T(8,128)S(1)} %get-tuple-element.129), channel_id=1, source_target_pairs={{0,2},{1,3},{2,0},{3,1},{4,6},{5,7},{6,4},{7,5},{8,10},{9,11},{10,... | collective-permute-start | bytes 221192 | tf_op jit(solution)/shard_map/ppermute | solution.py:404
  81.0 5.3 %collective-permute-start.28 = (f32[12,768]{1,0:T(8,128)S(1)}, f32[12,768]{1,0:T(8,128)S(1)}, u32[]{:S(2)}, u32[]{:S(2)}) collective-permute-start(f32[12,768]{1,0:T(8,128)S(1)} %get-tuple-element.132), channel_id=1, source_target_pairs={{0,1},{1,0},{2,3},{3,2},{4,5},{5,4},{6,7},{7,6},{8,9},{9,8},{10,11... | collective-permute-start | bytes 110600 | tf_op jit(solution)/shard_map/ppermute | solution.py:404
  (14 other events, 82.9 us)

commit v6 on v5

--- a/solution.py
+++ b/solution.py
@@ -450,12 +450,12 @@
     z1, z3, z2 = across(s1, 2), across(s3, 6), across(s2, 4)
     s, kept = merge(bits, [(after(a_k, own), a_r), (b_k, b_r)], YH, 1, 96)
     s_r = across(s, 24)
-    gq = placed(join_kernel, [((T, D), BF)], "join", 0.7, 8, bits, after(gq_a, kept), gq_b)[0]
     send, keep = small(back_chip_kernel, [((32, PAIR), BF), ((32, PAIR), F)], "back_chip")(
-        near_a, after(near_b, gq), own, z1, z2, z3
+        near_a, after(near_b, kept), own, z1, z2, z3
     )
     c1 = across(send, 1)
-    s1, s2, s3, kept = last_merge(bits, after(kept, keep), s_r)
+    gq = placed(join_kernel, [((T, D), BF)], "join", 0.7, 8, bits, after(gq_a, keep), gq_b)[0]
+    s1, s2, s3, kept = last_merge(bits, after(kept, gq), s_r)
     r1, r2, r3 = across(s1, 8), across(s2, 2), across(s3, 10)
     gk, gv = placed(
         finish_kernel, [((T, D), BF)] * 2, "finish", 1.7, 12, bits, after(fine_a, kept), fine_b, keep, c1

time: 87.1 us -> 87.1 us (level)
  transfers between devices with their start and end apart: 29 -> 29, of which waited for: 12 -> 11; matrix products, arithmetic and copies ran while one was open for 0% -> 0% of each run, Pallas kernels for 15% -> 15%
where the time goes in v6:
time: 87.1 us; the launch traced here: 86.9 us
  starting transfers between devices  46.1 us (53%)
  Pallas kernels  20 us (23%)
  waiting for transfers between devices  14.6 us (17%)
  local copies, waits for them, and re-layouts  4.62 us (5%)
    ppermute x24, starting transfers between devices, across(): return lax.ppermute(x, 'seq', [(i, i ^ flip) for i in range(32)])  39.6 us
    pallas_call x6, Pallas kernels, placed(): pl.pallas_call(lambda *refs: kernel(bits, *refs), in_specs=[vmem] * len(o...  14 us
    ppermute x24, waiting for transfers between devices, across(): return lax.ppermute(x, 'seq', [(i, i ^ flip) for i in range(32)])  13.5 us
    ppermute x5, starting transfers between devices, across_x(): return lax.ppermute(x, 'dp', [(i, i ^ flip) for i in range(4)])  6.47 us
    unnamed x18, local copies, waits for them, and re-layouts  4.62 us
    pallas_call x2, Pallas kernels, weight(): pl.pallas_call(lambda *refs: weight_kernel(bits, *refs, color=color, bit=...  2.1 us
  transfers between devices with their start and end apart: 29, of which 11 were waited for; matrix products, arithmetic and copies ran while one was open for 0% of the time, Pallas kernels for 15%

profile of v6, /device:TPU:1, one launch (start us, length us, event | category | flops | bytes accessed | tf_op | source)
XLA Modules:
  0.0 86.9 jit_solution(15094970137051971729)
XLA Ops:
  3.7 1.5 %collective-permute-start.1 = (bf16[256,768]{1,0:T(8,128)(2,1)S(1)}, bf16[256,768]{1,0:T(8,128)(2,1)S(1)}, u32[]{:S(2)}, u32[]{:S(2)}) collective-permute-start(bf16[256,768]{1,0:T(8,128)(2,1)S(1)} %get-tuple-element.73), channel_id=1, source_target_pairs={{0,1},{1,0},{2,3},{3,2},{4,5},{5,4},{6,7},{7,6},{8,9},{9,8},{10,11... | collective-permute-start | bytes 1179656 | tf_op jit(solution)/shard_map/ppermute | solution.py:404
  5.3 2.6 %collective-permute-start = (bf16[256,768]{1,0:T(8,128)(2,1)S(1)}, bf16[256,768]{1,0:T(8,128)(2,1)S(1)}, u32[]{:S(2)}, u32[]{:S(2)}) collective-permute-start(bf16[256,768]{1,0:T(8,128)(2,1)S(1)} %get-tuple-element.72.refs_4_), channel_id=1, source_target_pairs={{0,96},{32,64},{64,32},{96,0},{1,97},{33,65},{65,33},{97,1},{2,98}... | collective-permute-start | bytes 1179656 | tf_op jit(solution)/shard_map/ppermute | solution.py:408
  9.4 1.7 %collective-permute-start.4 = (bf16[32,3072]{1,0:T(8,128)(2,1)S(1)}, bf16[32,3072]{1,0:T(8,128)(2,1)S(1)}, u32[]{:S(2)}, u32[]{:S(2)}) collective-permute-start(bf16[32,3072]{1,0:T(8,128)(2,1)S(1)} %get-tuple-element.77), channel_id=1, source_target_pairs={{0,2},{1,3},{2,0},{3,1},{4,6},{5,7},{6,4},{7,5},{8,10},{9,11},{10,... | collective-permute-start | bytes 589832 | tf_op jit(solution)/shard_map/ppermute | solution.py:404
  11.1 3.3 %collective-permute-start.5 = (bf16[16,3072]{1,0:T(8,128)(2,1)S(1)}, bf16[16,3072]{1,0:T(8,128)(2,1)S(1)}, u32[]{:S(2)}, u32[]{:S(2)}) collective-permute-start(bf16[16,3072]{1,0:T(8,128)(2,1)S(1)} %get-tuple-element.79.l5), channel_id=1, source_target_pairs={{0,4},{1,5},{2,6},{3,7},{4,0},{5,1},{6,2},{7,3},{8,12},{9,13},{10,... | collective-permute-start | bytes 294920 | tf_op jit(solution)/shard_map/ppermute | solution.py:404
  14.4 6.1 %collective-permute-done.5.z2.refs_7_ = bf16[16,3072]{1,0:T(8,128)(2,1)S(1)} collective-permute-done((bf16[16,3072]{1,0:T(8,128)(2,1)S(1)}, bf16[16,3072]{1,0:T(8,128)(2,1)S(1)}, u32[]{:S(2)}, u32[]{:S(2)}) %collective-permute-start.5) | collective-permute-done | bytes 98336 | tf_op jit(solution)/shard_map/ppermute | solution.py:404
  22.4 2.6 %collective-permute-start.8 = (bf16[16,3072]{1,0:T(8,128)(2,1)S(1)}, bf16[16,3072]{1,0:T(8,128)(2,1)S(1)}, u32[]{:S(2)}, u32[]{:S(2)}) collective-permute-start(bf16[16,3072]{1,0:T(8,128)(2,1)S(1)} %get-tuple-element.81), channel_id=1, source_target_pairs={{0,16},{1,17},{2,18},{3,19},{4,20},{5,21},{6,22},{7,23},{8,24},{9,... | collective-permute-start | bytes 294920 | tf_op jit(solution)/shard_map/ppermute | solution.py:404
  25.0 2.3 %copy-done = bf16[1536,1536]{1,0:T(8,128)(2,1)S(1)} copy-done((bf16[1536,1536]{1,0:T(8,128)(2,1)S(1)}, bf16[1536,1536]{1,0:T(8,128)(2,1)}, u32[]{:S(2)}) %copy-start) | copy-done | bytes 4718616
  30.2 4.5 %attention.2 = (bf16[256,768]{1,0:T(8,128)(2,1)S(1)}, bf16[256,768]{1,0:T(8,128)(2,1)S(1)}, f32[256,1536]{1,0:T(8,128)S(1)}, f32[96,1536]{1,0:T(8,128)S(1)}, bf1...) custom-call(bf16[256,1536]{1,0:T(8,128)(2,1)S(1)} %bitcast.18, bf16[256,1536]{1,0:T(8,128)(2,1)S(1)} %bitcast.11, ...), custom_call_target="tpu_custom_call" | custom-call | bytes 25900000 | tf_op jit(solution)/shard_map/attention/pallas_call | solution.py:228
  34.7 1.5 %collective-permute-start.11 = (bf16[768,256]{1,0:T(8,128)(2,1)S(1)}, bf16[768,256]{1,0:T(8,128)(2,1)S(1)}, u32[]{:S(2)}, u32[]{:S(2)}) collective-permute-start(bf16[768,256]{1,0:T(8,128)(2,1)S(1)} %get-tuple-element.84), channel_id=1, source_target_pairs={{0,96},{32,64},{64,32},{96,0},{1,97},{33,65},{65,33},{97,1},{2,98}... | collective-permute-start | bytes 1179656 | tf_op jit(solution)/shard_map/ppermute | solution.py:408
  36.2 4.5 %attention.3 = (bf16[256,768]{1,0:T(8,128)(2,1)S(1)}, bf16[256,768]{1,0:T(8,128)(2,1)S(1)}, f32[256,1536]{1,0:T(8,128)S(1)}, f32[96,1536]{1,0:T(8,128)S(1)}, bf1...) custom-call(bf16[256,1536]{1,0:T(8,128)(2,1)S(1)} %bitcast.19, ...), custom_call_target="tpu_custom_call" | custom-call | bytes 25900000 | tf_op jit(solution)/shard_map/attention/pallas_call | solution.py:228
  40.8 4.2 %collective-permute-start.10 = (bf16[768,256]{1,0:T(8,128)(2,1)S(1)}, bf16[768,256]{1,0:T(8,128)(2,1)S(1)}, u32[]{:S(2)}, u32[]{:S(2)}) collective-permute-start(bf16[768,256]{1,0:T(8,128)(2,1)S(1)} %get-tuple-element.89.refs_0_), channel_id=1, source_target_pairs={{0,1},{1,0},{2,3},{3,2},{4,5},{5,4},{6,7},{7,6},{8,9},{9,8},{10,11... | collective-permute-start | bytes 1179656 | tf_op jit(solution)/shard_map/ppermute | solution.py:404
  45.0 2.8 %collective-permute-start.12 = (bf16[768,256]{1,0:T(8,128)(2,1)S(1)}, bf16[768,256]{1,0:T(8,128)(2,1)S(1)}, u32[]{:S(2)}, u32[]{:S(2)}) collective-permute-start(bf16[768,256]{1,0:T(8,128)(2,1)S(1)} %collective-permute-done.11.refs_2_), channel_id=1, source_target_pairs={{0,1},{1,0},{2,3},{3,2},{4,5},{5,4},{6,7},{7,6},{8,9},{9,8},{10,11... | collective-permute-start | bytes 1179656 | tf_op jit(solution)/shard_map/ppermute | solution.py:404
  50.2 1.6 %collective-permute-start.13 = (bf16[384,384]{1,0:T(8,128)(2,1)S(1)}, bf16[384,384]{1,0:T(8,128)(2,1)S(1)}, u32[]{:S(2)}, u32[]{:S(2)}) collective-permute-start(bf16[384,384]{1,0:T(8,128)(2,1)S(1)} %get-tuple-element.97), channel_id=1, source_target_pairs={{0,6},{1,7},{2,4},{3,5},{4,2},{5,3},{6,0},{7,1},{8,14},{9,15},{10,... | collective-permute-start | bytes 884744 | tf_op jit(solution)/shard_map/ppermute | solution.py:404
  53.0 2.1 %collective-permute-start.16 = (bf16[16,3072]{1,0:T(8,128)(2,1)S(1)}, bf16[16,3072]{1,0:T(8,128)(2,1)S(1)}, u32[]{:S(2)}, u32[]{:S(2)}) collective-permute-start(bf16[16,3072]{1,0:T(8,128)(2,1)S(1)} %get-tuple-element.104), channel_id=1, source_target_pairs={{0,16},{1,17},{2,18},{3,19},{4,20},{5,21},{6,22},{7,23},{8,24},{9,... | collective-permute-start | bytes 294920 | tf_op jit(solution)/shard_map/ppermute | solution.py:404
  55.1 1.8 %collective-permute-start.17 = (bf16[16,3072]{1,0:T(8,128)(2,1)S(1)}, bf16[16,3072]{1,0:T(8,128)(2,1)S(1)}, u32[]{:S(2)}, u32[]{:S(2)}) collective-permute-start(bf16[16,3072]{1,0:T(8,128)(2,1)S(1)} %get-tuple-element.105), channel_id=1, source_target_pairs={{0,24},{1,25},{2,26},{3,27},{4,28},{5,29},{6,30},{7,31},{8,16},{9,... | collective-permute-start | bytes 294920 | tf_op jit(solution)/shard_map/ppermute | solution.py:404
  56.9 2.3 %mixed.1 = bf16[256,1536]{1,0:T(8,128)(2,1)} custom-call(bf16[256,768]{1,0:T(8,128)(2,1)S(1)} %get-tuple-element.91.refs_0_, bf16[256,768]{1,0:T(8,128)(2,1)S(1)} %get-tuple-element.92.refs_1_, bf16[1536,1536]{1,0:T(8,128)(2,1)S(1)} %bitcast.9), custom_call_target="tpu_custom_call" | custom-call | bytes 8510000 | tf_op jit(solution)/shard_map/mixed/pallas_call | solution.py:228
  61.8 1.7 %collective-permute-start.18 = (bf16[192,384]{1,0:T(8,128)(2,1)S(1)}, bf16[192,384]{1,0:T(8,128)(2,1)S(1)}, u32[]{:S(2)}, u32[]{:S(2)}) collective-permute-start(bf16[192,384]{1,0:T(8,128)(2,1)S(1)} %get-tuple-element.108), channel_id=1, source_target_pairs={{0,6},{1,7},{2,4},{3,5},{4,2},{5,3},{6,0},{7,1},{8,14},{9,15},{10,... | collective-permute-start | bytes 442376 | tf_op jit(solution)/shard_map/ppermute | solution.py:404
  64.5 1.6 %collective-permute-start.21 = (bf16[16,3072]{1,0:T(8,128)(2,1)S(1)}, bf16[16,3072]{1,0:T(8,128)(2,1)S(1)}, u32[]{:S(2)}, u32[]{:S(2)}) collective-permute-start(bf16[16,3072]{1,0:T(8,128)(2,1)S(1)} %get-tuple-element.113), channel_id=1, source_target_pairs={{0,4},{1,5},{2,6},{3,7},{4,0},{5,1},{6,2},{7,3},{8,12},{9,13},{10,... | collective-permute-start | bytes 294920 | tf_op jit(solution)/shard_map/ppermute | solution.py:404
  66.1 1.6 %collective-permute-start.22 = (bf16[16,3072]{1,0:T(8,128)(2,1)S(1)}, bf16[16,3072]{1,0:T(8,128)(2,1)S(1)}, u32[]{:S(2)}, u32[]{:S(2)}) collective-permute-start(bf16[16,3072]{1,0:T(8,128)(2,1)S(1)} %get-tuple-element.114), channel_id=1, source_target_pairs={{0,6},{1,7},{2,4},{3,5},{4,2},{5,3},{6,0},{7,1},{8,14},{9,15},{10,... | collective-permute-start | bytes 294920 | tf_op jit(solution)/shard_map/ppermute | solution.py:404
  70.5 1.5 %collective-permute-done.22.z3 = bf16[16,3072]{1,0:T(8,128)(2,1)S(1)} collective-permute-done((bf16[16,3072]{1,0:T(8,128)(2,1)S(1)}, bf16[16,3072]{1,0:T(8,128)(2,1)S(1)}, u32[]{:S(2)}, u32[]{:S(2)}) %collective-permute-start.22) | collective-permute-done | bytes 98336 | tf_op jit(solution)/shard_map/ppermute | solution.py:404
  72.5 3.7 %collective-permute-start.24 = (bf16[32,3072]{1,0:T(8,128)(2,1)S(1)}, bf16[32,3072]{1,0:T(8,128)(2,1)S(1)}, u32[]{:S(2)}, u32[]{:S(2)}) collective-permute-start(bf16[32,3072]{1,0:T(8,128)(2,1)S(1)} %get-tuple-element.124), channel_id=1, source_target_pairs={{0,1},{1,0},{2,3},{3,2},{4,5},{5,4},{6,7},{7,6},{8,9},{9,8},{10,11... | collective-permute-start | bytes 589832 | tf_op jit(solution)/shard_map/ppermute | solution.py:404
  77.4 2.5 %collective-permute-start.27 = (f32[24,768]{1,0:T(8,128)S(1)}, f32[24,768]{1,0:T(8,128)S(1)}, u32[]{:S(2)}, u32[]{:S(2)}) collective-permute-start(f32[24,768]{1,0:T(8,128)S(1)} %get-tuple-element.130), channel_id=1, source_target_pairs={{0,10},{1,11},{2,8},{3,9},{4,14},{5,15},{6,12},{7,13},{8,2},{9,3},... | collective-permute-start | bytes 221192 | tf_op jit(solution)/shard_map/ppermute | solution.py:404
  79.9 1.7 %finish.1 = (bf16[256,1536]{1,0:T(8,128)(2,1)}, bf16[256,1536]{1,0:T(8,128)(2,1)}) custom-call(f32[256,1536]{1,0:T(8,128)S(1)} %get-tuple-element.122.refs_0_, f32[256,1536]{1,0:T(8,128)S(1)} %get-tuple-element.123.refs_1_, f32[32,3072]{1,0:T(8,128)S(1)} %get-tuple-element.115.refs_2_, bf16[32,3072]{1,0:T(8,128)(2,1)S(1)} %collective-permute-done.24.refs_3_), custom_call_target="tpu_custom_call" | custom-call | bytes 6290000 | tf_op jit(solution)/shard_map/finish/pallas_call | solution.py:228
  81.7 3.6 %collective-permute-start.28 = (f32[12,768]{1,0:T(8,128)S(1)}, f32[12,768]{1,0:T(8,128)S(1)}, u32[]{:S(2)}, u32[]{:S(2)}) collective-permute-start(f32[12,768]{1,0:T(8,128)S(1)} %get-tuple-element.132), channel_id=1, source_target_pairs={{0,1},{1,0},{2,3},{3,2},{4,5},{5,4},{6,7},{7,6},{8,9},{9,8},{10,11... | collective-permute-start | bytes 110600 | tf_op jit(solution)/shard_map/ppermute | solution.py:404
  (75 shorter events, 22.6 us)
Async XLA Ops:
  5.3 23.5 %collective-permute-start = (bf16[256,768]{1,0:T(8,128)(2,1)S(1)}, bf16[256,768]{1,0:T(8,128)(2,1)S(1)}, u32[]{:S(2)}, u32[]{:S(2)}) collective-permute-start(bf16[256,768]{1,0:T(8,128)(2,1)S(1)} %get-tuple-element.72.refs_4_), channel_id=1, source_target_pairs={{0,96},{32,64},{64,32},{96,0},{1,97},{33,65},{65,33},{97,1},{2,98}... | collective-permute-start | bytes 1179656 | tf_op jit(solution)/shard_map/ppermute | solution.py:408
  7.8 20.9 %collective-permute-start.2 = (bf16[256,768]{1,0:T(8,128)(2,1)S(1)}, bf16[256,768]{1,0:T(8,128)(2,1)S(1)}, u32[]{:S(2)}, u32[]{:S(2)}) collective-permute-start(bf16[256,768]{1,0:T(8,128)(2,1)S(1)} %collective-permute-done.1.refs_5_), channel_id=1, source_target_pairs={{0,96},{32,64},{64,32},{96,0},{1,97},{33,65},{65,33},{97,1},{2,98}... | collective-permute-start | bytes 1179656 | tf_op jit(solution)/shard_map/ppermute | solution.py:408
  9.4 11.2 %collective-permute-start.4 = (bf16[32,3072]{1,0:T(8,128)(2,1)S(1)}, bf16[32,3072]{1,0:T(8,128)(2,1)S(1)}, u32[]{:S(2)}, u32[]{:S(2)}) collective-permute-start(bf16[32,3072]{1,0:T(8,128)(2,1)S(1)} %get-tuple-element.77), channel_id=1, source_target_pairs={{0,2},{1,3},{2,0},{3,1},{4,6},{5,7},{6,4},{7,5},{8,10},{9,11},{10,... | collective-permute-start | bytes 589832 | tf_op jit(solution)/shard_map/ppermute | solution.py:404
  11.1 9.4 %collective-permute-start.5 = (bf16[16,3072]{1,0:T(8,128)(2,1)S(1)}, bf16[16,3072]{1,0:T(8,128)(2,1)S(1)}, u32[]{:S(2)}, u32[]{:S(2)}) collective-permute-start(bf16[16,3072]{1,0:T(8,128)(2,1)S(1)} %get-tuple-element.79.l5), channel_id=1, source_target_pairs={{0,4},{1,5},{2,6},{3,7},{4,0},{5,1},{6,2},{7,3},{8,12},{9,13},{10,... | collective-permute-start | bytes 294920 | tf_op jit(solution)/shard_map/ppermute | solution.py:404
  14.4 6.1 %collective-permute-start.6 = (bf16[16,3072]{1,0:T(8,128)(2,1)S(1)}, bf16[16,3072]{1,0:T(8,128)(2,1)S(1)}, u32[]{:S(2)}, u32[]{:S(2)}) collective-permute-start(bf16[16,3072]{1,0:T(8,128)(2,1)S(1)} %get-tuple-element.79.l5), channel_id=1, source_target_pairs={{0,6},{1,7},{2,4},{3,5},{4,2},{5,3},{6,0},{7,1},{8,14},{9,15},{10,... | collective-permute-start | bytes 294920 | tf_op jit(solution)/shard_map/ppermute | solution.py:404
  21.0 9.2 %collective-permute-start.7 = (bf16[32,3072]{1,0:T(8,128)(2,1)S(1)}, bf16[32,3072]{1,0:T(8,128)(2,1)S(1)}, u32[]{:S(2)}, u32[]{:S(2)}) collective-permute-start(bf16[32,3072]{1,0:T(8,128)(2,1)S(1)} %get-tuple-element.80), channel_id=1, source_target_pairs={{0,8},{1,9},{2,10},{3,11},{4,12},{5,13},{6,14},{7,15},{8,0},{9,1},... | collective-permute-start | bytes 589832 | tf_op jit(solution)/shard_map/ppermute | solution.py:404
  22.4 7.0 %collective-permute-start.8 = (bf16[16,3072]{1,0:T(8,128)(2,1)S(1)}, bf16[16,3072]{1,0:T(8,128)(2,1)S(1)}, u32[]{:S(2)}, u32[]{:S(2)}) collective-permute-start(bf16[16,3072]{1,0:T(8,128)(2,1)S(1)} %get-tuple-element.81), channel_id=1, source_target_pairs={{0,16},{1,17},{2,18},{3,19},{4,20},{5,21},{6,22},{7,23},{8,24},{9,... | collective-permute-start | bytes 294920 | tf_op jit(solution)/shard_map/ppermute | solution.py:404
  25.0 5.2 %collective-permute-start.9 = (bf16[16,3072]{1,0:T(8,128)(2,1)S(1)}, bf16[16,3072]{1,0:T(8,128)(2,1)S(1)}, u32[]{:S(2)}, u32[]{:S(2)}) collective-permute-start(bf16[16,3072]{1,0:T(8,128)(2,1)S(1)} %get-tuple-element.81), channel_id=1, source_target_pairs={{0,24},{1,25},{2,26},{3,27},{4,28},{5,29},{6,30},{7,31},{8,16},{9,... | collective-permute-start | bytes 294920 | tf_op jit(solution)/shard_map/ppermute | solution.py:404
  34.7 10.3 %collective-permute-start.11 = (bf16[768,256]{1,0:T(8,128)(2,1)S(1)}, bf16[768,256]{1,0:T(8,128)(2,1)S(1)}, u32[]{:S(2)}, u32[]{:S(2)}) collective-permute-start(bf16[768,256]{1,0:T(8,128)(2,1)S(1)} %get-tuple-element.84), channel_id=1, source_target_pairs={{0,96},{32,64},{64,32},{96,0},{1,97},{33,65},{65,33},{97,1},{2,98}... | collective-permute-start | bytes 1179656 | tf_op jit(solution)/shard_map/ppermute | solution.py:408
  40.8 7.1 %collective-permute-start.10 = (bf16[768,256]{1,0:T(8,128)(2,1)S(1)}, bf16[768,256]{1,0:T(8,128)(2,1)S(1)}, u32[]{:S(2)}, u32[]{:S(2)}) collective-permute-start(bf16[768,256]{1,0:T(8,128)(2,1)S(1)} %get-tuple-element.89.refs_0_), channel_id=1, source_target_pairs={{0,1},{1,0},{2,3},{3,2},{4,5},{5,4},{6,7},{7,6},{8,9},{9,8},{10,11... | collective-permute-start | bytes 1179656 | tf_op jit(solution)/shard_map/ppermute | solution.py:404
  50.2 9.5 %collective-permute-start.13 = (bf16[384,384]{1,0:T(8,128)(2,1)S(1)}, bf16[384,384]{1,0:T(8,128)(2,1)S(1)}, u32[]{:S(2)}, u32[]{:S(2)}) collective-permute-start(bf16[384,384]{1,0:T(8,128)(2,1)S(1)} %get-tuple-element.97), channel_id=1, source_target_pairs={{0,6},{1,7},{2,4},{3,5},{4,2},{5,3},{6,0},{7,1},{8,14},{9,15},{10,... | collective-permute-start | bytes 884744 | tf_op jit(solution)/shard_map/ppermute | solution.py:404
  52.9 8.0 %collective-permute-start.14 = (bf16[384,384]{1,0:T(8,128)(2,1)S(1)}, bf16[384,384]{1,0:T(8,128)(2,1)S(1)}, u32[]{:S(2)}, u32[]{:S(2)}) collective-permute-start(bf16[384,384]{1,0:T(8,128)(2,1)S(1)} %get-tuple-element.100), channel_id=1, source_target_pairs={{0,32},{32,0},{64,96},{96,64},{1,33},{33,1},{65,97},{97,65},{2,34}... | collective-permute-start | bytes 884744 | tf_op jit(solution)/shard_map/ppermute | solution.py:408
  52.9 8.3 %collective-permute-start.15 = (bf16[32,3072]{1,0:T(8,128)(2,1)S(1)}, bf16[32,3072]{1,0:T(8,128)(2,1)S(1)}, u32[]{:S(2)}, u32[]{:S(2)}) collective-permute-start(bf16[32,3072]{1,0:T(8,128)(2,1)S(1)} %get-tuple-element.103), channel_id=1, source_target_pairs={{0,8},{1,9},{2,10},{3,11},{4,12},{5,13},{6,14},{7,15},{8,0},{9,1},... | collective-permute-start | bytes 589832 | tf_op jit(solution)/shard_map/ppermute | solution.py:404
  53.0 8.2 %collective-permute-start.16 = (bf16[16,3072]{1,0:T(8,128)(2,1)S(1)}, bf16[16,3072]{1,0:T(8,128)(2,1)S(1)}, u32[]{:S(2)}, u32[]{:S(2)}) collective-permute-start(bf16[16,3072]{1,0:T(8,128)(2,1)S(1)} %get-tuple-element.104), channel_id=1, source_target_pairs={{0,16},{1,17},{2,18},{3,19},{4,20},{5,21},{6,22},{7,23},{8,24},{9,... | collective-permute-start | bytes 294920 | tf_op jit(solution)/shard_map/ppermute | solution.py:404
  55.1 6.1 %collective-permute-start.17 = (bf16[16,3072]{1,0:T(8,128)(2,1)S(1)}, bf16[16,3072]{1,0:T(8,128)(2,1)S(1)}, u32[]{:S(2)}, u32[]{:S(2)}) collective-permute-start(bf16[16,3072]{1,0:T(8,128)(2,1)S(1)} %get-tuple-element.105), channel_id=1, source_target_pairs={{0,24},{1,25},{2,26},{3,27},{4,28},{5,29},{6,30},{7,31},{8,16},{9,... | collective-permute-start | bytes 294920 | tf_op jit(solution)/shard_map/ppermute | solution.py:404
  61.7 10.4 %collective-permute-start.20 = (bf16[32,3072]{1,0:T(8,128)(2,1)S(1)}, bf16[32,3072]{1,0:T(8,128)(2,1)S(1)}, u32[]{:S(2)}, u32[]{:S(2)}) collective-permute-start(bf16[32,3072]{1,0:T(8,128)(2,1)S(1)} %get-tuple-element.112), channel_id=1, source_target_pairs={{0,2},{1,3},{2,0},{3,1},{4,6},{5,7},{6,4},{7,5},{8,10},{9,11},{10,... | collective-permute-start | bytes 589832 | tf_op jit(solution)/shard_map/ppermute | solution.py:404
  61.8 5.9 %collective-permute-start.18 = (bf16[192,384]{1,0:T(8,128)(2,1)S(1)}, bf16[192,384]{1,0:T(8,128)(2,1)S(1)}, u32[]{:S(2)}, u32[]{:S(2)}) collective-permute-start(bf16[192,384]{1,0:T(8,128)(2,1)S(1)} %get-tuple-element.108), channel_id=1, source_target_pairs={{0,6},{1,7},{2,4},{3,5},{4,2},{5,3},{6,0},{7,1},{8,14},{9,15},{10,... | collective-permute-start | bytes 442376 | tf_op jit(solution)/shard_map/ppermute | solution.py:404
  64.5 6.0 %collective-permute-start.21 = (bf16[16,3072]{1,0:T(8,128)(2,1)S(1)}, bf16[16,3072]{1,0:T(8,128)(2,1)S(1)}, u32[]{:S(2)}, u32[]{:S(2)}) collective-permute-start(bf16[16,3072]{1,0:T(8,128)(2,1)S(1)} %get-tuple-element.113), channel_id=1, source_target_pairs={{0,4},{1,5},{2,6},{3,7},{4,0},{5,1},{6,2},{7,3},{8,12},{9,13},{10,... | collective-permute-start | bytes 294920 | tf_op jit(solution)/shard_map/ppermute | solution.py:404
  66.1 6.0 %collective-permute-start.22 = (bf16[16,3072]{1,0:T(8,128)(2,1)S(1)}, bf16[16,3072]{1,0:T(8,128)(2,1)S(1)}, u32[]{:S(2)}, u32[]{:S(2)}) collective-permute-start(bf16[16,3072]{1,0:T(8,128)(2,1)S(1)} %get-tuple-element.114), channel_id=1, source_target_pairs={{0,6},{1,7},{2,4},{3,5},{4,2},{5,3},{6,0},{7,1},{8,14},{9,15},{10,... | collective-permute-start | bytes 294920 | tf_op jit(solution)/shard_map/ppermute | solution.py:404
  67.8 9.3 %collective-permute-start.23 = (bf16[96,768]{1,0:T(8,128)(2,1)S(1)}, bf16[96,768]{1,0:T(8,128)(2,1)S(1)}, u32[]{:S(2)}, u32[]{:S(2)}) collective-permute-start(bf16[96,768]{1,0:T(8,128)(2,1)S(1)} %get-tuple-element.120), channel_id=1, source_target_pairs={{0,24},{1,25},{2,26},{3,27},{4,28},{5,29},{6,30},{7,31},{8,16},{9,... | collective-permute-start | bytes 442376 | tf_op jit(solution)/shard_map/ppermute | solution.py:404
  72.5 7.5 %collective-permute-start.24 = (bf16[32,3072]{1,0:T(8,128)(2,1)S(1)}, bf16[32,3072]{1,0:T(8,128)(2,1)S(1)}, u32[]{:S(2)}, u32[]{:S(2)}) collective-permute-start(bf16[32,3072]{1,0:T(8,128)(2,1)S(1)} %get-tuple-element.124), channel_id=1, source_target_pairs={{0,1},{1,0},{2,3},{3,2},{4,5},{5,4},{6,7},{7,6},{8,9},{9,8},{10,11... | collective-permute-start | bytes 589832 | tf_op jit(solution)/shard_map/ppermute | solution.py:404
  77.2 4.4 %collective-permute-start.25 = (f32[24,768]{1,0:T(8,128)S(1)}, f32[24,768]{1,0:T(8,128)S(1)}, u32[]{:S(2)}, u32[]{:S(2)}) collective-permute-start(f32[24,768]{1,0:T(8,128)S(1)} %get-tuple-element.128), channel_id=1, source_target_pairs={{0,8},{1,9},{2,10},{3,11},{4,12},{5,13},{6,14},{7,15},{8,0},{9,1},... | collective-permute-start | bytes 221192 | tf_op jit(solution)/shard_map/ppermute | solution.py:404
  77.3 4.3 %collective-permute-start.26 = (f32[24,768]{1,0:T(8,128)S(1)}, f32[24,768]{1,0:T(8,128)S(1)}, u32[]{:S(2)}, u32[]{:S(2)}) collective-permute-start(f32[24,768]{1,0:T(8,128)S(1)} %get-tuple-element.129), channel_id=1, source_target_pairs={{0,2},{1,3},{2,0},{3,1},{4,6},{5,7},{6,4},{7,5},{8,10},{9,11},{10,... | collective-permute-start | bytes 221192 | tf_op jit(solution)/shard_map/ppermute | solution.py:404
  81.7 4.5 %collective-permute-start.28 = (f32[12,768]{1,0:T(8,128)S(1)}, f32[12,768]{1,0:T(8,128)S(1)}, u32[]{:S(2)}, u32[]{:S(2)}) collective-permute-start(f32[12,768]{1,0:T(8,128)S(1)} %get-tuple-element.132), channel_id=1, source_target_pairs={{0,1},{1,0},{2,3},{3,2},{4,5},{5,4},{6,7},{7,6},{8,9},{9,8},{10,11... | collective-permute-start | bytes 110600 | tf_op jit(solution)/shard_map/ppermute | solution.py:404
  (14 other events, 83.1 us)
